TPU v7x, 32 devices: a whole 2x2x4 slice. The times are simulated.
32 devices in a mesh: groups: 2 (over x), req: 8 (over z, y), tp: 2 (over core).
Axes of the slice: x: 2, y: 2, z: 4, core: 2. Of those that a mesh axis runs over, the one named last changes fastest.
Arguments:
- x_inputs: bfloat16 [32, 256, 4096], P(('groups', 'req'), None, 'tp'), parts along dimension 0, may hold values from -6 to 6
- z_gates: bfloat16 [32, 256, 4096], P(('groups', 'req'), None, 'tp'), parts along dimension 0, may hold values from -6 to 6
- b_proj: bfloat16 [32, 256, 256], P(('groups', 'req')), parts along dimension 0, may hold values from -1.5 to 1.5
- c_proj: bfloat16 [32, 256, 256], P(('groups', 'req')), parts along dimension 0, may hold values from -1.5 to 1.5
- dt_raw: float32 [32, 256, 32], P(('groups', 'req'), None, 'tp'), parts along dimension 0, may hold values from -1.5 to 7.5
- dt_bias: float32 [32], P('tp'), may hold values from -4.5 to -3.8
- a_log: float32 [32], P('tp'), may hold values from -2.31 to 2.08
- d_skip: float32 [32], P('tp'), may hold values from 0.5 to 1.5
- pool_codes: bfloat16 [2048, 64, 256], P(('groups', 'req', 'tp')), parts along dimension 0, may hold values from -6 to 6
- pool_scales: bfloat16 [2048, 64], P(('groups', 'req', 'tp')), parts along dimension 0, may hold values from 0.049804688 to 0.5
- page_holder: int32 [2, 32, 32, 1], P('tp', 'groups'), parts along dimension 1, may hold values from 0 to 7; in each aligned block of 64 rows (0 to 63, 64 to 127, ..., all dimensions but the last counted through in order) at most 16 rows name the same one
- page_index: int32 [2, 32, 32], P('tp', 'groups'), parts along dimension 1, may hold values from 0 to 63
- hit_blocks: int32 [32], P(('groups', 'req')), parts along dimension 0, may hold values 0 or 1
- suffix_len: int32 [32], P(('groups', 'req')), parts along dimension 0, may hold values from 1 to 256, 3072 in all
- w_out: bfloat16 [4096, 2, 2560], P(None, 'tp', 'req'), may hold values from -0.09375 to 0.09375
Outputs:
- mixed_out: bfloat16 [32, 256, 5120], P(('groups', 'req'), None, 'tp'), parts along dimension 0
- end_state: bfloat16 [32, 4096, 256], P(('groups', 'req'), 'tp'), parts along dimension 0
There are 2 independent parts, one for each index of `groups`. A program takes and returns all parts, laid end to end along the dimension named above; an argument that names none is the same for every part. Nothing has to cross between parts.
Inputs may be any that keep to these rules, and one draw needn't show every extreme that they name: `page_holder`: in each aligned block of 64 rows (the pages of one device's requests on one tp index) no holder is named more than 16 times, a bound that some block reaches. `suffix_len`: some request has 256 suffix tokens.
All inputs are finite; a program needn't handle non-finite values. No bound on the sum of `hit_blocks` or of `suffix_len` on one device may be relied on, other than what follows from the above.
Results may differ from a plain program's by a relative error of at most 0.0055.
Values may be sent and summed in bfloat16 or wider, within the bound.
No kernel may reach another device: no remote copies, remote signals or barrier semaphores. Data moves between devices by JAX's collectives and lax.ppermute only.
A program may use at most 128 MiB of HBM per device.

v0:
```python
import jax
import jax.numpy as jnp
from jax import lax
from jax.sharding import PartitionSpec as P


def swapped(value, axis, bit):
    mask = 2**bit
    pairs = [(source, source ^ mask) for source in range(lax.axis_size(axis))]
    return lax.ppermute(value, axis, pairs)


def on_device(
    x_inputs,
    z_gates,
    b_proj,
    c_proj,
    dt_raw,
    dt_bias,
    a_log,
    d_skip,
    pool_codes,
    pool_scales,
    page_holder,
    page_index,
    hit_blocks,
    suffix_len,
    w_out,
):
    n_req = lax.axis_size("req")
    own_index = lax.axis_index("req")
    reqs_dev, slots, inner_tp = x_inputs.shape
    heads_tp = dt_raw.shape[2]
    head_dim = inner_tp // heads_tp
    state_width = b_proj.shape[2]
    need_count = page_index.shape[2] * reqs_dev
    capacity = max(2, 2 * need_count // n_req)
    holders = page_holder[0, :, :, 0].reshape(n_req, need_count)
    indices = page_index[0].reshape(n_req, need_count)
    is_mine = holders == own_index
    send_rank = jnp.cumsum(is_mine.astype(jnp.int32), axis=1) - 1
    chosen = is_mine[:, None, :] & (
        send_rank[:, None, :] == jnp.arange(capacity, dtype=jnp.int32)[None, :, None]
    )
    filled_slots = jnp.any(chosen, axis=2).reshape(-1)
    wanted = jnp.sum(jnp.where(chosen, indices[:, None, :], 0), axis=2).reshape(-1)
    send_codes = jnp.where(
        filled_slots[:, None, None], pool_codes[wanted], jnp.zeros((), jnp.bfloat16)
    )
    send_scales = jnp.where(filled_slots[:, None], pool_scales[wanted], jnp.zeros((), jnp.bfloat16))
    got_codes, got_scales = (
        lax.all_to_all(send_codes, "req", split_axis=0, concat_axis=0, tiled=True),
        lax.all_to_all(send_scales, "req", split_axis=0, concat_axis=0, tiled=True),
    )
    own_holders = lax.dynamic_index_in_dim(holders, own_index, 0, keepdims=False)
    position = jnp.arange(need_count, dtype=jnp.int32)
    earlier = (own_holders[:, None] == own_holders[None, :]) & (
        position[:, None] < position[None, :]
    )
    where_from = own_holders * capacity + jnp.sum(earlier.astype(jnp.int32), axis=0)
    page_codes = got_codes[where_from].reshape(reqs_dev, heads_tp, head_dim, state_width)
    hit_mask = (hit_blocks > 0).astype(jnp.float32)
    row_scales = (
        got_scales[where_from].reshape(reqs_dev, heads_tp, head_dim).astype(jnp.float32)
        * hit_mask[:, None, None]
    )
    start_state = page_codes.astype(jnp.float32) * row_scales[:, :, :, None]
    token_rows = jnp.arange(slots, dtype=jnp.int32)
    live_mask = (token_rows[None, :] < suffix_len[:, None]).astype(jnp.float32)
    step_size = jax.nn.softplus(dt_raw + dt_bias) * live_mask[:, :, None]
    log_decay = -jnp.exp(a_log) * jnp.cumsum(step_size, axis=1)
    inner_cb = jnp.einsum("rtn,rsn->rts", c_proj, b_proj, preferred_element_type=jnp.float32)
    causal = token_rows[:, None] >= token_rows[None, :]
    decay_gap = log_decay[:, :, None, :] - log_decay[:, None, :, :]
    decay_mat = jnp.exp(jnp.where(causal[None, :, :, None], decay_gap, -jnp.inf))
    mixer = (decay_mat * inner_cb[:, :, :, None] * step_size[:, None, :, :]).astype(jnp.bfloat16)
    x_heads = x_inputs.reshape(reqs_dev, slots, heads_tp, head_dim)
    within = jnp.einsum("rtsh,rshp->rthp", mixer, x_heads, preferred_element_type=jnp.float32)
    from_start = jnp.einsum(
        "rtn,rhpn->rthp", c_proj.astype(jnp.float32), start_state, precision=lax.Precision.HIGHEST
    )
    y_total = (
        within
        + jnp.exp(log_decay)[:, :, :, None] * from_start
        + d_skip[:, None] * x_heads.astype(jnp.float32)
    )
    gates = z_gates.reshape(reqs_dev, slots, heads_tp, head_dim).astype(jnp.float32)
    gated = (
        (y_total * jax.nn.silu(gates) * live_mask[:, :, None, None])
        .astype(jnp.bfloat16)
        .reshape(reqs_dev * slots, inner_tp)
    )
    log_total = log_decay[:, slots - 1, :]
    weight = jnp.exp(log_total[:, None, :] - log_decay) * step_size
    x_weighted = (x_heads.astype(jnp.float32) * weight[:, :, :, None]).astype(jnp.bfloat16)
    accumulated = jnp.einsum(
        "rshp,rsn->rhpn", x_weighted, b_proj, preferred_element_type=jnp.float32
    )
    end_state = (jnp.exp(log_total)[:, :, None, None] * start_state + accumulated).astype(
        jnp.bfloat16
    )
    end_state = end_state.reshape(reqs_dev, inner_tp, state_width)
    weight_cols = w_out[:, 0, :]
    half_width = weight_cols.shape[1] * n_req
    tp_index = lax.axis_index("tp")
    own_rows = lax.dynamic_slice_in_dim(weight_cols, tp_index * inner_tp, inner_tp, 0)
    give_rows = lax.dynamic_slice_in_dim(weight_cols, (1 - tp_index) * inner_tp, inner_tp, 0)
    came_rows = swapped(give_rows, "tp", 0)
    first_half = jnp.where(tp_index == 0, own_rows, came_rows)
    second_half = jnp.where(tp_index == 0, came_rows, own_rows)
    empty = jnp.zeros((gated.shape[0], 2 * half_width), jnp.float32)
    total = empty
    start = jnp.int32(0)
    lower = jnp.dot(
        gated,
        lax.all_gather(first_half, "req", axis=1, tiled=True),
        preferred_element_type=jnp.float32,
    )
    upper = jnp.dot(
        gated,
        lax.all_gather(second_half, "req", axis=1, tiled=True),
        preferred_element_type=jnp.float32,
    )
    total = lax.dynamic_update_slice(total, lower, (jnp.int32(0), start))
    partial_value = lax.dynamic_update_slice(total, upper, (jnp.int32(0), start + half_width))
    summed = lax.psum_scatter(partial_value, "tp", scatter_dimension=1, tiled=True)
    mixed_out = summed.astype(jnp.bfloat16).reshape(reqs_dev, slots, summed.shape[1])
    return (mixed_out, end_state)


def solution(mesh):
    in_specs = (
        P(("groups", "req"), None, "tp"),
        P(("groups", "req"), None, "tp"),
        P(("groups", "req"), None, None),
        P(("groups", "req"), None, None),
        P(("groups", "req"), None, "tp"),
        P("tp"),
        P("tp"),
        P("tp"),
        P(("groups", "req", "tp"), None, None),
        P(("groups", "req", "tp"), None),
        P("tp", "groups", None, None),
        P("tp", "groups", None),
        P(("groups", "req")),
        P(("groups", "req")),
        P(None, "tp", "req"),
    )
    out_specs = (P(("groups", "req"), None, "tp"), P(("groups", "req"), "tp", None))
    return jax.shard_map(
        on_device, mesh=mesh, in_specs=in_specs, out_specs=out_specs, check_vma=False
    )
```

profile of v0, /device:TPU:16, one launch (start us, length us, event | category | flops | bytes accessed | tf_op | source)
XLA Modules:
  0.0 446.9 jit_solution(7631054628678436269)
XLA Ops:
  7.2 0.0 copy-start
  7.2 0.0 all-gather.3.cloned.1.call-start
  7.2 1.6 dynamic-slice_bitcast_fusion
  8.8 0.0 copy-start.9
  8.9 0.0 copy-start.3
  8.9 0.1 collective-permute-start
  9.0 3.1 collective-permute-done
  12.1 3.9 bitcast_select_fusion.1
  16.0 0.0 all-gather.3.cloned.1.call-update
  16.1 0.0 all-gather.5.cloned.1.call-start
  16.1 0.7 all-gather.5.cloned.1.call-update
  16.8 0.5 broadcast.157
  17.3 0.7 reduce.7
  18.0 0.1 reshape_squeeze.3
  18.1 0.2 reduce_window_sum.28
  18.3 0.1 broadcast_in_dim.56
  18.4 0.2 select_reduce_fusion
  18.6 0.1 reshape.205
  18.7 0.7 gather_fusion.2
  19.4 0.2 fusion.29
  19.6 0.1 broadcast_select_fusion.1
  19.7 0.7 reshape.257
  20.4 6.2 %all-to-all-start.1 = ((bf16[8,2,512]{2,1,0:T(2,128)(2,1)}), bf16[8,2,512]{2,1,0:T(2,128)(2,1)S(1)}, u32[]{:S(2)}, u32[]{:S(2)}) async-start(bf16[8,2,512]{2,1,0:T(2,128)(2,1)} %reshape.257), calls=%async_computation.1 | async-start | bytes 32768 | tf_op jit(solution)/shard_map/all_to_all | solution.py:53
  26.6 0.1 broadcast_in_dim.50
  26.7 2.9 gather_fusion
  29.6 4.6 %broadcast_select_fusion = bf16[128,64,256]{2,1,0:T(8,128)(2,1)} fusion(bf16[128,64,256]{2,1,0:T(8,128)(2,1)} %gather_fusion, pred[128]{0:T(512)(128)(4,1)S(1)} %broadcast_in_dim.50), kind=kLoop, calls=%fused_computation.26 | loop fusion | flops 2097152 | bytes 8388736 | tf_op jit(solution)/shard_map/jit(_where)/select_n | solution.py:47
  34.2 6.1 %all-to-all-start = ((bf16[128,64,256]{2,1,0:T(8,128)(2,1)}), bf16[128,64,256]{2,1,0:T(8,128)(2,1)}, u32[]{:S(2)}, u32[]{:S(2)}) async-start(bf16[128,64,256]{2,1,0:T(8,128)(2,1)} %broadcast_select_fusion), calls=%async_computation | async-start | bytes 8388608 | tf_op jit(solution)/shard_map/all_to_all | solution.py:52
  40.3 0.1 compare_convert_fusion
  40.4 0.1 copy_bitcast_fusion
  40.5 1.2 reduce-window.6
  41.7 0.2 slice_reduce_fusion
  41.9 2.9 copy.33
  44.7 1.3 copy-done.2
  46.1 2.4 copy.36
  48.4 2.8 copy.37
  51.3 0.0 copy-start.13
  51.3 0.0 copy-start.6
  51.3 0.0 copy-start.7
  51.3 2.9 copy.39
  54.2 0.1 convert_reduce_fusion
  54.4 0.1 fusion.30
  54.5 0.1 fusion.37
  54.6 0.3 fusion.40
  54.9 4.9 %fusion = f32[2,16,256,128]{3,2,1,0:T(8,128)} fusion(bf16[2,256,16,128]{1,3,2,0:T(8,128)(2,1)} %bitcast.76, f32[2,256,16]{1,2,0:T(8,128)S(1)} %fusion.30, f32[2,256,256]{2,1,0:T(8,128)S(1)} %fusion.40, f32[2,256,16]{1,2,0:T(8,128)S(1)} %get-tuple-element.3, pred[256,256]{1,0:T(8,128)(4,1)S(1)} %iota_compare_fusion), kind=kOutput, calls=%fused_computation.8 | convolution fusion | flops 547356672 | bytes 6946816 | tf_op jit(solution)/shard_map/rtsh,rshp->rthp/dot_general | solution.py:78
  59.8 0.1 reshape.258
  59.9 0.6 gather_fusion.3
  60.5 0.1 reshape.210
  60.6 0.1 broadcast_multiply_fusion
  60.7 156.8 %all-to-all-done = bf16[128,64,256]{2,1,0:T(8,128)(2,1)} async-done(((bf16[128,64,256]{2,1,0:T(8,128)(2,1)}), bf16[128,64,256]{2,1,0:T(8,128)(2,1)}, u32[]{:S(2)}, u32[]{:S(2)}) %all-to-all-start) | async-done | bytes 4194336 | tf_op jit(solution)/shard_map/all_to_all | solution.py:52
  217.5 4.2 gather_fusion.1
  221.7 7.2 %fusion.4 = bf16[2,256,16,128]{3,1,2,0:T(8,128)(2,1)S(1)} fusion(bf16[2,256,16,128]{3,1,2,0:T(8,128)(2,1)S(1)} %copy-done.4, f32[2,16,256,128]{3,2,1,0:T(8,128)} %fusion, f32[2,256,16,128]{3,1,2,0:T(8,128)} %copy.39, bf16[2,16,128,256]{3,2,1,0:T(8,128)(2,1)} %bitcast.78, f32[2,256]{1,0:T(2,128)S(1)} %compare_convert_fusion, f32[16]{0:T(128)S(1)} %copy-done.15, ...), kind=kOutput, calls=%fused_computation.12 | convolution fusion | flops 3235905536 | bytes 14993472 | tf_op jit(solution)/shard_map/rtn,rhpn->rthp/dot_general | solution.py:79
  228.9 1.4 copy.40
  230.3 14.5 %all-gather.3.cloned.1.call-done = bf16[2048,2560]{0,1:T(8,128)(2,1)} async-done(((bf16[2048,320]{0,1:T(8,128)(2,1)}), bf16[2048,2560]{0,1:T(8,128)(2,1)}) %all-gather.3.cloned.1.call-update) | async-done | bytes 10485776 | tf_op jit(solution)/shard_map/all_gather | solution.py:116
  244.8 9.9 %fusion.20 = f32[512,2560]{1,0:T(8,128)} fusion(bf16[2048,2560]{0,1:T(8,128)(2,1)} %all-gather.3.cloned.1.call-done, bf16[64,8,16,128]{3,2,1,0:T(8,128)(2,1)S(1)} %bitcast.80), kind=kOutput, calls=%fused_computation.30 | convolution fusion | flops 5368709120 | bytes 17825792 | tf_op jit(solution)/shard_map/dot_general | solution.py:114
  254.6 143.9 %all-gather.5.cloned.1.call-done = bf16[2048,2560]{0,1:T(8,128)(2,1)} async-done(((bf16[2048,320]{0,1:T(8,128)(2,1)}), bf16[2048,2560]{0,1:T(8,128)(2,1)}) %all-gather.5.cloned.1.call-update) | async-done | bytes 10485776 | tf_op jit(solution)/shard_map/all_gather | solution.py:121
  398.5 9.9 %fusion.18 = f32[512,2560]{1,0:T(8,128)} fusion(bf16[2048,2560]{0,1:T(8,128)(2,1)} %all-gather.5.cloned.1.call-done, bf16[64,8,16,128]{3,2,1,0:T(8,128)(2,1)S(1)} %bitcast.81), kind=kOutput, calls=%fused_computation.28 | convolution fusion | flops 5368709120 | bytes 17825792 | tf_op jit(solution)/shard_map/dot_general | solution.py:119
  408.4 9.1 %pad_maximum_fusion = f32[512,5120]{1,0:T(8,128)} fusion(f32[512,2560]{1,0:T(8,128)} %fusion.18, f32[512,2560]{1,0:T(8,128)} %fusion.20), kind=kLoop, calls=%fused_computation.4 | loop fusion | flops 2621440 | bytes 20971520 | tf_op jit(solution)/shard_map/dynamic_update_slice | solution.py:125
  417.5 0.0 reduce-scatter.2.cloned.1.call-update
  417.6 0.2 slice_reduce_fusion.1
  417.7 0.1 exponential_multiply_fusion
  417.8 0.0 copy-start.1
  417.9 5.8 %fusion.9 = bf16[2,16,128,256]{3,2,1,0:T(8,128)(2,1)} fusion(bf16[2,16,128,256]{3,2,1,0:T(8,128)(2,1)} %bitcast.79, bf16[2,256,16,128]{3,1,2,0:T(8,128)(2,1)} %copy.36, f32[2,256,16]{1,2,0:T(8,128)S(1)} %exponential_multiply_fusion, f32[2,16]{1,0:T(2,128)S(1)} %exp.32, f32[2,16,128]{2,1,0:T(8,128)S(1)} %broadcast_multiply_fusion, ...), kind=kOutput, calls=%fused_computation.18 | convolution fusion | flops 545259520 | bytes 6602880 | tf_op jit(solution)/shard_map/rshp,rsn->rhpn/dot_general | solution.py:96
  423.6 12.5 %reduce-scatter.2.cloned.1.call-done = f32[512,2560]{1,0:T(8,128)} async-done(((f32[512,5120]{1,0:T(8,128)}), f32[512,2560]{1,0:T(8,128)}) %reduce-scatter.2.cloned.1.call-update) | async-done | bytes 5242896 | tf_op jit(solution)/shard_map/reduce_scatter | solution.py:126
  436.2 4.3 convert_element_type.79
  (40 shorter events, 0.2 us)
Async XLA Ops:
  7.2 19.5 %copy-start = (bf16[64,64,256]{2,1,0:T(8,128)(2,1)S(1)}, bf16[64,64,256]{2,1,0:T(8,128)(2,1)}, u32[]{:S(2)}) copy-start(bf16[64,64,256]{2,1,0:T(8,128)(2,1)} %param.23) | copy-start | bytes 6291460
  7.2 237.6 %all-gather.3.cloned.1.call-start = ((), (), s32[]{:S(2)}) async-start(), calls=%async_computation.3 | async-start | bytes 11796480 | tf_op jit(solution)/shard_map/all_gather | solution.py:116
  8.8 8.5 %copy-start.10 = (s32[1,16,32,1]{2,3,1,0:T(1,128)S(1)}, s32[1,16,32,1]{2,3,1,0:T(1,128)}, u32[]{:S(2)}) copy-start(s32[1,16,32,1]{2,3,1,0:T(1,128)} %param.25) | copy-start | bytes 6148
  8.8 9.5 %copy-start.9 = (s32[1,16,32]{2,1,0:T(8,128)S(1)}, s32[1,16,32]{2,1,0:T(8,128)}, u32[]{:S(2)}) copy-start(s32[1,16,32]{2,1,0:T(8,128)} %param.26) | copy-start | bytes 6148
  8.9 9.8 %copy-start.3 = (bf16[64,64]{1,0:T(8,128)(2,1)S(1)}, bf16[64,64]{1,0:T(8,128)(2,1)}, u32[]{:S(2)}) copy-start(bf16[64,64]{1,0:T(8,128)(2,1)} %param.24) | copy-start | bytes 24580
  8.9 3.2 collective-permute-start
  16.1 382.5 %all-gather.5.cloned.1.call-start = ((), (), s32[]{:S(2)}) async-start(), calls=%async_computation.4 | async-start | bytes 11796480 | tf_op jit(solution)/shard_map/all_gather | solution.py:121
  20.4 13.7 %all-to-all-start.1 = ((bf16[8,2,512]{2,1,0:T(2,128)(2,1)}), bf16[8,2,512]{2,1,0:T(2,128)(2,1)S(1)}, u32[]{:S(2)}, u32[]{:S(2)}) async-start(bf16[8,2,512]{2,1,0:T(2,128)(2,1)} %reshape.257), calls=%async_computation.1 | async-start | bytes 32768 | tf_op jit(solution)/shard_map/all_to_all | solution.py:53
  34.2 6.2 %copy-start.12 = (s32[2]{0:T(128)S(1)}, s32[2]{0:T(128)}, u32[]{:S(2)}) copy-start(s32[2]{0:T(128)} %param.28) | copy-start | bytes 28
  34.2 6.2 %copy-start.5 = (f32[2,256,16]{1,2,0:T(8,128)S(1)}, f32[2,256,16]{1,2,0:T(8,128)}, u32[]{:S(2)}) copy-start(f32[2,256,16]{1,2,0:T(8,128)} %param.19) | copy-start | bytes 98308
  34.2 6.2 %copy-start.11 = (f32[16]{0:T(128)S(1)}, f32[16]{0:T(128)}, u32[]{:S(2)}) copy-start(f32[16]{0:T(128)} %param.20) | copy-start | bytes 196
  34.2 183.3 %all-to-all-start = ((bf16[128,64,256]{2,1,0:T(8,128)(2,1)}), bf16[128,64,256]{2,1,0:T(8,128)(2,1)}, u32[]{:S(2)}, u32[]{:S(2)}) async-start(bf16[128,64,256]{2,1,0:T(8,128)(2,1)} %broadcast_select_fusion), calls=%async_computation | async-start | bytes 8388608 | tf_op jit(solution)/shard_map/all_to_all | solution.py:52
  40.3 395.8 %reduce-scatter.2.cloned.1.call-start = ((), (), s32[]{:S(2)}) async-start(), calls=%async_computation.5 | async-start | bytes 15728640 | tf_op jit(solution)/shard_map/reduce_scatter | solution.py:126
  41.9 6.6 %copy-start.8 = (f32[2,16,3]{1,2,0:T(4,128)}, f32[2,16,3]{1,2,0:T(4,128)S(1)}, u32[]{:S(2)}) copy-start(f32[2,16,3]{1,2,0:T(4,128)S(1)} %reduce-window.9) | copy-start | bytes 1156
  44.7 1.3 copy-start.2
  51.3 3.1 copy-start.13
  51.3 3.1 copy-start.14
  51.3 3.2 slice-start
  51.3 3.3 copy-start.6
  51.3 3.3 copy-start.7
  59.8 161.9 %copy-start.4 = (bf16[2,256,16,128]{3,1,2,0:T(8,128)(2,1)S(1)}, bf16[2,256,16,128]{3,1,2,0:T(8,128)(2,1)}, u32[]{:S(2)}) copy-start(bf16[2,256,16,128]{3,1,2,0:T(8,128)(2,1)} %copy.36) | copy-start | bytes 6291460
  59.8 161.9 %copy-start.15 = (f32[16]{0:T(128)S(1)}, f32[16]{0:T(128)}, u32[]{:S(2)}) copy-start(f32[16]{0:T(128)} %param.22) | copy-start | bytes 196
  417.8 22.6 %copy-start.1 = (bf16[64,64,256]{2,1,0:T(8,128)(2,1)S(1)}, bf16[64,64,256]{2,1,0:T(8,128)(2,1)}, u32[]{:S(2)}) copy-start(bf16[64,64,256]{2,1,0:T(8,128)(2,1)} %param.23) | copy-start | bytes 6291460
Sparse Core Ops, SparseCore 0:
  16.2 228.5 all-gather.2
  246.9 151.5 all-gather.4
  417.7 18.4 reduce-scatter.1
where the time goes:
time: 449 us; the launch traced here: 447 us
  waiting for transfers between devices  332 us (74%)
  matrix products  37.9 us (8%)
  local copies, waits for them, and re-layouts  25.7 us (6%)
  other arithmetic  25.2 us (6%)
  between operations  14.1 us (3%)
  starting transfers between devices  12.5 us (3%)
    all_to_all x1, waiting for transfers between devices, on_device(): lax.all_to_all(send_codes, 'req', split_axis=0, concat_axis=0, tiled=True)  157 us
    all_gather x1, waiting for transfers between devices, on_device(): lax.all_gather(second_half, 'req', axis=1, tiled=True)  144 us
    all_gather x1, waiting for transfers between devices, on_device(): lax.all_gather(first_half, 'req', axis=1, tiled=True)  14.5 us
    reduce_scatter x1, waiting for transfers between devices, on_device(): lax.psum_scatter(partial_value, 'tp', scatter_dimension=1, tiled=True)  12.5 us
    dot_general x1, matrix products, on_device(): jnp.dot(gated, lax.all_gather(second_half, 'req', axis=1, tiled=True), pr...  9.89 us
    dot_general x1, matrix products, on_device(): jnp.dot(gated, lax.all_gather(first_half, 'req', axis=1, tiled=True), pre...  9.85 us
    dynamic_update_slice x1, other arithmetic, on_device(): lax.dynamic_update_slice(total, upper, (jnp.int32(0), start + half_width))  9.12 us
  transfers between devices with their start and end apart: 6, of which 5 were waited for; matrix products, arithmetic and copies ran while one was open for 13% of the time, Pallas kernels for 0%

commit v1 on v0

v1 whole, which is shorter than its diff:
```python
import jax
import jax.numpy as jnp
from jax import lax
from jax.sharding import PartitionSpec as P

BF16 = jnp.bfloat16
F32 = jnp.float32


def swapped(value, axis, mask):
    pairs = [(source, source ^ mask) for source in range(lax.axis_size(axis))]
    return lax.ppermute(value, axis, pairs)


def ordered(first_is_mine, mine, other, axis):
    first = jnp.where(first_is_mine, mine, other)
    second = jnp.where(first_is_mine, other, mine)
    return jnp.concatenate([first, second], axis=axis)


def after(value, *earlier):
    return lax.optimization_barrier((value,) + earlier)[0]


def rows_times(tokens, block):
    return lax.dot_general(
        tokens, block, (((1,), (1,)), ((), ())), preferred_element_type=F32
    ).astype(BF16)


def on_device(
    x_inputs,
    z_gates,
    b_proj,
    c_proj,
    dt_raw,
    dt_bias,
    a_log,
    d_skip,
    pool_codes,
    pool_scales,
    page_holder,
    page_index,
    hit_blocks,
    suffix_len,
    w_out,
):
    n_req = lax.axis_size("req")
    own_index = lax.axis_index("req")
    group = lax.axis_index("groups")
    tp_index = lax.axis_index("tp")
    reqs_dev, slots, inner_tp = x_inputs.shape
    heads_tp = dt_raw.shape[2]
    head_dim = inner_tp // heads_tp
    state_width = b_proj.shape[2]
    tokens = reqs_dev * slots

    block = w_out[:, 0, :].T
    columns = block.shape[0]
    share = columns // lax.axis_size("groups")
    piece = lax.dynamic_slice_in_dim(block, group * share, share, 0)
    line = n_req // 2
    chain = line == 4
    if chain:
        near = swapped(piece, "req", 2)
        middle = [(2, 4), (4, 2), (3, 5), (5, 3)]
        outward = [(2, 0), (3, 1), (4, 6), (5, 7)]
        second_inner = lax.ppermute(piece, "req", middle)

    need_count = page_index.shape[2] * reqs_dev
    capacity = max(2, 2 * need_count // n_req)
    holders = page_holder[0, :, :, 0].reshape(n_req, need_count)
    indices = page_index[0].reshape(n_req, need_count)
    is_mine = holders == own_index
    send_rank = jnp.cumsum(is_mine.astype(jnp.int32), axis=1) - 1
    chosen = is_mine[:, None, :] & (
        send_rank[:, None, :] == jnp.arange(capacity, dtype=jnp.int32)[None, :, None]
    )
    wanted = jnp.sum(jnp.where(chosen, indices[:, None, :], 0), axis=2).reshape(-1)
    got_codes = lax.all_to_all(
        pool_codes[wanted], "req", split_axis=0, concat_axis=0, tiled=True
    )
    send_scales = pool_scales[wanted]
    got_scales = lax.all_to_all(send_scales, "req", split_axis=0, concat_axis=0, tiled=True)
    own_holders = lax.dynamic_index_in_dim(holders, own_index, 0, keepdims=False)
    position = jnp.arange(need_count, dtype=jnp.int32)
    earlier = (own_holders[:, None] == own_holders[None, :]) & (
        position[:, None] < position[None, :]
    )
    where_from = own_holders * capacity + jnp.sum(earlier.astype(jnp.int32), axis=0)

    hit_mask = (hit_blocks > 0).astype(F32)
    token_rows = jnp.arange(slots, dtype=jnp.int32)
    live_mask = (token_rows[None, :] < suffix_len[:, None]).astype(F32)
    step_size = jax.nn.softplus(dt_raw + dt_bias) * live_mask[:, :, None]
    log_decay = -jnp.exp(a_log) * jnp.cumsum(step_size, axis=1)
    inner_cb = jnp.einsum("rtn,rsn->rts", c_proj, b_proj, preferred_element_type=F32)
    causal = token_rows[:, None] >= token_rows[None, :]
    decay_gap = log_decay[:, :, None, :] - log_decay[:, None, :, :]
    decay_mat = jnp.exp(jnp.where(causal[None, :, :, None], decay_gap, -jnp.inf))
    mixer = (decay_mat * inner_cb[:, :, :, None] * step_size[:, None, :, :]).astype(BF16)
    x_heads = x_inputs.reshape(reqs_dev, slots, heads_tp, head_dim)
    within = jnp.einsum("rtsh,rshp->rthp", mixer, x_heads, preferred_element_type=F32)
    local = within + d_skip[:, None] * x_heads.astype(F32)
    gates = z_gates.reshape(reqs_dev, slots, heads_tp, head_dim).astype(F32)
    silu = jax.nn.silu(gates) * live_mask[:, :, None, None]
    log_total = log_decay[:, slots - 1, :]
    weight = jnp.exp(log_total[:, None, :] - log_decay) * step_size
    x_weighted = (x_heads.astype(F32) * weight[:, :, :, None]).astype(BF16)
    accumulated = jnp.einsum(
        "rshp,rsn->rhpn", x_weighted, b_proj, preferred_element_type=F32
    )

    page_codes = got_codes[where_from].reshape(reqs_dev, heads_tp, head_dim, state_width)
    row_scales = (
        got_scales[where_from].reshape(reqs_dev, heads_tp, head_dim).astype(F32)
        * hit_mask[:, None, None]
    )
    from_start = jnp.einsum(
        "rtn,rhpn->rthp", c_proj, page_codes, preferred_element_type=F32
    )
    y_total = (
        local + jnp.exp(log_decay)[:, :, :, None] * row_scales[:, None, :, :] * from_start
    )
    gated = (y_total * silu).astype(BF16).reshape(tokens, inner_tp)
    start_state = page_codes.astype(F32) * row_scales[:, :, :, None]
    end_state = (jnp.exp(log_total)[:, :, None, None] * start_state + accumulated).astype(BF16)
    end_state = end_state.reshape(reqs_dev, inner_tp, state_width)

    theirs = swapped(gated, "req", 1)
    own_rows = ordered(tp_index == 0, gated, swapped(gated, "tp", 1), 1)
    their_rows = ordered(tp_index == 0, theirs, swapped(theirs, "tp", 1), 1)

    if chain:
        spot = own_index // 2
        inner = (spot == 1) | (spot == 2)
        low = spot < 2
        second_outer = lax.ppermute(second_inner, "req", outward)
        second = jnp.where(inner, second_inner, second_outer)
        third_inner = lax.ppermute(near, "req", middle)
        third_outer = lax.ppermute(third_inner, "req", outward)
        third = jnp.where(inner, third_inner, third_outer)
        items = [block] + [
            ordered(group == 0, part, swapped(part, "groups", 1), 0)
            for part in (near, second, third)
        ]

        def in_order(parts):
            own, one, two, three = parts
            return (
                jnp.where(spot == 0, own, jnp.where(spot == 1, one, three)),
                jnp.where(spot == 0, one, jnp.where(spot == 1, own, two)),
                jnp.where(spot == 2, own, jnp.where(spot == 3, one, two)),
                jnp.where(spot == 2, one, jnp.where(spot == 3, own, three)),
            )
    else:
        parity = [list(range(first, n_req, 2)) for first in range(2)]
        mine = lax.all_gather(piece, "req", axis=0, axis_index_groups=parity)
        whole = ordered(group == 0, mine, swapped(mine, "groups", 1), 1)
        items = [whole.reshape(line * columns, whole.shape[2])]

        def in_order(parts):
            one = parts[0].reshape(tokens, line, columns)
            return tuple(one[:, at] for at in range(line))

    came = in_order([swapped(rows_times(their_rows, item), "req", 1) for item in items])
    kept = in_order([rows_times(own_rows, item) for item in items])
    even = own_index % 2 == 0
    columns_out = []
    for mine, other in zip(kept, came):
        columns_out += [jnp.where(even, mine, other), jnp.where(even, other, mine)]
    mixed_out = jnp.concatenate(columns_out, axis=1).reshape(reqs_dev, slots, n_req * columns)
    return (mixed_out, end_state)


def solution(mesh):
    in_specs = (
        P(("groups", "req"), None, "tp"),
        P(("groups", "req"), None, "tp"),
        P(("groups", "req"), None, None),
        P(("groups", "req"), None, None),
        P(("groups", "req"), None, "tp"),
        P("tp"),
        P("tp"),
        P("tp"),
        P(("groups", "req", "tp"), None, None),
        P(("groups", "req", "tp"), None),
        P("tp", "groups", None, None),
        P("tp", "groups", None),
        P(("groups", "req")),
        P(("groups", "req")),
        P(None, "tp", "req"),
    )
    out_specs = (P(("groups", "req"), None, "tp"), P(("groups", "req"), "tp", None))
    return jax.shard_map(
        on_device, mesh=mesh, in_specs=in_specs, out_specs=out_specs, check_vma=False
    )
```

time: 449 us -> 300 us (0.67)
  waiting for transfers between devices: 332 us -> 180 us
  starting transfers between devices: 12.5 us -> 32.8 us
  between operations: 14.1 us -> 1.02 us
  local copies, waits for them, and re-layouts: 25.7 us -> 36.8 us
  matrix products: 37.9 us -> 30.4 us
  other arithmetic: 25.2 us -> 17.9 us
    all_gather x2 -> x0, waiting for transfers between devices: 158 us -> none  [the longest x1 144 us: on_device(): lax.all_gather(second_half, 'req', axis=1, tiled=True)]
    all_to_all x1, waiting for transfers between devices: 157 us -> 0.01 us  [on_device(): lax.all_to_all(pool_codes[wanted], 'req', split_axis=0, concat_axis=0, ti...]
    ppermute x0 -> x4, waiting for transfers between devices: none -> 128 us  [the longest x1 96 us: on_device(): second_inner = lax.ppermute(piece, 'req', middle)]
    ppermute x1 -> x11, waiting for transfers between devices: 3.15 us -> 51.8 us  [swapped(): return lax.ppermute(value, axis, pairs)]
    reduce_scatter x1 -> x0, waiting for transfers between devices: 12.5 us -> none  [on_device(): lax.psum_scatter(partial_value, 'tp', scatter_dimension=1, tiled=True)]
    ppermute x1 -> x11, starting transfers between devices: 0.07 us -> 10.2 us  [swapped(): return lax.ppermute(value, axis, pairs)]
    ppermute x0 -> x4, starting transfers between devices: none -> 9.76 us  [the longest x1 2.53 us: on_device(): third_inner = lax.ppermute(near, 'req', middle)]
    dynamic_update_slice x1 -> x0, other arithmetic: 9.12 us -> none  [on_device(): lax.dynamic_update_slice(total, upper, (jnp.int32(0), start + half_width))]
  transfers between devices with their start and end apart: 6 -> 17, of which waited for: 5 -> 9; matrix products, arithmetic and copies ran while one was open for 13% -> 21% of each run, Pallas kernels for 0% -> 0%
where the time goes in v1:
time: 300 us; the launch traced here: 299 us
  waiting for transfers between devices  180 us (60%)
  local copies, waits for them, and re-layouts  36.8 us (12%)
  starting transfers between devices  32.8 us (11%)
  matrix products  30.4 us (10%)
  other arithmetic  17.9 us (6%)
    ppermute x1, waiting for transfers between devices, on_device(): second_inner = lax.ppermute(piece, 'req', middle)  96 us
    ppermute x11, waiting for transfers between devices, swapped(): return lax.ppermute(value, axis, pairs)  51.8 us
    ppermute x1, waiting for transfers between devices, on_device(): third_inner = lax.ppermute(near, 'req', middle)  22.8 us
    dot_general x8, matrix products, rows_times(): lax.dot_general(tokens, block, (((1,), (1,)), ((), ())), preferred_elemen...  14.3 us
    unnamed x29, local copies, waits for them, and re-layouts  14.2 us
    ppermute x11, starting transfers between devices, swapped(): return lax.ppermute(value, axis, pairs)  10.2 us
    ppermute x1, waiting for transfers between devices, on_device(): third_outer = lax.ppermute(third_inner, 'req', outward)  9.36 us
    dot_general x1, matrix products, on_device(): jnp.einsum('rtn,rhpn->rthp', c_proj, page_codes, preferred_element_type=F32)  6.67 us
  transfers between devices with their start and end apart: 17, of which 9 were waited for; matrix products, arithmetic and copies ran while one was open for 21% of the time, Pallas kernels for 0%

profile of v1, /device:TPU:16, one launch (start us, length us, event | category | flops | bytes accessed | tf_op | source)
XLA Modules:
  0.0 298.9 jit_solution(9927927592109134385)
XLA Ops:
  0.7 0.5 broadcast.159
  1.2 1.6 reduce.7
  3.1 0.8 broadcast_in_dim.24
  4.2 1.4 gather_fusion
  5.6 0.7 reshape.257
  6.3 6.2 %all-to-all-start = ((bf16[8,2,512]{2,1,0:T(2,128)(2,1)}), bf16[8,2,512]{2,1,0:T(2,128)(2,1)S(1)}, u32[]{:S(2)}, u32[]{:S(2)}) async-start(bf16[8,2,512]{2,1,0:T(2,128)(2,1)} %reshape.257), calls=%async_computation | async-start | bytes 32768 | tf_op jit(solution)/shard_map/all_to_all | solution.py:84
  12.4 4.4 %gather_fusion.2 = bf16[128,64,256]{2,1,0:T(8,128)(2,1)} fusion(bf16[64,64,256]{2,1,0:T(8,128)(2,1)} %param.23, s32[1024]{0:T(1024)S(1)} %pad_clamp_fusion.1), kind=kCustom, calls=%fused_computation.2 | custom fusion | bytes 8389120 | tf_op jit(solution)/shard_map/gather | solution.py:81
  16.8 6.6 %all-to-all-start.1 = ((bf16[128,64,256]{2,1,0:T(8,128)(2,1)}), bf16[128,64,256]{2,1,0:T(8,128)(2,1)}, u32[]{:S(2)}, u32[]{:S(2)}) async-start(bf16[128,64,256]{2,1,0:T(8,128)(2,1)} %gather_fusion.2), calls=%async_computation.1 | async-start | bytes 8388608 | tf_op jit(solution)/shard_map/all_to_all | solution.py:80
  23.5 1.2 dynamic-slice_bitcast_fusion
  24.7 2.4 collective-permute-start.11
  27.2 0.7 collective-permute-start.1
  28.1 1.2 reduce-window.6
  29.6 3.9 %copy.35 = bf16[2,256,2048]{1,2,0:T(8,128)(2,1)} copy(bf16[2,256,2048]{2,1,0:T(8,128)(2,1)} %param.15) | data formatting | bytes 4194304 | tf_op args[0]
  33.5 3.9 %copy.37 = bf16[2,256,16,128]{3,1,2,0:T(8,128)(2,1)} copy(bf16[2,256,16,128]{1,3,2,0:T(8,128)(2,1)} %bitcast.85) | data formatting | bytes 4194304 | tf_op jit(solution)/shard_map/reshape | solution.py:102
  37.5 3.9 %copy.39 = bf16[2,256,2048]{1,2,0:T(8,128)(2,1)} copy(bf16[2,256,2048]{2,1,0:T(8,128)(2,1)} %param.16) | data formatting | bytes 4194304 | tf_op args[1]
  41.4 4.2 %copy.41 = f32[2,256,16,128]{3,1,2,0:T(8,128)} copy(bf16[2,256,16,128]{1,3,2,0:T(8,128)(2,1)} %bitcast.84) | data formatting | bytes 6291456 | tf_op jit(solution)/shard_map/convert_element_type | solution.py:105
  46.2 96.0 %collective-permute-done.11 = bf16[160,4096]{1,0:T(8,128)(2,1)} collective-permute-done((bf16[160,4096]{1,0:T(8,128)(2,1)}, bf16[160,4096]{1,0:T(8,128)(2,1)}, u32[]{:S(2)}, u32[]{:S(2)}) %collective-permute-start.11) | collective-permute-done | bytes 1310752 | tf_op jit(solution)/shard_map/ppermute | solution.py:68
  142.2 2.4 collective-permute-start.12
  144.6 2.5 collective-permute-start.3
  147.5 4.9 %fusion = f32[2,16,256,128]{3,2,1,0:T(8,128)} fusion(bf16[2,256,16,128]{1,3,2,0:T(8,128)(2,1)} %bitcast.86, f32[2,256,16]{1,2,0:T(8,128)S(1)} %fusion.39, f32[2,256,256]{2,1,0:T(8,128)S(1)} %fusion.55, f32[2,256,16]{1,2,0:T(8,128)S(1)} %get-tuple-element.21, pred[256,256]{1,0:T(8,128)(4,1)S(1)} %iota_compare_fusion), kind=kOutput, calls=%fused_computation.7 | convolution fusion | flops 547356672 | bytes 6946816 | tf_op jit(solution)/shard_map/rtsh,rshp->rthp/dot_general | solution.py:103
  152.5 0.6 gather_fusion.1
  153.3 1.5 collective-permute-start.2
  154.7 22.8 %collective-permute-done.3 = bf16[160,4096]{1,0:T(8,128)(2,1)} collective-permute-done((bf16[160,4096]{1,0:T(8,128)(2,1)}, bf16[160,4096]{1,0:T(8,128)(2,1)}, u32[]{:S(2)}, u32[]{:S(2)}) %collective-permute-start.3) | collective-permute-done | bytes 1310752 | tf_op jit(solution)/shard_map/ppermute | solution.py:140
  177.5 2.4 collective-permute-start.4
  179.9 2.6 broadcast_select_fusion.4
  182.4 1.5 collective-permute-start.13
  183.9 4.2 %gather_fusion.3 = bf16[64,64,256]{2,1,0:T(8,128)(2,1)} fusion(bf16[128,64,256]{2,1,0:T(8,128)(2,1)} %all-to-all-done.1, s32[1024]{0:T(1024)S(1)} %pad_clamp_fusion), kind=kCustom, calls=%fused_computation.3 | custom fusion | bytes 4194560 | tf_op jit(solution)/shard_map/gather | solution.py:114
  188.1 6.7 %fusion.4 = bf16[2,256,16,128]{3,1,2,0:T(8,128)(2,1)S(1)} fusion(bf16[2,256,16,128]{3,1,2,0:T(8,128)(2,1)} %copy.37, f32[2,16,256,128]{3,2,1,0:T(8,128)} %fusion, f32[2,256,16,128]{3,1,2,0:T(8,128)} %copy.41, bf16[2,16,128,256]{3,2,1,0:T(8,128)(2,1)} %bitcast.88, f32[2,256]{1,0:T(2,128)S(1)} %compare_convert_fusion, ...), kind=kOutput, calls=%fused_computation.11 | convolution fusion | flops 550502400 | bytes 14993472 | tf_op jit(solution)/shard_map/rtn,rhpn->rthp/dot_general | solution.py:119
  194.8 1.4 copy.42
  196.2 0.5 copy.62
  196.7 0.7 collective-permute-start.6
  197.4 9.4 %collective-permute-done.4 = bf16[160,4096]{1,0:T(8,128)(2,1)} collective-permute-done((bf16[160,4096]{1,0:T(8,128)(2,1)}, bf16[160,4096]{1,0:T(8,128)(2,1)}, u32[]{:S(2)}, u32[]{:S(2)}) %collective-permute-start.4) | collective-permute-done | bytes 1310752 | tf_op jit(solution)/shard_map/ppermute | solution.py:141
  206.8 1.5 broadcast_select_fusion.5
  208.2 1.6 collective-permute-start.5
  209.8 1.9 broadcast_select_fusion.11
  211.7 2.7 collective-permute-done.13
  214.5 1.9 broadcast_select_fusion.7
  216.4 26.8 %collective-permute-done.6 = bf16[512,2048]{1,0:T(8,128)(2,1)S(1)} collective-permute-done((bf16[512,2048]{1,0:T(8,128)(2,1)S(1)}, bf16[512,2048]{1,0:T(8,128)(2,1)S(1)}, u32[]{:S(2)}, u32[]{:S(2)}) %collective-permute-start.6) | collective-permute-done | bytes 2097184 | tf_op jit(solution)/shard_map/ppermute | solution.py:12
  243.4 4.3 %add_convert_fusion = bf16[2,16,128,256]{3,2,1,0:T(8,128)(2,1)} fusion(bf16[2,16,128,256]{3,2,1,0:T(8,128)(2,1)S(1)} %bitcast.89, bf16[2,256,16,128]{3,1,2,0:T(8,128)(2,1)S(1)} %copy-done.1, f32[2,256,16]{1,2,0:T(8,128)S(1)} %exponential_multiply_fusion, f32[2,16,128]{2,1,0:T(8,128)S(1)} %broadcast_multiply_fusion, f32[2,16]{1,0:T(2,128)S(1)} %exp.32, ...), kind=kOutput, calls=%fused_computation.16 | convolution fusion | flops 545259520 | bytes 6602880 | tf_op jit(solution)/shard_map/rshp,rsn->rhpn/dot_general | solution.py:110
  247.7 0.5 broadcast_select_fusion.3
  248.1 1.5 fusion.26
  249.7 1.5 fusion.24
  251.3 0.3 broadcast_select_fusion.1
  251.5 1.5 fusion.27
  253.1 1.5 fusion.25
  254.7 1.7 fusion.33
  256.4 0.7 collective-permute-start.10
  257.0 1.4 collective-permute-start.9
  258.4 0.6 collective-permute-start.8
  259.1 1.5 fusion.29
  260.6 1.5 collective-permute-start.14
  262.1 4.8 %collective-permute-done.10 = bf16[512,320]{0,1:T(8,128)(2,1)S(1)} collective-permute-done((bf16[512,320]{0,1:T(8,128)(2,1)S(1)}, bf16[512,320]{0,1:T(8,128)(2,1)S(1)}, u32[]{:S(2)}, u32[]{:S(2)}) %collective-permute-start.10) | collective-permute-done | bytes 327712 | tf_op jit(solution)/shard_map/ppermute | solution.py:12
  266.9 7.0 %collective-permute-done.9 = bf16[512,320]{0,1:T(8,128)(2,1)S(1)} collective-permute-done((bf16[512,320]{0,1:T(8,128)(2,1)S(1)}, bf16[512,320]{0,1:T(8,128)(2,1)S(1)}, u32[]{:S(2)}, u32[]{:S(2)}) %collective-permute-start.9) | collective-permute-done | bytes 327712 | tf_op jit(solution)/shard_map/ppermute | solution.py:12
  273.9 7.0 %collective-permute-done.8 = bf16[512,320]{0,1:T(8,128)(2,1)S(1)} collective-permute-done((bf16[512,320]{0,1:T(8,128)(2,1)S(1)}, bf16[512,320]{0,1:T(8,128)(2,1)S(1)}, u32[]{:S(2)}, u32[]{:S(2)}) %collective-permute-start.8) | collective-permute-done | bytes 327712 | tf_op jit(solution)/shard_map/ppermute | solution.py:12
  281.0 2.5 select_dynamic-update-slice_fusion.7
  283.4 0.8 select_dynamic-update-slice_fusion.6
  284.3 3.4 %collective-permute-done.14 = bf16[512,320]{0,1:T(8,128)(2,1)S(1)} collective-permute-done((bf16[512,320]{0,1:T(8,128)(2,1)S(1)}, bf16[512,320]{0,1:T(8,128)(2,1)S(1)}, u32[]{:S(2)}, u32[]{:S(2)}) %collective-permute-start.14) | collective-permute-done | bytes 327712 | tf_op jit(solution)/shard_map/ppermute | solution.py:12
  287.6 2.4 select_dynamic-update-slice_fusion.5
  290.0 0.8 select_dynamic-update-slice_fusion.4
  290.9 1.0 select_dynamic-update-slice_fusion.3
  291.9 0.8 select_dynamic-update-slice_fusion.2
  292.7 1.0 select_dynamic-update-slice_fusion.1
  293.7 0.8 select_dynamic-update-slice_fusion
  294.5 4.4 %copy.50 = bf16[512,2560]{1,0:T(8,128)(2,1)} copy(bf16[512,2560]{0,1:T(8,128)(2,1)} %select_dynamic-update-slice_fusion) | data formatting | bytes 5242880
  (62 shorter events, 2.4 us)
Async XLA Ops:
  0.6 22.8 %copy-start = (bf16[4096,1,320]{0,2,1:T(8,128)(2,1)S(1)}, bf16[4096,1,320]{0,2,1:T(8,128)(2,1)}, u32[]{:S(2)}) copy-start(bf16[4096,1,320]{0,2,1:T(8,128)(2,1)} %param.29) | copy-start | bytes 7864324
  6.3 10.6 %all-to-all-start = ((bf16[8,2,512]{2,1,0:T(2,128)(2,1)}), bf16[8,2,512]{2,1,0:T(2,128)(2,1)S(1)}, u32[]{:S(2)}, u32[]{:S(2)}) async-start(bf16[8,2,512]{2,1,0:T(2,128)(2,1)} %reshape.257), calls=%async_computation | async-start | bytes 32768 | tf_op jit(solution)/shard_map/all_to_all | solution.py:84
  16.8 167.1 %all-to-all-start.1 = ((bf16[128,64,256]{2,1,0:T(8,128)(2,1)}), bf16[128,64,256]{2,1,0:T(8,128)(2,1)}, u32[]{:S(2)}, u32[]{:S(2)}) async-start(bf16[128,64,256]{2,1,0:T(8,128)(2,1)} %gather_fusion.2), calls=%async_computation.1 | async-start | bytes 8388608 | tf_op jit(solution)/shard_map/all_to_all | solution.py:80
  23.4 4.5 %copy-start.7 = (s32[2]{0:T(128)S(1)}, s32[2]{0:T(128)}, u32[]{:S(2)}) copy-start(s32[2]{0:T(128)} %param.28) | copy-start | bytes 28
  23.4 4.5 %copy-start.3 = (f32[2,256,16]{1,2,0:T(8,128)S(1)}, f32[2,256,16]{1,2,0:T(8,128)}, u32[]{:S(2)}) copy-start(f32[2,256,16]{1,2,0:T(8,128)} %param.19) | copy-start | bytes 98308
  23.5 4.5 %copy-start.6 = (f32[16]{0:T(128)S(1)}, f32[16]{0:T(128)}, u32[]{:S(2)}) copy-start(f32[16]{0:T(128)} %param.20) | copy-start | bytes 196
  23.5 6.0 %copy-start.8 = (f32[16]{0:T(128)S(1)}, f32[16]{0:T(128)}, u32[]{:S(2)}) copy-start(f32[16]{0:T(128)} %param.21) | copy-start | bytes 196
  24.7 117.5 %collective-permute-start.11 = (bf16[160,4096]{1,0:T(8,128)(2,1)}, bf16[160,4096]{1,0:T(8,128)(2,1)}, u32[]{:S(2)}, u32[]{:S(2)}) collective-permute-start(bf16[160,4096]{1,0:T(8,128)(2,1)} %dynamic-slice_bitcast_fusion), channel_id=1, source_target_pairs={{4,8},{8,4},{6,10},{10,6},{5,9},{9,5},{7,11},{11,7},{20,24},{24,20... | collective-permute-start | bytes 3932168 | tf_op jit(solution)/shard_map/ppermute | solution.py:68
  27.2 117.5 %collective-permute-start.1 = (bf16[160,4096]{1,0:T(8,128)(2,1)}, bf16[160,4096]{1,0:T(8,128)(2,1)}, u32[]{:S(2)}, u32[]{:S(2)}) collective-permute-start(bf16[160,4096]{1,0:T(8,128)(2,1)} %dynamic-slice_bitcast_fusion), channel_id=1, source_target_pairs={{0,4},{2,6},{4,0},{6,2},{8,12},{10,14},{12,8},{14,10},{1,5},{3,7},... | collective-permute-start | bytes 3932168 | tf_op jit(solution)/shard_map/ppermute | solution.py:12
  41.4 105.7 %copy-start.9 = (s32[2]{0:T(128)S(1)}, s32[2]{0:T(128)}, u32[]{:S(2)}) copy-start(s32[2]{0:T(128)} %param.27) | copy-start | bytes 28
  41.4 105.8 %copy-start.4 = (bf16[2,256,256]{2,1,0:T(8,128)(2,1)S(1)}, bf16[2,256,256]{2,1,0:T(8,128)(2,1)}, u32[]{:S(2)}) copy-start(bf16[2,256,256]{2,1,0:T(8,128)(2,1)} %param.18) | copy-start | bytes 786436
  41.4 105.8 %copy-start.5 = (bf16[2,256,256]{2,1,0:T(8,128)(2,1)S(1)}, bf16[2,256,256]{2,1,0:T(8,128)(2,1)}, u32[]{:S(2)}) copy-start(bf16[2,256,256]{2,1,0:T(8,128)(2,1)} %param.17) | copy-start | bytes 786436
  142.2 37.7 %collective-permute-start.12 = (bf16[160,4096]{1,0:T(8,128)(2,1)}, bf16[160,4096]{1,0:T(8,128)(2,1)}, u32[]{:S(2)}, u32[]{:S(2)}) collective-permute-start(bf16[160,4096]{1,0:T(8,128)(2,1)} %collective-permute-done.11), channel_id=1, source_target_pairs={{4,0},{6,2},{8,12},{10,14},{5,1},{7,3},{9,13},{11,15},{20,16},{22,... | collective-permute-start | bytes 3932168 | tf_op jit(solution)/shard_map/ppermute | solution.py:138
  144.6 32.9 %collective-permute-start.3 = (bf16[160,4096]{1,0:T(8,128)(2,1)}, bf16[160,4096]{1,0:T(8,128)(2,1)}, u32[]{:S(2)}, u32[]{:S(2)}) collective-permute-start(bf16[160,4096]{1,0:T(8,128)(2,1)} %collective-permute-done.1), channel_id=1, source_target_pairs={{4,8},{8,4},{6,10},{10,6},{5,9},{9,5},{7,11},{11,7},{20,24},{24,20... | collective-permute-start | bytes 3932168 | tf_op jit(solution)/shard_map/ppermute | solution.py:140
  153.3 56.5 %collective-permute-start.2 = (bf16[160,4096]{1,0:T(8,128)(2,1)}, bf16[160,4096]{1,0:T(8,128)(2,1)}, u32[]{:S(2)}, u32[]{:S(2)}) collective-permute-start(bf16[160,4096]{1,0:T(8,128)(2,1)} %collective-permute-done.1), channel_id=1, source_target_pairs={{0,16},{16,0},{1,17},{17,1},{2,18},{18,2},{3,19},{19,3},{4,20},{20... | collective-permute-start | bytes 3932168 | tf_op jit(solution)/shard_map/ppermute | solution.py:12
  177.5 29.2 %collective-permute-start.4 = (bf16[160,4096]{1,0:T(8,128)(2,1)}, bf16[160,4096]{1,0:T(8,128)(2,1)}, u32[]{:S(2)}, u32[]{:S(2)}) collective-permute-start(bf16[160,4096]{1,0:T(8,128)(2,1)} %collective-permute-done.3), channel_id=1, source_target_pairs={{4,0},{6,2},{8,12},{10,14},{5,1},{7,3},{9,13},{11,15},{20,16},{22,... | collective-permute-start | bytes 3932168 | tf_op jit(solution)/shard_map/ppermute | solution.py:141
  182.4 5.7 %copy-start.10 = (f32[16]{0:T(128)S(1)}, f32[16]{0:T(128)}, u32[]{:S(2)}) copy-start(f32[16]{0:T(128)} %param.22) | copy-start | bytes 196
  182.4 32.0 %collective-permute-start.13 = (bf16[160,4096]{1,0:T(8,128)(2,1)}, bf16[160,4096]{1,0:T(8,128)(2,1)}, u32[]{:S(2)}, u32[]{:S(2)}) collective-permute-start(bf16[160,4096]{1,0:T(8,128)(2,1)} %broadcast_select_fusion.4), channel_id=1, source_target_pairs={{0,16},{16,0},{1,17},{17,1},{2,18},{18,2},{3,19},{19,3},{4,20},{20... | collective-permute-start | bytes 3932168 | tf_op jit(solution)/shard_map/ppermute | solution.py:12
  196.7 46.5 %collective-permute-start.6 = (bf16[512,2048]{1,0:T(8,128)(2,1)S(1)}, bf16[512,2048]{1,0:T(8,128)(2,1)S(1)}, u32[]{:S(2)}, u32[]{:S(2)}) collective-permute-start(bf16[512,2048]{1,0:T(8,128)(2,1)S(1)} %bitcast.90), channel_id=1, source_target_pairs={{0,2},{2,0},{4,6},{6,4},{8,10},{10,8},{12,14},{14,12},{1,3},{3,1},... | collective-permute-start | bytes 6291464 | tf_op jit(solution)/shard_map/ppermute | solution.py:12
  208.2 35.0 %collective-permute-start.5 = (bf16[160,4096]{1,0:T(8,128)(2,1)S(1)}, bf16[160,4096]{1,0:T(8,128)(2,1)S(1)}, u32[]{:S(2)}, u32[]{:S(2)}) collective-permute-start(bf16[160,4096]{1,0:T(8,128)(2,1)S(1)} %broadcast_select_fusion.5), channel_id=1, source_target_pairs={{0,16},{16,0},{1,17},{17,1},{2,18},{18,2},{3,19},{19,3},{4,20},{20... | collective-permute-start | bytes 3932168 | tf_op jit(solution)/shard_map/ppermute | solution.py:12
  211.7 36.0 %collective-permute-start = (bf16[512,2048]{1,0:T(8,128)(2,1)S(1)}, bf16[512,2048]{1,0:T(8,128)(2,1)S(1)}, u32[]{:S(2)}, u32[]{:S(2)}) collective-permute-start(bf16[512,2048]{1,0:T(8,128)(2,1)S(1)} %bitcast.91), channel_id=1, source_target_pairs={{0,1},{1,0},{2,3},{3,2},{4,5},{5,4},{6,7},{7,6},{8,9},{9,8},{10,11... | collective-permute-start | bytes 6291464 | tf_op jit(solution)/shard_map/ppermute | solution.py:12
  216.4 27.0 %copy-start.1 = (bf16[2,256,16,128]{3,1,2,0:T(8,128)(2,1)S(1)}, bf16[2,256,16,128]{3,1,2,0:T(8,128)(2,1)}, u32[]{:S(2)}) copy-start(bf16[2,256,16,128]{3,1,2,0:T(8,128)(2,1)} %copy.37) | copy-start | bytes 6291460
  216.4 27.0 %copy-start.2 = (bf16[64,64,256]{2,1,0:T(8,128)(2,1)S(1)}, bf16[64,64,256]{2,1,0:T(8,128)(2,1)}, u32[]{:S(2)}) copy-start(bf16[64,64,256]{2,1,0:T(8,128)(2,1)} %gather_fusion.3) | copy-start | bytes 6291460
  243.2 8.1 %collective-permute-start.7 = (bf16[512,2048]{1,0:T(8,128)(2,1)S(1)}, bf16[512,2048]{1,0:T(8,128)(2,1)S(1)}, u32[]{:S(2)}, u32[]{:S(2)}) collective-permute-start(bf16[512,2048]{1,0:T(8,128)(2,1)S(1)} %collective-permute-done.6), channel_id=1, source_target_pairs={{0,1},{1,0},{2,3},{3,2},{4,5},{5,4},{6,7},{7,6},{8,9},{9,8},{10,11... | collective-permute-start | bytes 6291464 | tf_op jit(solution)/shard_map/ppermute | solution.py:12
  256.4 10.6 %collective-permute-start.10 = (bf16[512,320]{0,1:T(8,128)(2,1)S(1)}, bf16[512,320]{0,1:T(8,128)(2,1)S(1)}, u32[]{:S(2)}, u32[]{:S(2)}) collective-permute-start(bf16[512,320]{0,1:T(8,128)(2,1)S(1)} %fusion.27), channel_id=1, source_target_pairs={{0,2},{2,0},{4,6},{6,4},{8,10},{10,8},{12,14},{14,12},{1,3},{3,1},... | collective-permute-start | bytes 983048 | tf_op jit(solution)/shard_map/ppermute | solution.py:12
  257.0 16.9 %collective-permute-start.9 = (bf16[512,320]{0,1:T(8,128)(2,1)S(1)}, bf16[512,320]{0,1:T(8,128)(2,1)S(1)}, u32[]{:S(2)}, u32[]{:S(2)}) collective-permute-start(bf16[512,320]{0,1:T(8,128)(2,1)S(1)} %fusion.25), channel_id=1, source_target_pairs={{0,2},{2,0},{4,6},{6,4},{8,10},{10,8},{12,14},{14,12},{1,3},{3,1},... | collective-permute-start | bytes 983048 | tf_op jit(solution)/shard_map/ppermute | solution.py:12
  258.4 22.5 %collective-permute-start.8 = (bf16[512,320]{0,1:T(8,128)(2,1)S(1)}, bf16[512,320]{0,1:T(8,128)(2,1)S(1)}, u32[]{:S(2)}, u32[]{:S(2)}) collective-permute-start(bf16[512,320]{0,1:T(8,128)(2,1)S(1)} %fusion.33), channel_id=1, source_target_pairs={{0,2},{2,0},{4,6},{6,4},{8,10},{10,8},{12,14},{14,12},{1,3},{3,1},... | collective-permute-start | bytes 983048 | tf_op jit(solution)/shard_map/ppermute | solution.py:12
  260.6 27.0 %collective-permute-start.14 = (bf16[512,320]{0,1:T(8,128)(2,1)S(1)}, bf16[512,320]{0,1:T(8,128)(2,1)S(1)}, u32[]{:S(2)}, u32[]{:S(2)}) collective-permute-start(bf16[512,320]{0,1:T(8,128)(2,1)S(1)} %fusion.29), channel_id=1, source_target_pairs={{0,2},{2,0},{4,6},{6,4},{8,10},{10,8},{12,14},{14,12},{1,3},{3,1},... | collective-permute-start | bytes 983048 | tf_op jit(solution)/shard_map/ppermute | solution.py:12

commit v2 on v1

v2 whole, which is shorter than its diff:
```python
import jax
import jax.numpy as jnp
from jax import lax
from jax.experimental import pallas as pl
from jax.experimental.pallas import tpu as pltpu
from jax.sharding import PartitionSpec as P

BF16 = jnp.bfloat16
F32 = jnp.float32


def swapped(value, axis, mask):
    pairs = [(source, source ^ mask) for source in range(lax.axis_size(axis))]
    return lax.ppermute(value, axis, pairs)


NO_COST = pl.CostEstimate(flops=0, bytes_accessed=0, transcendentals=0)
ANYWHERE = pl.BlockSpec(memory_space=pl.ANY)


def after(value, *earlier):
    return lax.optimization_barrier((value,) + earlier)[0]


def held(value, *earlier):
    return pl.pallas_call(
        lambda *refs: None,
        out_shape=jax.ShapeDtypeStruct(value.shape, value.dtype),
        in_specs=[ANYWHERE] * (1 + len(earlier)),
        out_specs=ANYWHERE,
        input_output_aliases={0: 0},
        cost_estimate=NO_COST,
    )(value, *earlier)


def local_kernel(
    heads, skip_ref, x_ref, z_ref, b_ref, c_ref, log_ref, log_rows_ref, step_rows_ref, start_ref, live_ref, *refs
):
    local_ref, factor_ref = refs[-2:]
    slots = x_ref.shape[1]
    width = x_ref.shape[2] // heads
    cb = lax.dot_general(
        c_ref[0], b_ref[0], (((1,), (1,)), ((), ())), preferred_element_type=F32
    )
    later = lax.broadcasted_iota(jnp.int32, (slots, slots), 0)
    causal = later >= lax.broadcasted_iota(jnp.int32, (slots, slots), 1)
    live = live_ref[0]
    for head in range(heads):
        at = slice(head * width, (head + 1) * width)
        gap = log_ref[0, :, head : head + 1] - log_rows_ref[0, head : head + 1, :]
        decay = jnp.exp(jnp.where(causal, gap, -jnp.inf))
        mixer = (decay * cb * step_rows_ref[0, head : head + 1, :]).astype(BF16)
        x = x_ref[0, :, at]
        within = jnp.dot(mixer, x, preferred_element_type=F32)
        z = z_ref[0, :, at].astype(F32)
        silu = z / (1.0 + jnp.exp(-z)) * live
        local_ref[0, :, at] = (within + skip_ref[head] * x.astype(F32)) * silu
        factor_ref[0, :, at] = start_ref[0, :, head : head + 1] * silu


def local_part(d_skip, x_inputs, z_gates, b_proj, c_proj, log_decay, step_size, start_share, live_mask, earlier):
    reqs_dev, slots, inner_tp = x_inputs.shape
    heads = log_decay.shape[2]
    operands = (
        x_inputs,
        z_gates,
        b_proj,
        c_proj,
        log_decay,
        log_decay.transpose(0, 2, 1),
        step_size.transpose(0, 2, 1),
        start_share,
        live_mask[:, :, None],
    )

    def one(array):
        return pl.BlockSpec((1,) + array.shape[1:], lambda request: (request, 0, 0))

    out = jax.ShapeDtypeStruct((reqs_dev, slots, inner_tp), F32)
    return pl.pallas_call(
        lambda *refs: local_kernel(heads, *refs),
        out_shape=[out, out],
        grid=(reqs_dev,),
        in_specs=[pl.BlockSpec(memory_space=pltpu.SMEM)]
        + [one(array) for array in operands]
        + [ANYWHERE] * len(earlier),
        out_specs=[one(out), one(out)],
        compiler_params=pltpu.CompilerParams(vmem_limit_bytes=48 * 2**20),
        cost_estimate=NO_COST,
    )(d_skip, *operands, *earlier)


def state_kernel(heads, where_ref, kept_ref, pages_ref, x_ref, b_ref, weight_ref, out_ref):
    request = pl.program_id(0)
    width = x_ref.shape[2] // heads
    pages = width // pages_ref.shape[1]
    for head in range(heads):
        at = slice(head * width, (head + 1) * width)
        first = (request * heads + head) * pages
        start = jnp.concatenate([pages_ref[where_ref[first + page]] for page in range(pages)], axis=0)
        weighted = (x_ref[0, :, at].astype(F32) * weight_ref[0, :, head : head + 1]).astype(BF16)
        added = lax.dot_general(
            weighted, b_ref[0], (((0,), (0,)), ((), ())), preferred_element_type=F32
        )
        out_ref[0, at, :] = (kept_ref[request, head] * start.astype(F32) + added).astype(BF16)


def state_part(where_from, kept_share, got_pages, x_inputs, b_proj, weight):
    reqs_dev, _, inner_tp = x_inputs.shape
    heads = weight.shape[2]

    def one(array):
        return pl.BlockSpec((1,) + array.shape[1:], lambda request, where_ref, kept_ref: (request, 0, 0))

    out = jax.ShapeDtypeStruct((reqs_dev, inner_tp, b_proj.shape[2]), BF16)
    return pl.pallas_call(
        lambda *refs: state_kernel(heads, *refs),
        out_shape=out,
        grid_spec=pltpu.PrefetchScalarGridSpec(
            num_scalar_prefetch=2,
            grid=(reqs_dev,),
            in_specs=[pl.BlockSpec(memory_space=pltpu.VMEM), one(x_inputs), one(b_proj), one(weight)],
            out_specs=one(out),
        ),
        compiler_params=pltpu.CompilerParams(vmem_limit_bytes=48 * 2**20),
        cost_estimate=NO_COST,
    )(where_from, kept_share, got_pages, x_inputs, b_proj, weight)


def gate_kernel(pages, where_ref, pages_ref, c_ref, local_ref, factor_ref, *refs):
    request, step = pl.program_id(0), pl.program_id(1)
    first = (request * pl.num_programs(1) + step) * pages
    start = jnp.concatenate([pages_ref[where_ref[first + at]] for at in range(pages)], axis=0)
    from_start = lax.dot_general(
        c_ref[0], start, (((1,), (1,)), ((), ())), preferred_element_type=F32
    )
    refs[-1][...] = (local_ref[0] + factor_ref[0] * from_start).astype(BF16)


def gate(where_from, got_pages, c_proj, local, factor, earlier):
    reqs_dev, slots, inner_tp = local.shape
    _, page_rows, state_width = got_pages.shape
    pages = min(8, inner_tp // page_rows)
    wide = pages * page_rows
    steps = inner_tp // wide
    wide_spec = pl.BlockSpec((1, slots, wide), lambda request, step, where_ref: (request, 0, step))

    return pl.pallas_call(
        lambda *refs: gate_kernel(pages, *refs),
        out_shape=jax.ShapeDtypeStruct((reqs_dev * slots, inner_tp), BF16),
        grid_spec=pltpu.PrefetchScalarGridSpec(
            num_scalar_prefetch=1,
            grid=(reqs_dev, steps),
            in_specs=[
                pl.BlockSpec(memory_space=pltpu.VMEM),
                pl.BlockSpec(
                    (1, slots, state_width), lambda request, step, where_ref: (request, 0, 0)
                ),
                wide_spec,
                wide_spec,
            ]
            + [ANYWHERE] * len(earlier),
            out_specs=pl.BlockSpec((slots, wide), lambda request, step, where_ref: (request, step)),
        ),
        compiler_params=pltpu.CompilerParams(vmem_limit_bytes=48 * 2**20),
        cost_estimate=NO_COST,
    )(where_from, got_pages, c_proj, local, factor, *earlier)


def project_kernel(rows, blocks, earlier, place_ref, *refs):
    row_refs, block_refs = refs[: len(rows)], refs[len(rows) : len(rows) + len(blocks)]
    out_ref, held_rows, held_blocks, sems = refs[len(rows) + len(blocks) + earlier :]
    copies = []
    for at, (ref, (first, count, width)) in enumerate(zip(row_refs, rows)):
        lanes = pl.ds(pl.multiple_of(place_ref[at], 128), width)
        copies.append(
            pltpu.make_async_copy(ref, held_rows.at[pl.ds(first, count), lanes], sems.at[at])
        )
    for at, (ref, count) in enumerate(zip(block_refs, blocks), len(rows)):
        first = place_ref[at]
        first = 0 if len(blocks) == 1 else pl.multiple_of(first, 16)
        copies.append(
            pltpu.make_async_copy(ref, held_blocks.at[pl.ds(first, count)], sems.at[at])
        )
    for copy in copies:
        copy.start()
    for copy in copies:
        copy.wait()
    columns = held_blocks.shape[0]
    for first in range(0, columns, 256):
        at = slice(first, min(first + 256, columns))
        out_ref[:, at] = lax.dot_general(
            held_rows[...], held_blocks[at, :], (((1,), (1,)), ((), ())), preferred_element_type=F32
        ).astype(BF16)


def project(rows, blocks, earlier=()):
    count = max(first + array.shape[0] for array, first, _ in rows)
    columns = sum(array.shape[0] for array, _ in blocks)
    inner = blocks[0][0].shape[1]
    place = jnp.stack(
        [jnp.asarray(at, jnp.int32) for _, _, at in rows]
        + [jnp.asarray(at, jnp.int32) for _, at in blocks]
    )
    row_plan = [(first,) + array.shape for array, first, _ in rows]
    block_plan = [array.shape[0] for array, _ in blocks]
    return pl.pallas_call(
        lambda *refs: project_kernel(row_plan, block_plan, len(earlier), *refs),
        out_shape=jax.ShapeDtypeStruct((count, columns), BF16),
        grid_spec=pltpu.PrefetchScalarGridSpec(
            num_scalar_prefetch=1,
            grid=(),
            in_specs=[ANYWHERE] * (len(rows) + len(blocks) + len(earlier)),
            out_specs=pl.BlockSpec(memory_space=pltpu.VMEM),
            scratch_shapes=[
                pltpu.VMEM((count, inner), BF16),
                pltpu.VMEM((columns, inner), BF16),
                pltpu.SemaphoreType.DMA((len(rows) + len(blocks),)),
            ],
        ),
        compiler_params=pltpu.CompilerParams(vmem_limit_bytes=40 * 2**20),
        cost_estimate=NO_COST,
    )(place, *[array for array, _, _ in rows], *[array for array, _ in blocks], *earlier)


def pick_kernel(flag_ref, yes_ref, no_ref, *refs):
    refs[-1][...] = jnp.where(flag_ref[0] == 1, yes_ref[...], no_ref[...])


def pick(flag, yes, no, earlier=()):
    rows, width = yes.shape
    spec = pl.BlockSpec((rows, width), lambda step: (0, 0))
    return pl.pallas_call(
        pick_kernel,
        out_shape=jax.ShapeDtypeStruct(yes.shape, yes.dtype),
        grid=(1,),
        in_specs=[pl.BlockSpec(memory_space=pltpu.SMEM), spec, spec] + [ANYWHERE] * len(earlier),
        out_specs=spec,
        cost_estimate=NO_COST,
    )(flag.astype(jnp.int32).reshape(1), yes, no, *earlier)


def halves_kernel(in_ref, low_ref, high_ref):
    half = low_ref.shape[0]
    low_ref[...] = in_ref[:half]
    high_ref[...] = in_ref[half:]


def halves(array):
    rows, width = array.shape
    out = jax.ShapeDtypeStruct((rows // 2, width), array.dtype)

    def spec(count):
        return pl.BlockSpec((count, width), lambda step: (0, 0))

    return pl.pallas_call(
        halves_kernel,
        out_shape=[out, out],
        grid=(1,),
        in_specs=[spec(rows)],
        out_specs=[spec(rows // 2)] * 2,
        cost_estimate=NO_COST,
    )(array)


def assemble_kernel(place_ref, near_ref, kept_two, kept_three, came_two, came_three, out_ref):
    low, even = place_ref[0] == 1, place_ref[1] == 1
    half = near_ref.shape[1]
    two, three = kept_two[...], kept_three[...]
    kept = (jnp.where(low, two, three), jnp.where(low, three, two))
    two, three = came_two[...], came_three[...]
    came = (jnp.where(low, two, three), jnp.where(low, three, two))
    parts = []
    for mine, other in zip(kept, came):
        parts += [jnp.where(even, mine, other), jnp.where(even, other, mine)]
    far = jnp.concatenate(parts, axis=1)

    @pl.when(low)
    def _():
        out_ref[:, :half] = near_ref[...]
        out_ref[:, half:] = far

    @pl.when(jnp.logical_not(low))
    def _():
        out_ref[:, :half] = far
        out_ref[:, half:] = near_ref[...]


def assemble(low, even, near, kept, came):
    tokens, half = near.shape
    tile = min(128, tokens)

    def spec(width):
        return pl.BlockSpec((tile, width), lambda step, place_ref: (step, 0))

    place = jnp.stack([low.astype(jnp.int32), even.astype(jnp.int32)])
    return pl.pallas_call(
        assemble_kernel,
        out_shape=jax.ShapeDtypeStruct((tokens, 2 * half), BF16),
        grid_spec=pltpu.PrefetchScalarGridSpec(
            num_scalar_prefetch=1,
            grid=(tokens // tile,),
            in_specs=[spec(half)] + [spec(kept[0].shape[1])] * 4,
            out_specs=spec(2 * half),
        ),
        compiler_params=pltpu.CompilerParams(vmem_limit_bytes=16 * 2**20),
        cost_estimate=NO_COST,
    )(place, near, *kept, *came)


def on_device(
    x_inputs,
    z_gates,
    b_proj,
    c_proj,
    dt_raw,
    dt_bias,
    a_log,
    d_skip,
    pool_codes,
    pool_scales,
    page_holder,
    page_index,
    hit_blocks,
    suffix_len,
    w_out,
):
    n_req = lax.axis_size("req")
    own_index = lax.axis_index("req")
    group = lax.axis_index("groups")
    tp_index = lax.axis_index("tp")
    reqs_dev, slots, inner_tp = x_inputs.shape
    tokens = reqs_dev * slots

    latest = []

    def in_turn(value):
        if latest:
            value = after(value, *latest)
        latest[:] = [value]
        return value

    block = w_out[:, 0, :].T
    columns, inner = block.shape
    share = columns // lax.axis_size("groups")
    piece = lax.dynamic_slice_in_dim(block, group * share, share, 0)
    line = n_req // 2
    chain = line == 4
    spot = own_index // 2
    even = own_index % 2 == 0
    low = spot < 2
    inside = (spot == 1) | (spot == 2)
    middle = [(2, 4), (4, 2), (3, 5), (5, 3)]
    outward = [(2, 0), (3, 1), (4, 6), (5, 7)]
    if chain:
        near = swapped(piece, "req", 2)
        second_inner = lax.ppermute(piece, "req", middle)
        beside = swapped(piece, "req", 1)

    need_count = page_index.shape[2] * reqs_dev
    capacity = max(2, 2 * need_count // n_req)
    holders = page_holder[0, :, :, 0].reshape(n_req, need_count)
    indices = page_index[0].reshape(n_req, need_count)
    is_mine = holders == own_index
    send_rank = jnp.cumsum(is_mine.astype(jnp.int32), axis=1) - 1
    chosen = is_mine[:, None, :] & (
        send_rank[:, None, :] == jnp.arange(capacity, dtype=jnp.int32)[None, :, None]
    )
    wanted = jnp.sum(jnp.where(chosen, indices[:, None, :], 0), axis=2).reshape(-1)
    pool = (pool_codes.astype(F32) * pool_scales.astype(F32)[:, :, None]).astype(BF16)
    send_pages = pool[wanted]
    if chain:
        near = in_turn(near)
        second_inner = in_turn(second_inner)
        beside = in_turn(beside)
        near_halves = list(halves(near))
        third_inner = [lax.ppermute(near_halves[0], "req", middle)]
        send_pages = held(send_pages, near, second_inner, beside)
    send_pages = in_turn(send_pages)
    got_pages = lax.all_to_all(send_pages, "req", split_axis=0, concat_axis=0, tiled=True)
    own_holders = lax.dynamic_index_in_dim(holders, own_index, 0, keepdims=False)
    position = jnp.arange(need_count, dtype=jnp.int32)
    earlier = (own_holders[:, None] == own_holders[None, :]) & (
        position[:, None] < position[None, :]
    )
    where_from = own_holders * capacity + jnp.sum(earlier.astype(jnp.int32), axis=0)


    dt_raw = in_turn(dt_raw)
    hit_mask = (hit_blocks > 0).astype(F32)
    token_rows = jnp.arange(slots, dtype=jnp.int32)
    live_mask = (token_rows[None, :] < suffix_len[:, None]).astype(F32)
    step_size = jax.nn.softplus(dt_raw + dt_bias) * live_mask[:, :, None]
    log_decay = -jnp.exp(a_log) * jnp.cumsum(step_size, axis=1)
    start_share = jnp.exp(log_decay) * hit_mask[:, None, None]
    log_total = log_decay[:, slots - 1, :]
    weight = jnp.exp(log_total[:, None, :] - log_decay) * step_size
    kept_share = jnp.exp(log_total) * hit_mask[:, None]
    local, factor = local_part(
        d_skip, x_inputs, z_gates, b_proj, c_proj, log_decay, step_size, start_share, live_mask, [send_pages]
    )

    if chain:
        beside_across = swapped(beside, "groups", 1)
        near_across = swapped(near, "groups", 1)
        near_beside = swapped(near, "req", 1)
        second_outer = lax.ppermute(second_inner, "req", outward)
        local = in_turn(local)
        beside_across = in_turn(beside_across)
        near_across = in_turn(near_across)
        near_beside_across = swapped(near_across, "req", 1)
        near_beside = in_turn(near_beside)
        second_outer = in_turn(second_outer)
        near_beside_across = in_turn(near_beside_across)
        third_inner[0] = in_turn(third_inner[0])
        third_outer = [lax.ppermute(third_inner[0], "req", outward)]
        earlier = [third_inner[0], beside_across, near_beside, near_beside_across, second_outer]
    else:
        earlier = []
    got_pages = in_turn(got_pages)
    gated = in_turn(gate(where_from, got_pages, c_proj, local, factor, earlier))

    first_unit = tp_index * inner_tp
    other_unit = inner_tp - first_unit
    partners = swapped(gated, "tp", 1)
    theirs = swapped(gated, "req", 1)
    if chain:
        third_inner += [lax.ppermute(held(near_halves[1], gated), "req", middle)]
        second = in_turn(pick(inside, second_inner, second_outer, [gated]))
        second_across = swapped(second, "groups", 1)
    partners = in_turn(partners)
    own_rows = [(gated, 0, first_unit), (partners, 0, other_unit)]
    end_state = in_turn(
        state_part(after(where_from, partners), kept_share, got_pages, x_inputs, b_proj, weight)
    )

    if chain:
        spot_bit, parity = spot % 2, own_index % 2
        mine_first, across_first = group * share, (1 - group) * share
        third, third_across = [], []

        def third_part(at):
            part = in_turn(pick(inside, third_inner[at], in_turn(third_outer[at])))
            third.append(part)
            third_across.append(swapped(part, "groups", 1))

        third_inner[1] = in_turn(third_inner[1])
        third_outer += [lax.ppermute(third_inner[1], "req", outward)]
        third_part(0)
        near_blocks = [(block, (spot_bit * 2 + parity) * columns)]
        for bit, odd, mine, across in (
            (spot_bit, 1 - parity, beside, beside_across),
            (1 - spot_bit, parity, near, near_across),
            (1 - spot_bit, 1 - parity, near_beside, near_beside_across),
        ):
            first = (bit * 2 + odd) * columns
            near_blocks += [(mine, first + mine_first), (across, first + across_first)]
        near_out = in_turn(project(own_rows, near_blocks, [third[0]]))
        third_across[0] = in_turn(third_across[0])
        third_part(1)
        second_blocks = [(second, mine_first), (in_turn(second_across), across_first)]
        theirs = in_turn(theirs)
        theirs_other = swapped(theirs, "tp", 1)
        kept = [in_turn(project(own_rows, second_blocks, [third[1], theirs]))]
        theirs_other = in_turn(theirs_other)
        their_rows = [(theirs, 0, first_unit), (theirs_other, 0, other_unit)]
        came = [swapped(in_turn(project(their_rows, second_blocks)), "req", 1)]
        third_across[1] = in_turn(third_across[1])
        third_blocks = []
        for at in range(2):
            half = at * (share // 2)
            third_blocks += [
                (third[at], mine_first + half),
                (third_across[at], across_first + half),
            ]
        came_third = in_turn(project(their_rows, third_blocks))
        came += [swapped(came_third, "req", 1)]
        kept += [project(own_rows, third_blocks, [came_third])]
        mixed_out = assemble(low, even, near_out, kept, came)
    else:
        parities = [list(range(first, n_req, 2)) for first in range(2)]
        mine = lax.all_gather(piece, "req", axis=0, axis_index_groups=parities)
        across = swapped(mine, "groups", 1)
        first_half = jnp.where(group == 0, mine, across)
        second_half = jnp.where(group == 0, across, mine)
        whole = jnp.concatenate([first_half, second_half], axis=1)
        blocks = [(whole.reshape(line * columns, inner), 0)]
        their_rows = [(theirs, 0, first_unit), (swapped(theirs, "tp", 1), 0, other_unit)]
        came = swapped(project(their_rows, blocks), "req", 1).reshape(tokens, line, columns)
        kept = project(own_rows, blocks).reshape(tokens, line, columns)
        both = [jnp.where(even, kept, came), jnp.where(even, came, kept)]
        mixed_out = jnp.stack(both, axis=2)
    mixed_out = mixed_out.reshape(reqs_dev, slots, n_req * columns)
    return (mixed_out, end_state)


def solution(mesh):
    in_specs = (
        P(("groups", "req"), None, "tp"),
        P(("groups", "req"), None, "tp"),
        P(("groups", "req"), None, None),
        P(("groups", "req"), None, None),
        P(("groups", "req"), None, "tp"),
        P("tp"),
        P("tp"),
        P("tp"),
        P(("groups", "req", "tp"), None, None),
        P(("groups", "req", "tp"), None),
        P("tp", "groups", None, None),
        P("tp", "groups", None),
        P(("groups", "req")),
        P(("groups", "req")),
        P(None, "tp", "req"),
    )
    out_specs = (P(("groups", "req"), None, "tp"), P(("groups", "req"), "tp", None))
    return jax.shard_map(
        on_device, mesh=mesh, in_specs=in_specs, out_specs=out_specs, check_vma=False
    )
```

time: 300 us -> 266 us (0.89)
  waiting for transfers between devices: 180 us -> 102 us
  Pallas kernels: 0 us -> 70.7 us
  matrix products: 30.4 us -> 0 us
  starting transfers between devices: 32.8 us -> 41.7 us
  other arithmetic: 17.9 us -> 12.1 us
    ppermute x1, waiting for transfers between devices: 96 us -> 3.28 us  [on_device(): second_inner = lax.ppermute(piece, 'req', middle)]
    pallas_call x0 -> x15, Pallas kernels: none -> 70.7 us  [the longest x5 32.9 us: project(): pl.pallas_call(lambda *refs: project_kernel(row_plan, block_plan, len(ear...]
    ppermute x11 -> x14, waiting for transfers between devices: 51.8 us -> 89.6 us  [swapped(): return lax.ppermute(value, axis, pairs)]
    ppermute x2 -> x4, waiting for transfers between devices: 32.1 us -> 0.01 us  [the longest x1 0.01 us: on_device(): third_inner += [lax.ppermute(held(near_halves[1], gated), 'req', middle)]]
    dot_general x12 -> x0, matrix products: 30.4 us -> none  [the longest x8 14.3 us: rows_times(): lax.dot_general(tokens, block, (((1,), (1,)), ((), ())), preferred_elemen...]
    ppermute x2 -> x4, starting transfers between devices: 4.89 us -> 15.3 us  [the longest x1 5.04 us: on_device(): third_outer = [lax.ppermute(third_inner[0], 'req', outward)]]
    unnamed x29 -> x89, local copies, waits for them, and re-layouts: 14.2 us -> 24.5 us
    ppermute x1, waiting for transfers between devices: 0.01 us -> 9.33 us  [on_device(): second_outer = lax.ppermute(second_inner, 'req', outward)]
  transfers between devices with their start and end apart: 17 -> 21, of which waited for: 9 -> 8; matrix products, arithmetic and copies ran while one was open for 21% -> 8% of each run, Pallas kernels for 0% -> 21%
where the time goes in v2:
time: 266 us; the launch traced here: 264 us
  waiting for transfers between devices  102 us (38%)
  Pallas kernels  70.7 us (27%)
  starting transfers between devices  41.7 us (16%)
  local copies, waits for them, and re-layouts  36.7 us (14%)
  other arithmetic  12.1 us (5%)
    ppermute x14, waiting for transfers between devices, swapped(): return lax.ppermute(value, axis, pairs)  89.6 us
    pallas_call x5, Pallas kernels, project(): pl.pallas_call(lambda *refs: project_kernel(row_plan, block_plan, len(ear...  32.9 us
    unnamed x89, local copies, waits for them, and re-layouts  24.5 us
    ppermute x14, starting transfers between devices, swapped(): return lax.ppermute(value, axis, pairs)  14.4 us
    pallas_call x1, Pallas kernels, gate(): pl.pallas_call(lambda *refs: gate_kernel(pages, *refs), out_shape=jax.Sha...  9.63 us
    ppermute x1, waiting for transfers between devices, on_device(): second_outer = lax.ppermute(second_inner, 'req', outward)  9.33 us
    pallas_call x3, Pallas kernels, pick(): pl.pallas_call(pick_kernel, out_shape=jax.ShapeDtypeStruct(yes.shape, yes...  7.46 us
    pallas_call x1, Pallas kernels, state_part(): pl.pallas_call(lambda *refs: state_kernel(heads, *refs), out_shape=out, g...  7.35 us
  transfers between devices with their start and end apart: 21, of which 8 were waited for; matrix products, arithmetic and copies ran while one was open for 8% of the time, Pallas kernels for 21%

profile of v2, /device:TPU:16, one launch (start us, length us, event | category | flops | bytes accessed | tf_op | source)
XLA Modules:
  0.0 264.5 jit_solution(18193709414073979812)
XLA Ops:
  0.7 2.5 dynamic-slice_bitcast_fusion
  3.2 1.6 collective-permute-start
  4.7 1.9 collective-permute-start.1
  6.7 1.6 collective-permute-start.2
  10.1 2.9 %multiply_convert_fusion = bf16[64,64,256]{2,1,0:T(8,128)(2,1)} fusion(bf16[64,64,256]{2,1,0:T(8,128)(2,1)} %param.23, f32[64,64]{1,0:T(8,128)S(1)} %convert_element_type.42), kind=kLoop, calls=%fused_computation.1 | loop fusion | flops 3145728 | bytes 4210688 | tf_op jit(solution)/shard_map/convert_element_type | solution.py:370
  13.0 4.3 %gather_fusion = bf16[128,64,256]{2,1,0:T(8,128)(2,1)} fusion(bf16[64,64,256]{2,1,0:T(8,128)(2,1)} %multiply_convert_fusion, s32[1024]{0:T(1024)S(1)} %pad_clamp_fusion), kind=kCustom, calls=%fused_computation | custom fusion | bytes 8389120 | tf_op jit(solution)/shard_map/gather | solution.py:371
  17.4 16.5 %collective-permute-done.refs_1_.in_ref.refs_6_ = bf16[160,4096]{1,0:T(8,128)(2,1)S(1)} collective-permute-done((bf16[160,4096]{1,0:T(8,128)(2,1)}, bf16[160,4096]{1,0:T(8,128)(2,1)S(1)}, u32[]{:S(2)}, u32[]{:S(2)}) %collective-permute-start) | collective-permute-done | bytes 1310752 | tf_op jit(solution)/shard_map/ppermute | solution.py:14
  33.9 3.3 %collective-permute-done.1.refs_2_.yes_ref = bf16[160,4096]{1,0:T(8,128)(2,1)} collective-permute-done((bf16[160,4096]{1,0:T(8,128)(2,1)}, bf16[160,4096]{1,0:T(8,128)(2,1)}, u32[]{:S(2)}, u32[]{:S(2)}) %collective-permute-start.1) | collective-permute-done | bytes 1310752 | tf_op jit(solution)/shard_map/ppermute | solution.py:357
  37.2 1.1 copy-done.19
  38.3 5.6 %all-to-all-start = ((bf16[128,64,256]{2,1,0:T(8,128)(2,1)}), bf16[128,64,256]{2,1,0:T(8,128)(2,1)}, u32[]{:S(2)}, u32[]{:S(2)}) async-start(bf16[128,64,256]{2,1,0:T(8,128)(2,1)} %shard_map.158.refs_10_), calls=%async_computation | async-start | bytes 8388608 | tf_op jit(solution)/shard_map/all_to_all | solution.py:380
  44.0 1.5 collective-permute-start.5
  46.8 4.5 %collective-permute-start.7 = (bf16[160,4096]{1,0:T(8,128)(2,1)}, bf16[160,4096]{1,0:T(8,128)(2,1)}, u32[]{:S(2)}, u32[]{:S(2)}) collective-permute-start(bf16[160,4096]{1,0:T(8,128)(2,1)} %collective-permute-done.1.refs_2_.yes_ref), channel_id=1, source_target_pairs={{4,0},{6,2},{8,12},{10,14},{5,1},{7,3},{9,13},{11,15},{20,16},{22,... | collective-permute-start | bytes 3932168 | tf_op jit(solution)/shard_map/ppermute | solution.py:407
  52.2 1.8 fusion
  54.0 1.0 copy.36
  55.0 1.1 reduce-window.6
  57.3 1.8 exponential_multiply_fusion.1
  59.1 1.0 copy.38.refs_6_
  60.1 1.8 fusion.6
  61.9 1.0 copy.39.refs_7_
  64.0 1.6 copy-done.25
  65.6 0.9 copy-done.28
  66.5 0.9 copy-done.30
  67.5 0.9 copy-done.32
  68.4 0.9 copy-done.33
  69.4 6.5 %shard_map.160 = (f32[2,256,2048]{2,1,0:T(8,128)}, f32[2,256,2048]{2,1,0:T(8,128)}) custom-call(f32[16]{0:T(128)S(1)} %copy-done.34, bf16[2,256,2048]{2,1,0:T(8,128)(2,1)S(1)} %copy-done.15, bf16[2,256,2048]{2,1,0:T(8,128)(2,1)S(1)} %copy-done.25, bf16[2,256,256]{2,1,0:T(8,128)(2,1)S(1)} %copy-done.30, bf16[2,256,256]{2,1,0:T(8,128)(2,1)S(1)} %copy-done.28, ...), custom_call_target="tpu_custom_call" | custom-call | tf_op jit(solution)/shard_map/pallas_call | solution.py:80
  75.9 1.5 collective-permute-start.8
  77.3 23.7 %collective-permute-done.4.refs_7_ = bf16[160,4096]{1,0:T(8,128)(2,1)} collective-permute-done((bf16[160,4096]{1,0:T(8,128)(2,1)S(1)}, bf16[160,4096]{1,0:T(8,128)(2,1)}, u32[]{:S(2)}, u32[]{:S(2)}) %collective-permute-start.4) | collective-permute-done | bytes 1310752 | tf_op jit(solution)/shard_map/ppermute | solution.py:14
  101.0 1.5 collective-permute-start.6
  102.5 2.4 shard_map.159
  104.9 3.3 %collective-permute-start.3 = (bf16[80,4096]{1,0:T(8,128)(2,1)}, bf16[80,4096]{1,0:T(8,128)(2,1)}, u32[]{:S(2)}, u32[]{:S(2)}) collective-permute-start(bf16[80,4096]{1,0:T(8,128)(2,1)} %get-tuple-element.40), channel_id=1, source_target_pairs={{4,8},{8,4},{6,10},{10,6},{5,9},{9,5},{7,11},{11,7},{20,24},{24,20... | collective-permute-start | bytes 1966088 | tf_op jit(solution)/shard_map/ppermute | solution.py:377
  108.4 20.1 %collective-permute-done.8.refs_7_.refs_8_ = bf16[160,4096]{1,0:T(8,128)(2,1)S(1)} collective-permute-done((bf16[160,4096]{1,0:T(8,128)(2,1)S(1)}, bf16[160,4096]{1,0:T(8,128)(2,1)S(1)}, u32[]{:S(2)}, u32[]{:S(2)}) %collective-permute-start.8) | collective-permute-done | bytes 1310752 | tf_op jit(solution)/shard_map/ppermute | solution.py:14
  128.5 9.3 %collective-permute-done.7.refs_9_.no_ref = bf16[160,4096]{1,0:T(8,128)(2,1)} collective-permute-done((bf16[160,4096]{1,0:T(8,128)(2,1)}, bf16[160,4096]{1,0:T(8,128)(2,1)}, u32[]{:S(2)}, u32[]{:S(2)}) %collective-permute-start.7) | collective-permute-done | bytes 1310752 | tf_op jit(solution)/shard_map/ppermute | solution.py:407
  137.8 16.5 %collective-permute-done.6.refs_8_.refs_9_ = bf16[160,4096]{1,0:T(8,128)(2,1)} collective-permute-done((bf16[160,4096]{1,0:T(8,128)(2,1)}, bf16[160,4096]{1,0:T(8,128)(2,1)}, u32[]{:S(2)}, u32[]{:S(2)}) %collective-permute-start.6) | collective-permute-done | bytes 1310752 | tf_op jit(solution)/shard_map/ppermute | solution.py:14
  154.3 0.9 copy-done.29
  155.2 9.6 %shard_map.161.refs_0_.refs_1_ = bf16[512,2048]{1,0:T(8,128)(2,1)} custom-call(s32[64]{0:T(128)S(1)} %multiply_add_fusion.refs_0_, bf16[128,64,256]{2,1,0:T(8,128)(2,1)} %all-to-all-done.refs_1_.refs_2_, bf16[2,256,256]{2,1,0:T(8,128)(2,1)S(1)} %copy-done.29, f32[2,256,2048]{2,1,0:T(8,128)} %get-tuple-element.43.refs_3_, ...), custom_call_target="tpu_custom_call" | custom-call | tf_op jit(solution)/shard_map/pallas_call | solution.py:148
  164.9 1.1 copy-done.17
  166.0 1.9 collective-permute-start.11
  167.9 5.0 %collective-permute-start.10 = (bf16[80,4096]{1,0:T(8,128)(2,1)}, bf16[80,4096]{1,0:T(8,128)(2,1)}, u32[]{:S(2)}, u32[]{:S(2)}) collective-permute-start(bf16[80,4096]{1,0:T(8,128)(2,1)} %collective-permute-done.3.refs_5_.yes_ref), channel_id=1, source_target_pairs={{4,0},{6,2},{8,12},{10,14},{5,1},{7,3},{9,13},{11,15},{20,16},{22,... | collective-permute-start | bytes 1966088 | tf_op jit(solution)/shard_map/ppermute | solution.py:416
  173.0 3.0 %shard_map.162.refs_3_ = bf16[160,4096]{1,0:T(8,128)(2,1)} custom-call(s32[1]{0:T(128)} %bitcast.20.flag_ref, bf16[160,4096]{1,0:T(8,128)(2,1)} %collective-permute-done.1.refs_2_.yes_ref, bf16[160,4096]{1,0:T(8,128)(2,1)} %collective-permute-done.7.refs_9_.no_ref, bf16[512,2048]{1,0:T(8,128)(2,1)} %shard_map.161.refs_0_.refs_1_), custom_call_target="tpu_custom_call" | custom-call | tf_op jit(solution)/shard_map/pallas_call | solution.py:233
  175.9 1.5 collective-permute-start.12
  177.7 1.4 copy-done.1
  179.1 1.6 copy-done.16
  180.7 7.3 %shard_map.164 = bf16[2,2048,256]{2,1,0:T(8,128)(2,1)} custom-call(s32[64]{0:T(128)S(1)} %multiply_add_fusion.refs_0_, f32[2,16]{1,0:T(2,128)S(1)} %exponential_multiply_fusion.2.refs_1_, bf16[128,64,256]{2,1,0:T(8,128)(2,1)} %all-to-all-done.refs_1_.refs_2_, bf16[2,256,2048]{2,1,0:T(8,128)(2,1)S(1)} %copy-done.16, bf16[2,256,256]{2,1,0:T(8,128)(2,1)S(1)} %copy-done.31, ...), custom_call_target="tpu_custom_call" | custom-call | tf_op jit(solution)/shard_map/pallas_call | solution.py:116
  188.1 2.3 shard_map.165.refs_10_.refs_3_
  190.9 5.0 %collective-permute-start.13 = (bf16[80,4096]{1,0:T(8,128)(2,1)}, bf16[80,4096]{1,0:T(8,128)(2,1)}, u32[]{:S(2)}, u32[]{:S(2)}) collective-permute-start(bf16[80,4096]{1,0:T(8,128)(2,1)} %collective-permute-done.11.yes_ref), channel_id=1, source_target_pairs={{4,0},{6,2},{8,12},{10,14},{5,1},{7,3},{9,13},{11,15},{20,16},{22,... | collective-permute-start | bytes 1966088 | tf_op jit(solution)/shard_map/ppermute | solution.py:448
  196.1 1.6 copy-done.2
  197.6 1.1 copy-done.9
  198.7 1.3 copy-done.18
  200.0 1.3 copy-done.20
  201.4 9.9 %shard_map.166.near_ref = bf16[512,1280]{1,0:T(8,128)(2,1)S(1)} custom-call(s32[9]{0:T(128)S(1)} %stack.92.refs_0_, bf16[512,2048]{1,0:T(8,128)(2,1)S(1)} %copy-done, bf16[512,2048]{1,0:T(8,128)(2,1)S(1)} %copy-done.2, bf16[320,4096]{1,0:T(8,128)(2,1)} %bitcast.44, bf16[160,4096]{1,0:T(8,128)(2,1)S(1)} %copy-done.20, ...), custom_call_target="tpu_custom_call" | custom-call | tf_op jit(solution)/shard_map/pallas_call | solution.py:207
  211.3 1.1 copy-done.21
  212.4 8.8 %collective-permute-done.14.refs_4_ = bf16[80,4096]{1,0:T(8,128)(2,1)} collective-permute-done((bf16[80,4096]{1,0:T(8,128)(2,1)}, bf16[80,4096]{1,0:T(8,128)(2,1)}, u32[]{:S(2)}, u32[]{:S(2)}) %collective-permute-start.14) | collective-permute-done | bytes 655392 | tf_op jit(solution)/shard_map/ppermute | solution.py:14
  221.2 2.2 shard_map.167.refs_5_
  223.4 1.6 collective-permute-start.16
  225.1 1.6 copy-done.3
  226.7 1.1 copy-done.12
  227.8 5.1 %shard_map.168.kept_two = bf16[512,320]{1,0:T(8,128)(2,1)S(1)} custom-call(s32[4]{0:T(128)S(1)} %pad_add_fusion.refs_0_, bf16[512,2048]{1,0:T(8,128)(2,1)S(1)} %copy-done, bf16[512,2048]{1,0:T(8,128)(2,1)S(1)} %copy-done.3, bf16[160,4096]{1,0:T(8,128)(2,1)S(1)} %copy-done.8, bf16[160,4096]{1,0:T(8,128)(2,1)} %collective-permute-done.12.refs_4_, ...), custom_call_target="tpu_custom_call" | custom-call | tf_op jit(solution)/shard_map/pallas_call | solution.py:207
  233.7 6.3 %shard_map.169 = bf16[512,320]{1,0:T(8,128)(2,1)} custom-call(s32[4]{0:T(128)S(1)} %pad_add_fusion.refs_0_, bf16[512,2048]{1,0:T(8,128)(2,1)} %collective-permute-done.15.refs_6_.refs_1_, bf16[512,2048]{1,0:T(8,128)(2,1)} %collective-permute-done.17.refs_2_, bf16[160,4096]{1,0:T(8,128)(2,1)S(1)} %copy-done.8, bf16[160,4096]{1,0:T(8,128)(2,1)} %collective-permute-done.12.refs_4_), custom_call_target="tpu_custom_call" | custom-call | tf_op jit(solution)/shard_map/pallas_call | solution.py:207
  240.0 1.8 collective-permute-start.18
  241.8 6.3 %shard_map.170.refs_7_ = bf16[512,320]{1,0:T(8,128)(2,1)} custom-call(s32[6]{0:T(128)S(1)} %stack.98.refs_0_, bf16[512,2048]{1,0:T(8,128)(2,1)} %collective-permute-done.15.refs_6_.refs_1_, bf16[512,2048]{1,0:T(8,128)(2,1)} %collective-permute-done.17.refs_2_, bf16[80,4096]{1,0:T(8,128)(2,1)S(1)} %copy-done.10, ...), custom_call_target="tpu_custom_call" | custom-call | tf_op jit(solution)/shard_map/pallas_call | solution.py:207
  249.1 1.6 copy-done.4
  250.7 5.3 %shard_map.171.kept_three = bf16[512,320]{1,0:T(8,128)(2,1)S(1)} custom-call(s32[6]{0:T(128)S(1)} %stack.98.refs_0_, bf16[512,2048]{1,0:T(8,128)(2,1)S(1)} %copy-done, bf16[512,2048]{1,0:T(8,128)(2,1)S(1)} %copy-done.4, bf16[80,4096]{1,0:T(8,128)(2,1)S(1)} %copy-done.11, bf16[80,4096]{1,0:T(8,128)(2,1)} %collective-permute-done.14.refs_4_, ...), custom_call_target="tpu_custom_call" | custom-call | tf_op jit(solution)/shard_map/pallas_call | solution.py:207
  256.0 4.0 %collective-permute-done.19.came_three = bf16[512,320]{1,0:T(8,128)(2,1)} collective-permute-done((bf16[512,320]{1,0:T(8,128)(2,1)}, bf16[512,320]{1,0:T(8,128)(2,1)}, u32[]{:S(2)}, u32[]{:S(2)}) %collective-permute-start.19) | collective-permute-done | bytes 327712 | tf_op jit(solution)/shard_map/ppermute | solution.py:14
  260.0 4.5 %shard_map.172 = bf16[512,2560]{1,0:T(8,128)(2,1)} custom-call(s32[2]{0:T(128)S(1)} %add_convert_fusion.place_ref, bf16[512,1280]{1,0:T(8,128)(2,1)S(1)} %copy-done.22, bf16[512,320]{1,0:T(8,128)(2,1)S(1)} %copy-done.27, bf16[512,320]{1,0:T(8,128)(2,1)S(1)} %shard_map.171.kept_three, bf16[512,320]{1,0:T(8,128)(2,1)} %collective-permute-done.18.came_two, ...), custom_call_target="tpu_custom_call" | custom-call | tf_op jit(solution)/shard_map/pallas_call | solution.py:297
  (123 shorter events, 9.2 us)
Async XLA Ops:
  0.6 8.1 %copy-start.39 = (s32[1,16,32,1]{2,3,1,0:T(1,128)S(1)}, s32[1,16,32,1]{2,3,1,0:T(1,128)}, u32[]{:S(2)}) copy-start(s32[1,16,32,1]{2,3,1,0:T(1,128)} %param.25) | copy-start | bytes 6148
  0.6 8.9 %copy-start.37 = (bf16[64,64]{1,0:T(8,128)(2,1)S(1)}, bf16[64,64]{1,0:T(8,128)(2,1)}, u32[]{:S(2)}) copy-start(bf16[64,64]{1,0:T(8,128)(2,1)} %param.24) | copy-start | bytes 24580
  0.7 8.9 %copy-start.38 = (s32[1,16,32]{2,1,0:T(8,128)S(1)}, s32[1,16,32]{2,1,0:T(8,128)}, u32[]{:S(2)}) copy-start(s32[1,16,32]{2,1,0:T(8,128)} %param.26) | copy-start | bytes 6148
  3.2 30.7 %collective-permute-start = (bf16[160,4096]{1,0:T(8,128)(2,1)}, bf16[160,4096]{1,0:T(8,128)(2,1)S(1)}, u32[]{:S(2)}, u32[]{:S(2)}) collective-permute-start(bf16[160,4096]{1,0:T(8,128)(2,1)} %dynamic-slice_bitcast_fusion), channel_id=1, source_target_pairs={{0,4},{2,6},{4,0},{6,2},{8,12},{10,14},{12,8},{14,10},{1,5},{3,7},... | collective-permute-start | bytes 3932168 | tf_op jit(solution)/shard_map/ppermute | solution.py:14
  4.7 32.4 %collective-permute-start.1 = (bf16[160,4096]{1,0:T(8,128)(2,1)}, bf16[160,4096]{1,0:T(8,128)(2,1)}, u32[]{:S(2)}, u32[]{:S(2)}) collective-permute-start(bf16[160,4096]{1,0:T(8,128)(2,1)} %dynamic-slice_bitcast_fusion), channel_id=1, source_target_pairs={{4,8},{8,4},{6,10},{10,6},{5,9},{9,5},{7,11},{11,7},{20,24},{24,20... | collective-permute-start | bytes 3932168 | tf_op jit(solution)/shard_map/ppermute | solution.py:357
  6.7 30.5 %collective-permute-start.2 = (bf16[160,4096]{1,0:T(8,128)(2,1)}, bf16[160,4096]{1,0:T(8,128)(2,1)S(1)}, u32[]{:S(2)}, u32[]{:S(2)}) collective-permute-start(bf16[160,4096]{1,0:T(8,128)(2,1)} %dynamic-slice_bitcast_fusion), channel_id=1, source_target_pairs={{0,2},{2,0},{4,6},{6,4},{8,10},{10,8},{12,14},{14,12},{1,3},{3,1},... | collective-permute-start | bytes 3932168 | tf_op jit(solution)/shard_map/ppermute | solution.py:14
  33.9 3.3 %copy-start.5 = (bf16[160,4096]{1,0:T(8,128)(2,1)}, bf16[160,4096]{1,0:T(8,128)(2,1)S(1)}, u32[]{:S(2)}) copy-start(bf16[160,4096]{1,0:T(8,128)(2,1)S(1)} %collective-permute-done.refs_1_.in_ref.refs_6_) | copy-start | bytes 3932164
  37.2 1.1 copy-start.19
  38.3 5.6 %copy-start.42 = (s32[2]{0:T(128)S(1)}, s32[2]{0:T(128)}, u32[]{:S(2)}) copy-start(s32[2]{0:T(128)} %param.27) | copy-start | bytes 28
  38.3 5.6 %copy-start.41 = (s32[2]{0:T(128)S(1)}, s32[2]{0:T(128)}, u32[]{:S(2)}) copy-start(s32[2]{0:T(128)} %param.28) | copy-start | bytes 28
  38.3 7.2 %copy-start.6 = (bf16[160,4096]{1,0:T(8,128)(2,1)S(1)}, bf16[160,4096]{1,0:T(8,128)(2,1)}, u32[]{:S(2)}) copy-start(bf16[160,4096]{1,0:T(8,128)(2,1)} %copy-done.5) | copy-start | bytes 3932164
  38.3 7.7 %copy-start.43 = (f32[16]{0:T(128)S(1)}, f32[16]{0:T(128)}, u32[]{:S(2)}) copy-start(f32[16]{0:T(128)} %param.21) | copy-start | bytes 196
  38.3 13.0 %copy-start.36 = (f32[2,256,16]{1,2,0:T(8,128)S(1)}, f32[2,256,16]{1,2,0:T(8,128)}, u32[]{:S(2)}) copy-start(f32[2,256,16]{1,2,0:T(8,128)} %param.19) | copy-start | bytes 98308
  38.3 13.9 %copy-start.40 = (f32[16]{0:T(128)S(1)}, f32[16]{0:T(128)}, u32[]{:S(2)}) copy-start(f32[16]{0:T(128)} %param.20) | copy-start | bytes 196
  38.3 116.0 %all-to-all-start = ((bf16[128,64,256]{2,1,0:T(8,128)(2,1)}), bf16[128,64,256]{2,1,0:T(8,128)(2,1)}, u32[]{:S(2)}, u32[]{:S(2)}) async-start(bf16[128,64,256]{2,1,0:T(8,128)(2,1)} %shard_map.158.refs_10_), calls=%async_computation | async-start | bytes 8388608 | tf_op jit(solution)/shard_map/all_to_all | solution.py:380
  43.9 19.1 %copy-start.15 = (bf16[2,256,2048]{2,1,0:T(8,128)(2,1)S(1)}, bf16[2,256,2048]{2,1,0:T(8,128)(2,1)}, u32[]{:S(2)}) copy-start(bf16[2,256,2048]{2,1,0:T(8,128)(2,1)} %refs_3_.3) | copy-start | bytes 6291460
  43.9 19.1 %copy-start.34 = (f32[16]{0:T(128)S(1)}, f32[16]{0:T(128)}, u32[]{:S(2)}) copy-start(f32[16]{0:T(128)} %refs_0_.1) | copy-start | bytes 196
  44.0 33.3 %collective-permute-start.5 = (bf16[160,4096]{1,0:T(8,128)(2,1)}, bf16[160,4096]{1,0:T(8,128)(2,1)}, u32[]{:S(2)}, u32[]{:S(2)}) collective-permute-start(bf16[160,4096]{1,0:T(8,128)(2,1)} %copy-done.19), channel_id=1, source_target_pairs={{0,16},{16,0},{1,17},{17,1},{2,18},{18,2},{3,19},{19,3},{4,20},{20... | collective-permute-start | bytes 3932168 | tf_op jit(solution)/shard_map/ppermute | solution.py:14
  45.5 55.5 %collective-permute-start.4 = (bf16[160,4096]{1,0:T(8,128)(2,1)S(1)}, bf16[160,4096]{1,0:T(8,128)(2,1)}, u32[]{:S(2)}, u32[]{:S(2)}) collective-permute-start(bf16[160,4096]{1,0:T(8,128)(2,1)S(1)} %copy-done.6), channel_id=1, source_target_pairs={{0,16},{16,0},{1,17},{17,1},{2,18},{18,2},{3,19},{19,3},{4,20},{20... | collective-permute-start | bytes 3932168 | tf_op jit(solution)/shard_map/ppermute | solution.py:14
  46.8 90.9 %collective-permute-start.7 = (bf16[160,4096]{1,0:T(8,128)(2,1)}, bf16[160,4096]{1,0:T(8,128)(2,1)}, u32[]{:S(2)}, u32[]{:S(2)}) collective-permute-start(bf16[160,4096]{1,0:T(8,128)(2,1)} %collective-permute-done.1.refs_2_.yes_ref), channel_id=1, source_target_pairs={{4,0},{6,2},{8,12},{10,14},{5,1},{7,3},{9,13},{11,15},{20,16},{22,... | collective-permute-start | bytes 3932168 | tf_op jit(solution)/shard_map/ppermute | solution.py:407
  63.0 1.0 copy-start.23
  64.0 1.6 copy-start.25
  65.6 0.9 copy-start.28
  66.5 0.9 copy-start.30
  67.5 0.9 copy-start.32
  68.4 0.9 copy-start.33
  75.9 52.6 %collective-permute-start.8 = (bf16[160,4096]{1,0:T(8,128)(2,1)S(1)}, bf16[160,4096]{1,0:T(8,128)(2,1)S(1)}, u32[]{:S(2)}, u32[]{:S(2)}) collective-permute-start(bf16[160,4096]{1,0:T(8,128)(2,1)S(1)} %copy-done.6), channel_id=1, source_target_pairs={{0,2},{2,0},{4,6},{6,4},{8,10},{10,8},{12,14},{14,12},{1,3},{3,1},... | collective-permute-start | bytes 3932168 | tf_op jit(solution)/shard_map/ppermute | solution.py:14
  101.0 53.3 %collective-permute-start.6 = (bf16[160,4096]{1,0:T(8,128)(2,1)}, bf16[160,4096]{1,0:T(8,128)(2,1)}, u32[]{:S(2)}, u32[]{:S(2)}) collective-permute-start(bf16[160,4096]{1,0:T(8,128)(2,1)} %collective-permute-done.4.refs_7_), channel_id=1, source_target_pairs={{0,2},{2,0},{4,6},{6,4},{8,10},{10,8},{12,14},{14,12},{1,3},{3,1},... | collective-permute-start | bytes 3932168 | tf_op jit(solution)/shard_map/ppermute | solution.py:14
  104.9 49.4 %collective-permute-start.3 = (bf16[80,4096]{1,0:T(8,128)(2,1)}, bf16[80,4096]{1,0:T(8,128)(2,1)}, u32[]{:S(2)}, u32[]{:S(2)}) collective-permute-start(bf16[80,4096]{1,0:T(8,128)(2,1)} %get-tuple-element.40), channel_id=1, source_target_pairs={{4,8},{8,4},{6,10},{10,6},{5,9},{9,5},{7,11},{11,7},{20,24},{24,20... | collective-permute-start | bytes 1966088 | tf_op jit(solution)/shard_map/ppermute | solution.py:377
  154.3 1.0 copy-start.29
  164.9 1.1 copy-start.17
  166.0 11.7 %collective-permute-start.9 = (bf16[512,2048]{1,0:T(8,128)(2,1)}, bf16[512,2048]{1,0:T(8,128)(2,1)S(1)}, u32[]{:S(2)}, u32[]{:S(2)}) collective-permute-start(bf16[512,2048]{1,0:T(8,128)(2,1)} %shard_map.161.refs_0_.refs_1_), channel_id=1, source_target_pairs={{0,1},{1,0},{2,3},{3,2},{4,5},{5,4},{6,7},{7,6},{8,9},{9,8},{10,11... | collective-permute-start | bytes 6291464 | tf_op jit(solution)/shard_map/ppermute | solution.py:14
  166.0 57.4 %collective-permute-start.15 = (bf16[512,2048]{1,0:T(8,128)(2,1)}, bf16[512,2048]{1,0:T(8,128)(2,1)}, u32[]{:S(2)}, u32[]{:S(2)}) collective-permute-start(bf16[512,2048]{1,0:T(8,128)(2,1)} %shard_map.161.refs_0_.refs_1_), channel_id=1, source_target_pairs={{0,2},{2,0},{4,6},{6,4},{8,10},{10,8},{12,14},{14,12},{1,3},{3,1},... | collective-permute-start | bytes 6291464 | tf_op jit(solution)/shard_map/ppermute | solution.py:14
  166.0 22.1 %collective-permute-start.11 = (bf16[80,4096]{1,0:T(8,128)(2,1)}, bf16[80,4096]{1,0:T(8,128)(2,1)}, u32[]{:S(2)}, u32[]{:S(2)}) collective-permute-start(bf16[80,4096]{1,0:T(8,128)(2,1)} %shard_map.163), channel_id=1, source_target_pairs={{4,8},{8,4},{6,10},{10,6},{5,9},{9,5},{7,11},{11,7},{20,24},{24,20... | collective-permute-start | bytes 1966088 | tf_op jit(solution)/shard_map/ppermute | solution.py:428
  167.9 20.1 %collective-permute-start.10 = (bf16[80,4096]{1,0:T(8,128)(2,1)}, bf16[80,4096]{1,0:T(8,128)(2,1)}, u32[]{:S(2)}, u32[]{:S(2)}) collective-permute-start(bf16[80,4096]{1,0:T(8,128)(2,1)} %collective-permute-done.3.refs_5_.yes_ref), channel_id=1, source_target_pairs={{4,0},{6,2},{8,12},{10,14},{5,1},{7,3},{9,13},{11,15},{20,16},{22,... | collective-permute-start | bytes 1966088 | tf_op jit(solution)/shard_map/ppermute | solution.py:416
  173.0 4.5 %copy-start.24 = (f32[2,16,256]{1,2,0:T(8,128)S(1)}, f32[2,16,256]{1,2,0:T(8,128)}, u32[]{:S(2)}) copy-start(f32[2,16,256]{1,2,0:T(8,128)} %get-tuple-element.73) | copy-start | bytes 98308
  173.0 4.5 %copy-start.35 = (f32[2,256,16]{2,1,0:T(8,128)S(1)}, f32[2,256,16]{2,1,0:T(8,128)}, u32[]{:S(2)}) copy-start(f32[2,256,16]{2,1,0:T(8,128)} %copy.34) | copy-start | bytes 98308
  173.0 6.1 %copy-start.31 = (bf16[2,256,256]{2,1,0:T(8,128)(2,1)S(1)}, bf16[2,256,256]{2,1,0:T(8,128)(2,1)}, u32[]{:S(2)}) copy-start(bf16[2,256,256]{2,1,0:T(8,128)(2,1)} %refs_4_.3) | copy-start | bytes 786436
  175.9 47.5 %collective-permute-start.12 = (bf16[160,4096]{1,0:T(8,128)(2,1)}, bf16[160,4096]{1,0:T(8,128)(2,1)}, u32[]{:S(2)}, u32[]{:S(2)}) collective-permute-start(bf16[160,4096]{1,0:T(8,128)(2,1)} %shard_map.162.refs_3_), channel_id=1, source_target_pairs={{0,16},{16,0},{1,17},{17,1},{2,18},{18,2},{3,19},{19,3},{4,20},{20... | collective-permute-start | bytes 3932168 | tf_op jit(solution)/shard_map/ppermute | solution.py:14
  177.7 1.4 copy-start.1
  179.1 1.6 copy-start.16
  180.7 15.3 %copy-start = (bf16[512,2048]{1,0:T(8,128)(2,1)S(1)}, bf16[512,2048]{1,0:T(8,128)(2,1)}, u32[]{:S(2)}) copy-start(bf16[512,2048]{1,0:T(8,128)(2,1)} %shard_map.161.refs_0_.refs_1_) | copy-start | bytes 6291460
  188.1 8.0 %copy-start.7 = (bf16[160,4096]{1,0:T(8,128)(2,1)S(1)}, bf16[160,4096]{1,0:T(8,128)(2,1)}, u32[]{:S(2)}) copy-start(bf16[160,4096]{1,0:T(8,128)(2,1)} %copy-done.5) | copy-start | bytes 3932164
  190.4 30.8 %collective-permute-start.14 = (bf16[80,4096]{1,0:T(8,128)(2,1)}, bf16[80,4096]{1,0:T(8,128)(2,1)}, u32[]{:S(2)}, u32[]{:S(2)}) collective-permute-start(bf16[80,4096]{1,0:T(8,128)(2,1)} %shard_map.165.refs_10_.refs_3_), channel_id=1, source_target_pairs={{0,16},{16,0},{1,17},{17,1},{2,18},{18,2},{3,19},{19,3},{4,20},{20... | collective-permute-start | bytes 1966088 | tf_op jit(solution)/shard_map/ppermute | solution.py:14
  190.9 30.3 %collective-permute-start.13 = (bf16[80,4096]{1,0:T(8,128)(2,1)}, bf16[80,4096]{1,0:T(8,128)(2,1)}, u32[]{:S(2)}, u32[]{:S(2)}) collective-permute-start(bf16[80,4096]{1,0:T(8,128)(2,1)} %collective-permute-done.11.yes_ref), channel_id=1, source_target_pairs={{4,0},{6,2},{8,12},{10,14},{5,1},{7,3},{9,13},{11,15},{20,16},{22,... | collective-permute-start | bytes 1966088 | tf_op jit(solution)/shard_map/ppermute | solution.py:448
  196.0 1.6 copy-start.2
  197.6 1.1 copy-start.9
  198.7 1.3 copy-start.18
  200.0 1.3 copy-start.20
  211.3 1.1 copy-start.21
  212.4 12.7 %copy-start.8 = (bf16[160,4096]{1,0:T(8,128)(2,1)S(1)}, bf16[160,4096]{1,0:T(8,128)(2,1)}, u32[]{:S(2)}) copy-start(bf16[160,4096]{1,0:T(8,128)(2,1)} %shard_map.162.refs_3_) | copy-start | bytes 3932164
  223.4 10.3 %collective-permute-start.17 = (bf16[512,2048]{1,0:T(8,128)(2,1)}, bf16[512,2048]{1,0:T(8,128)(2,1)}, u32[]{:S(2)}, u32[]{:S(2)}) collective-permute-start(bf16[512,2048]{1,0:T(8,128)(2,1)} %collective-permute-done.15.refs_6_.refs_1_), channel_id=1, source_target_pairs={{0,1},{1,0},{2,3},{3,2},{4,5},{5,4},{6,7},{7,6},{8,9},{9,8},{10,11... | collective-permute-start | bytes 6291464 | tf_op jit(solution)/shard_map/ppermute | solution.py:14
  223.4 18.4 %collective-permute-start.16 = (bf16[80,4096]{1,0:T(8,128)(2,1)}, bf16[80,4096]{1,0:T(8,128)(2,1)}, u32[]{:S(2)}, u32[]{:S(2)}) collective-permute-start(bf16[80,4096]{1,0:T(8,128)(2,1)} %shard_map.167.refs_5_), channel_id=1, source_target_pairs={{0,16},{16,0},{1,17},{17,1},{2,18},{18,2},{3,19},{19,3},{4,20},{20... | collective-permute-start | bytes 1966088 | tf_op jit(solution)/shard_map/ppermute | solution.py:14
  225.1 1.6 copy-start.3
  226.7 1.1 copy-start.12
  233.7 8.1 %copy-start.10 = (bf16[80,4096]{1,0:T(8,128)(2,1)S(1)}, bf16[80,4096]{1,0:T(8,128)(2,1)}, u32[]{:S(2)}) copy-start(bf16[80,4096]{1,0:T(8,128)(2,1)} %shard_map.165.refs_10_.refs_3_) | copy-start | bytes 1966084
  233.7 8.1 %copy-start.13 = (bf16[80,4096]{1,0:T(8,128)(2,1)S(1)}, bf16[80,4096]{1,0:T(8,128)(2,1)}, u32[]{:S(2)}) copy-start(bf16[80,4096]{1,0:T(8,128)(2,1)} %shard_map.167.refs_5_) | copy-start | bytes 1966084
  239.9 9.1 %copy-start.11 = (bf16[80,4096]{1,0:T(8,128)(2,1)S(1)}, bf16[80,4096]{1,0:T(8,128)(2,1)}, u32[]{:S(2)}) copy-start(bf16[80,4096]{1,0:T(8,128)(2,1)} %shard_map.165.refs_10_.refs_3_) | copy-start | bytes 1966084
  239.9 9.1 %copy-start.14 = (bf16[80,4096]{1,0:T(8,128)(2,1)S(1)}, bf16[80,4096]{1,0:T(8,128)(2,1)}, u32[]{:S(2)}) copy-start(bf16[80,4096]{1,0:T(8,128)(2,1)} %shard_map.167.refs_5_) | copy-start | bytes 1966084
  240.0 16.0 %collective-permute-start.18 = (bf16[512,320]{1,0:T(8,128)(2,1)}, bf16[512,320]{1,0:T(8,128)(2,1)}, u32[]{:S(2)}, u32[]{:S(2)}) collective-permute-start(bf16[512,320]{1,0:T(8,128)(2,1)} %shard_map.169), channel_id=1, source_target_pairs={{0,2},{2,0},{4,6},{6,4},{8,10},{10,8},{12,14},{14,12},{1,3},{3,1},... | collective-permute-start | bytes 983048 | tf_op jit(solution)/shard_map/ppermute | solution.py:14
  248.1 11.8 %collective-permute-start.19 = (bf16[512,320]{1,0:T(8,128)(2,1)}, bf16[512,320]{1,0:T(8,128)(2,1)}, u32[]{:S(2)}, u32[]{:S(2)}) collective-permute-start(bf16[512,320]{1,0:T(8,128)(2,1)} %shard_map.170.refs_7_), channel_id=1, source_target_pairs={{0,2},{2,0},{4,6},{6,4},{8,10},{10,8},{12,14},{14,12},{1,3},{3,1},... | collective-permute-start | bytes 983048 | tf_op jit(solution)/shard_map/ppermute | solution.py:14
  249.1 1.6 copy-start.4
  250.7 9.3 %copy-start.22 = (bf16[512,1280]{1,0:T(8,128)(2,1)S(1)}, bf16[512,1280]{1,0:T(8,128)(2,1)}, u32[]{:S(2)}) copy-start(bf16[512,1280]{1,0:T(8,128)(2,1)} %copy-done.21) | copy-start | bytes 3932164
  250.7 9.3 %copy-start.27 = (bf16[512,320]{1,0:T(8,128)(2,1)S(1)}, bf16[512,320]{1,0:T(8,128)(2,1)}, u32[]{:S(2)}) copy-start(bf16[512,320]{1,0:T(8,128)(2,1)} %copy-done.26) | copy-start | bytes 983044
  (1 other events, 0.7 us)

commit v3 on v2

--- a/solution.py
+++ b/solution.py
@@ -90,7 +90,8 @@
     )(d_skip, *operands, *earlier)
 
 
-def state_kernel(heads, where_ref, kept_ref, pages_ref, x_ref, b_ref, weight_ref, out_ref):
+def state_kernel(heads, where_ref, kept_ref, pages_ref, x_ref, b_ref, weight_ref, *refs):
+    out_ref = refs[-1]
     request = pl.program_id(0)
     width = x_ref.shape[2] // heads
     pages = width // pages_ref.shape[1]
@@ -105,7 +106,7 @@
         out_ref[0, at, :] = (kept_ref[request, head] * start.astype(F32) + added).astype(BF16)
 
 
-def state_part(where_from, kept_share, got_pages, x_inputs, b_proj, weight):
+def state_part(where_from, kept_share, got_pages, x_inputs, b_proj, weight, earlier):
     reqs_dev, _, inner_tp = x_inputs.shape
     heads = weight.shape[2]
 
@@ -119,12 +120,13 @@
         grid_spec=pltpu.PrefetchScalarGridSpec(
             num_scalar_prefetch=2,
             grid=(reqs_dev,),
-            in_specs=[pl.BlockSpec(memory_space=pltpu.VMEM), one(x_inputs), one(b_proj), one(weight)],
+            in_specs=[pl.BlockSpec(memory_space=pltpu.VMEM), one(x_inputs), one(b_proj), one(weight)]
+            + [ANYWHERE] * len(earlier),
             out_specs=one(out),
         ),
         compiler_params=pltpu.CompilerParams(vmem_limit_bytes=48 * 2**20),
         cost_estimate=NO_COST,
-    )(where_from, kept_share, got_pages, x_inputs, b_proj, weight)
+    )(where_from, kept_share, got_pages, x_inputs, b_proj, weight, *earlier)
 
 
 def gate_kernel(pages, where_ref, pages_ref, c_ref, local_ref, factor_ref, *refs):
@@ -218,7 +220,7 @@
                 pltpu.SemaphoreType.DMA((len(rows) + len(blocks),)),
             ],
         ),
-        compiler_params=pltpu.CompilerParams(vmem_limit_bytes=40 * 2**20),
+        compiler_params=pltpu.CompilerParams(vmem_limit_bytes=60 * 2**20),
         cost_estimate=NO_COST,
     )(place, *[array for array, _, _ in rows], *[array for array, _ in blocks], *earlier)
 
@@ -263,49 +265,49 @@
     )(array)
 
 
-def assemble_kernel(place_ref, near_ref, kept_two, kept_three, came_two, came_three, out_ref):
-    low, even = place_ref[0] == 1, place_ref[1] == 1
-    half = near_ref.shape[1]
-    two, three = kept_two[...], kept_three[...]
-    kept = (jnp.where(low, two, three), jnp.where(low, three, two))
-    two, three = came_two[...], came_three[...]
-    came = (jnp.where(low, two, three), jnp.where(low, three, two))
-    parts = []
-    for mine, other in zip(kept, came):
-        parts += [jnp.where(even, mine, other), jnp.where(even, other, mine)]
-    far = jnp.concatenate(parts, axis=1)
-
-    @pl.when(low)
-    def _():
-        out_ref[:, :half] = near_ref[...]
-        out_ref[:, half:] = far
-
-    @pl.when(jnp.logical_not(low))
-    def _():
-        out_ref[:, :half] = far
-        out_ref[:, half:] = near_ref[...]
-
-
-def assemble(low, even, near, kept, came):
-    tokens, half = near.shape
+def assemble_kernel(place_ref, own_ref, kept_ref, two_ref, third_ref, out_ref):
+    even = place_ref[0] == 1
+    columns = third_ref.shape[1]
+    pair = 2 * columns
+
+    def both(mine, other):
+        parts = [jnp.where(even, mine, other), jnp.where(even, other, mine)]
+        return jnp.concatenate(parts, axis=1)
+
+    pairs = (
+        own_ref[:, :pair],
+        both(own_ref[:, pair:], two_ref[:, :columns]),
+        both(kept_ref[:, :columns], two_ref[:, columns:]),
+        both(kept_ref[:, columns:], third_ref[...]),
+    )
+    for at, value in enumerate(pairs):
+        first = pl.multiple_of(place_ref[1 + at], 128)
+        out_ref[:, pl.ds(first, pair)] = value
+
+
+def assemble(spot, even, own, kept, came_two, came_third):
+    tokens = own.shape[0]
+    columns = came_third.shape[1]
     tile = min(128, tokens)
 
     def spec(width):
         return pl.BlockSpec((tile, width), lambda step, place_ref: (step, 0))
 
-    place = jnp.stack([low.astype(jnp.int32), even.astype(jnp.int32)])
+    low = spot < 2
+    order = [spot, spot ^ 1, jnp.where(low, 2, 1), jnp.where(low, 3, 0)]
+    place = jnp.stack([even.astype(jnp.int32)] + [(at * 2 * columns).astype(jnp.int32) for at in order])
     return pl.pallas_call(
         assemble_kernel,
-        out_shape=jax.ShapeDtypeStruct((tokens, 2 * half), BF16),
+        out_shape=jax.ShapeDtypeStruct((tokens, 8 * columns), BF16),
         grid_spec=pltpu.PrefetchScalarGridSpec(
             num_scalar_prefetch=1,
             grid=(tokens // tile,),
-            in_specs=[spec(half)] + [spec(kept[0].shape[1])] * 4,
-            out_specs=spec(2 * half),
+            in_specs=[spec(part.shape[1]) for part in (own, kept, came_two, came_third)],
+            out_specs=spec(8 * columns),
         ),
         compiler_params=pltpu.CompilerParams(vmem_limit_bytes=16 * 2**20),
         cost_estimate=NO_COST,
-    )(place, near, *kept, *came)
+    )(place, own, kept, came_two, came_third)
 
 
 def on_device(
@@ -403,18 +405,16 @@
     if chain:
         beside_across = swapped(beside, "groups", 1)
         near_across = swapped(near, "groups", 1)
-        near_beside = swapped(near, "req", 1)
         second_outer = lax.ppermute(second_inner, "req", outward)
         local = in_turn(local)
         beside_across = in_turn(beside_across)
         near_across = in_turn(near_across)
-        near_beside_across = swapped(near_across, "req", 1)
-        near_beside = in_turn(near_beside)
         second_outer = in_turn(second_outer)
-        near_beside_across = in_turn(near_beside_across)
+        second = in_turn(pick(inside, second_inner, second_outer))
+        second_across = swapped(second, "groups", 1)
         third_inner[0] = in_turn(third_inner[0])
         third_outer = [lax.ppermute(third_inner[0], "req", outward)]
-        earlier = [third_inner[0], beside_across, near_beside, near_beside_across, second_outer]
+        earlier = [third_inner[0], beside_across, near_across, second]
     else:
         earlier = []
     got_pages = in_turn(got_pages)
@@ -426,17 +426,31 @@
     theirs = swapped(gated, "req", 1)
     if chain:
         third_inner += [lax.ppermute(held(near_halves[1], gated), "req", middle)]
-        second = in_turn(pick(inside, second_inner, second_outer, [gated]))
-        second_across = swapped(second, "groups", 1)
     partners = in_turn(partners)
     own_rows = [(gated, 0, first_unit), (partners, 0, other_unit)]
-    end_state = in_turn(
-        state_part(after(where_from, partners), kept_share, got_pages, x_inputs, b_proj, weight)
-    )
+
+    def state(earlier):
+        return in_turn(
+            state_part(where_from, kept_share, got_pages, x_inputs, b_proj, weight, earlier)
+        )
 
     if chain:
-        spot_bit, parity = spot % 2, own_index % 2
         mine_first, across_first = group * share, (1 - group) * share
+
+        def halved(mine, across, first):
+            return [(mine, first + mine_first), (across, first + across_first)]
+
+        def quartered(mine, across, first):
+            quarters = []
+            for at in range(2):
+                quarters += halved(mine[at], across[at], first + at * (share // 2))
+            return quarters
+
+        parity = own_index % 2
+        own_blocks = [(block, parity * columns)]
+        own_blocks += halved(beside, beside_across, (1 - parity) * columns)
+        own_blocks += halved(near, near_across, 2 * columns)
+        own_out = in_turn(project(own_rows, own_blocks))
         third, third_across = [], []
 
         def third_part(at):
@@ -447,37 +461,28 @@
         third_inner[1] = in_turn(third_inner[1])
         third_outer += [lax.ppermute(third_inner[1], "req", outward)]
         third_part(0)
-        near_blocks = [(block, (spot_bit * 2 + parity) * columns)]
-        for bit, odd, mine, across in (
-            (spot_bit, 1 - parity, beside, beside_across),
-            (1 - spot_bit, parity, near, near_across),
-            (1 - spot_bit, 1 - parity, near_beside, near_beside_across),
-        ):
-            first = (bit * 2 + odd) * columns
-            near_blocks += [(mine, first + mine_first), (across, first + across_first)]
-        near_out = in_turn(project(own_rows, near_blocks, [third[0]]))
+        third_part(1)
+        end_state = state([third[1]])
+        second_across = in_turn(second_across)
         third_across[0] = in_turn(third_across[0])
-        third_part(1)
-        second_blocks = [(second, mine_first), (in_turn(second_across), across_first)]
-        theirs = in_turn(theirs)
-        theirs_other = swapped(theirs, "tp", 1)
-        kept = [in_turn(project(own_rows, second_blocks, [third[1], theirs]))]
-        theirs_other = in_turn(theirs_other)
+        theirs = held(theirs, second_across, third_across[0])
+        theirs_other = in_turn(swapped(theirs, "tp", 1))
         their_rows = [(theirs, 0, first_unit), (theirs_other, 0, other_unit)]
-        came = [swapped(in_turn(project(their_rows, second_blocks)), "req", 1)]
+        far_blocks = halved(near, near_across, 0) + halved(second, second_across, columns)
+        came_two = swapped(in_turn(project(their_rows, far_blocks, [end_state])), "req", 1)
         third_across[1] = in_turn(third_across[1])
-        third_blocks = []
-        for at in range(2):
-            half = at * (share // 2)
-            third_blocks += [
-                (third[at], mine_first + half),
-                (third_across[at], across_first + half),
-            ]
+        third_blocks = quartered(third, third_across, 0)
         came_third = in_turn(project(their_rows, third_blocks))
-        came += [swapped(came_third, "req", 1)]
-        kept += [project(own_rows, third_blocks, [came_third])]
-        mixed_out = assemble(low, even, near_out, kept, came)
+        came_two = in_turn(came_two)
+        kept = project(
+            own_rows,
+            halved(second, second_across, 0) + quartered(third, third_across, columns),
+            [came_third],
+        )
+        came_third = swapped(came_third, "req", 1)
+        mixed_out = assemble(spot, even, own_out, kept, came_two, came_third)
     else:
+        end_state = state([])
         parities = [list(range(first, n_req, 2)) for first in range(2)]
         mine = lax.all_gather(piece, "req", axis=0, axis_index_groups=parities)
         across = swapped(mine, "groups", 1)

time: 266 us -> 255 us (0.959)
  local copies, waits for them, and re-layouts: 36.7 us -> 23.7 us
  waiting for transfers between devices: 102 us -> 112 us
  starting transfers between devices: 41.7 us -> 33.2 us
    ppermute x14 -> x12, waiting for transfers between devices: 89.6 us -> 56.3 us  [swapped(): return lax.ppermute(value, axis, pairs)]
    ppermute x1, waiting for transfers between devices: 9.33 us -> 36.8 us  [on_device(): second_outer = lax.ppermute(second_inner, 'req', outward)]
    unnamed x89 -> x61, local copies, waits for them, and re-layouts: 24.5 us -> 12.6 us
    ppermute x1, waiting for transfers between devices: 0.01 us -> 7.74 us  [on_device(): third_inner = [lax.ppermute(near_halves[0], 'req', middle)]]
    ppermute x1, waiting for transfers between devices: 0.01 us -> 6.98 us  [on_device(): third_outer += [lax.ppermute(third_inner[1], 'req', outward)]]
    ppermute x1, starting transfers between devices: 5.03 us -> 2.13 us  [on_device(): third_outer += [lax.ppermute(third_inner[1], 'req', outward)]]
    ppermute x1, starting transfers between devices: 5.04 us -> 2.14 us  [on_device(): third_outer = [lax.ppermute(third_inner[0], 'req', outward)]]
    ppermute x14 -> x12, starting transfers between devices: 14.4 us -> 11.7 us  [swapped(): return lax.ppermute(value, axis, pairs)]
  transfers between devices with their start and end apart: 21 -> 19, of which waited for: 8 -> 13; matrix products, arithmetic and copies ran while one was open for 8% -> 8% of each run, Pallas kernels for 21% -> 23%
where the time goes in v3:
time: 255 us; the launch traced here: 252 us
  waiting for transfers between devices  112 us (44%)
  Pallas kernels  71.6 us (28%)
  starting transfers between devices  33.2 us (13%)
  local copies, waits for them, and re-layouts  23.7 us (9%)
  other arithmetic  11 us (4%)
    ppermute x12, waiting for transfers between devices, swapped(): return lax.ppermute(value, axis, pairs)  56.3 us
    ppermute x1, waiting for transfers between devices, on_device(): second_outer = lax.ppermute(second_inner, 'req', outward)  36.8 us
    pallas_call x4, Pallas kernels, project(): pl.pallas_call(lambda *refs: project_kernel(row_plan, block_plan, len(ear...  34.9 us
    unnamed x61, local copies, waits for them, and re-layouts  12.6 us
    ppermute x12, starting transfers between devices, swapped(): return lax.ppermute(value, axis, pairs)  11.7 us
    pallas_call x1, Pallas kernels, gate(): pl.pallas_call(lambda *refs: gate_kernel(pages, *refs), out_shape=jax.Sha...  9.64 us
    ppermute x1, waiting for transfers between devices, on_device(): third_inner = [lax.ppermute(near_halves[0], 'req', middle)]  7.74 us
    pallas_call x3, Pallas kernels, pick(): pl.pallas_call(pick_kernel, out_shape=jax.ShapeDtypeStruct(yes.shape, yes...  7.33 us
  transfers between devices with their start and end apart: 19, of which 13 were waited for; matrix products, arithmetic and copies ran while one was open for 8% of the time, Pallas kernels for 23%

profile of v3, /device:TPU:16, one launch (start us, length us, event | category | flops | bytes accessed | tf_op | source)
XLA Modules:
  0.0 252.3 jit_solution(16082362205350854739)
XLA Ops:
  0.7 2.5 dynamic-slice_bitcast_fusion
  3.2 1.6 collective-permute-start
  4.7 1.9 collective-permute-start.1
  6.7 1.6 collective-permute-start.2
  8.8 0.7 reduce.5
  10.2 2.0 multiply_convert_fusion
  12.1 2.8 %gather_fusion = bf16[128,64,256]{2,1,0:T(8,128)(2,1)} fusion(bf16[64,64,256]{2,1,0:T(8,128)(2,1)S(1)} %multiply_convert_fusion, s32[1024]{0:T(1024)S(1)} %pad_clamp_fusion), kind=kCustom, calls=%fused_computation | custom fusion | bytes 8389120 | tf_op jit(solution)/shard_map/gather | solution.py:373
  14.9 19.0 %collective-permute-done.refs_1_.in_ref.refs_6_.refs_3_ = bf16[160,4096]{1,0:T(8,128)(2,1)S(1)} collective-permute-done((bf16[160,4096]{1,0:T(8,128)(2,1)}, bf16[160,4096]{1,0:T(8,128)(2,1)S(1)}, u32[]{:S(2)}, u32[]{:S(2)}) %collective-permute-start) | collective-permute-done | bytes 1310752 | tf_op jit(solution)/shard_map/ppermute | solution.py:14
  33.9 3.3 %collective-permute-done.1.refs_2_.yes_ref = bf16[160,4096]{1,0:T(8,128)(2,1)} collective-permute-done((bf16[160,4096]{1,0:T(8,128)(2,1)}, bf16[160,4096]{1,0:T(8,128)(2,1)}, u32[]{:S(2)}, u32[]{:S(2)}) %collective-permute-start.1) | collective-permute-done | bytes 1310752 | tf_op jit(solution)/shard_map/ppermute | solution.py:359
  37.3 5.6 %all-to-all-start = ((bf16[128,64,256]{2,1,0:T(8,128)(2,1)}), bf16[128,64,256]{2,1,0:T(8,128)(2,1)}, u32[]{:S(2)}, u32[]{:S(2)}) async-start(bf16[128,64,256]{2,1,0:T(8,128)(2,1)} %shard_map.158.refs_10_), calls=%async_computation | async-start | bytes 8388608 | tf_op jit(solution)/shard_map/all_to_all | solution.py:382
  43.1 1.5 collective-permute-start.6
  44.6 4.4 %collective-permute-start.4 = (bf16[160,4096]{1,0:T(8,128)(2,1)}, bf16[160,4096]{1,0:T(8,128)(2,1)}, u32[]{:S(2)}, u32[]{:S(2)}) collective-permute-start(bf16[160,4096]{1,0:T(8,128)(2,1)} %collective-permute-done.1.refs_2_.yes_ref), channel_id=1, source_target_pairs={{4,0},{6,2},{8,12},{10,14},{5,1},{7,3},{9,13},{11,15},{20,16},{22,... | collective-permute-start | bytes 3932168 | tf_op jit(solution)/shard_map/ppermute | solution.py:408
  49.6 0.8 fusion.1.refs_9_
  50.5 0.7 copy-done.20
  51.5 1.1 reduce-window.6
  52.9 2.5 shard_map.159
  55.3 1.9 collective-permute-start.3
  57.3 0.8 copy.38
  58.2 1.7 exponential_multiply_fusion.1
  60.0 1.8 fusion.6
  61.8 1.0 copy.40.refs_7_
  62.9 1.6 copy-done.5
  64.5 1.6 copy-done.11
  66.1 0.9 copy-done.15
  67.0 0.9 copy-done.17
  68.0 6.7 %shard_map.160 = (f32[2,256,2048]{2,1,0:T(8,128)}, f32[2,256,2048]{2,1,0:T(8,128)}) custom-call(f32[16]{0:T(128)S(1)} %copy-done.18, bf16[2,256,2048]{2,1,0:T(8,128)(2,1)S(1)} %copy-done.5, bf16[2,256,2048]{2,1,0:T(8,128)(2,1)S(1)} %copy-done.11, bf16[2,256,256]{2,1,0:T(8,128)(2,1)S(1)} %copy-done.13, bf16[2,256,256]{2,1,0:T(8,128)(2,1)S(1)} %copy-done.12, ...), custom_call_target="tpu_custom_call" | custom-call | tf_op jit(solution)/shard_map/pallas_call | solution.py:80
  75.1 24.9 %collective-permute-done.5.refs_7_.refs_4_ = bf16[160,4096]{1,0:T(8,128)(2,1)S(1)} collective-permute-done((bf16[160,4096]{1,0:T(8,128)(2,1)}, bf16[160,4096]{1,0:T(8,128)(2,1)S(1)}, u32[]{:S(2)}, u32[]{:S(2)}) %collective-permute-start.5) | collective-permute-done | bytes 1310752 | tf_op jit(solution)/shard_map/ppermute | solution.py:14
  99.9 36.8 %collective-permute-done.4.no_ref = bf16[160,4096]{1,0:T(8,128)(2,1)} collective-permute-done((bf16[160,4096]{1,0:T(8,128)(2,1)}, bf16[160,4096]{1,0:T(8,128)(2,1)}, u32[]{:S(2)}, u32[]{:S(2)}) %collective-permute-start.4) | collective-permute-done | bytes 1310752 | tf_op jit(solution)/shard_map/ppermute | solution.py:408
  136.7 2.9 %shard_map.161.refs_8_.refs_5_.refs_3_ = bf16[160,4096]{1,0:T(8,128)(2,1)} custom-call(s32[1]{0:T(128)} %bitcast.17.flag_ref, bf16[160,4096]{1,0:T(8,128)(2,1)} %collective-permute-done.1.refs_2_.yes_ref, bf16[160,4096]{1,0:T(8,128)(2,1)} %collective-permute-done.4.no_ref), custom_call_target="tpu_custom_call" | custom-call | tf_op jit(solution)/shard_map/pallas_call | solution.py:235
  139.6 7.7 %collective-permute-done.3.refs_5_.yes_ref = bf16[80,4096]{1,0:T(8,128)(2,1)} collective-permute-done((bf16[80,4096]{1,0:T(8,128)(2,1)}, bf16[80,4096]{1,0:T(8,128)(2,1)}, u32[]{:S(2)}, u32[]{:S(2)}) %collective-permute-start.3) | collective-permute-done | bytes 655392 | tf_op jit(solution)/shard_map/ppermute | solution.py:379
  147.4 1.3 copy-done
  148.7 9.6 %shard_map.162.refs_1_ = bf16[512,2048]{1,0:T(8,128)(2,1)} custom-call(s32[64]{0:T(128)S(1)} %multiply_add_fusion.refs_0_, bf16[128,64,256]{2,1,0:T(8,128)(2,1)} %all-to-all-done.refs_1_.refs_2_, bf16[2,256,256]{2,1,0:T(8,128)(2,1)S(1)} %copy-done.12, f32[2,256,2048]{2,1,0:T(8,128)} %get-tuple-element.39.refs_3_, f32[2,256,2048]{2,1,0:T(8,128)} %get-tuple-element.46.refs_4_, ...), custom_call_target="tpu_custom_call" | custom-call | tf_op jit(solution)/shard_map/pallas_call | solution.py:150
  158.4 0.6 collective-permute-start.14
  159.0 3.4 %collective-permute-start.9 = (bf16[80,4096]{1,0:T(8,128)(2,1)}, bf16[80,4096]{1,0:T(8,128)(2,1)}, u32[]{:S(2)}, u32[]{:S(2)}) collective-permute-start(bf16[80,4096]{1,0:T(8,128)(2,1)} %shard_map.164), channel_id=1, source_target_pairs={{4,8},{8,4},{6,10},{10,6},{5,9},{9,5},{7,11},{11,7},{20,24},{24,20... | collective-permute-start | bytes 1966088 | tf_op jit(solution)/shard_map/ppermute | solution.py:428
  162.4 2.1 collective-permute-start.11
  164.5 1.5 collective-permute-start.8
  166.6 10.6 %shard_map.163.own_ref = bf16[512,960]{1,0:T(8,128)(2,1)} custom-call(s32[7]{0:T(128)} %stack.104.refs_0_, bf16[512,2048]{1,0:T(8,128)(2,1)} %shard_map.162.refs_1_, bf16[512,2048]{1,0:T(8,128)(2,1)} %collective-permute-done.7.refs_2_, bf16[320,4096]{1,0:T(8,128)(2,1)} %bitcast.49, bf16[160,4096]{1,0:T(8,128)(2,1)} %collective-permute-done.2.refs_3_.refs_4_, ...), custom_call_target="tpu_custom_call" | custom-call | tf_op jit(solution)/shard_map/pallas_call | solution.py:209
  177.3 0.7 collective-permute-done.9.yes_ref
  178.0 2.1 collective-permute-start.10
  180.1 2.2 shard_map.165.refs_3_.refs_5_
  182.3 1.5 collective-permute-start.12
  183.8 0.7 slice.16
  184.6 1.9 exponential_multiply_fusion.refs_5_
  186.5 7.0 %collective-permute-done.10.no_ref = bf16[80,4096]{1,0:T(8,128)(2,1)} collective-permute-done((bf16[80,4096]{1,0:T(8,128)(2,1)}, bf16[80,4096]{1,0:T(8,128)(2,1)}, u32[]{:S(2)}, u32[]{:S(2)}) %collective-permute-start.10) | collective-permute-done | bytes 655392 | tf_op jit(solution)/shard_map/ppermute | solution.py:462
  193.5 2.2 shard_map.166.refs_6_.refs_5_.refs_7_
  195.7 1.1 copy-done.3
  196.8 0.9 copy-done.14
  197.8 0.9 copy-done.16
  198.7 7.3 %shard_map.167.refs_7_ = bf16[2,2048,256]{2,1,0:T(8,128)(2,1)} custom-call(s32[64]{0:T(128)S(1)} %multiply_add_fusion.refs_0_, f32[2,16]{1,0:T(2,128)S(1)} %exponential_multiply_fusion.2.refs_1_, bf16[128,64,256]{2,1,0:T(8,128)(2,1)} %all-to-all-done.refs_1_.refs_2_, bf16[2,256,2048]{2,1,0:T(8,128)(2,1)S(1)} %copy-done.6, ...), custom_call_target="tpu_custom_call" | custom-call | tf_op jit(solution)/shard_map/pallas_call | solution.py:117
  206.1 3.2 %collective-permute-done.12.refs_2_.refs_4_.refs_6_ = bf16[80,4096]{1,0:T(8,128)(2,1)} collective-permute-done((bf16[80,4096]{1,0:T(8,128)(2,1)}, bf16[80,4096]{1,0:T(8,128)(2,1)}, u32[]{:S(2)}, u32[]{:S(2)}) %collective-permute-start.12) | collective-permute-done | bytes 655392 | tf_op jit(solution)/shard_map/ppermute | solution.py:14
  209.3 1.6 collective-permute-start.13
  210.8 0.7 stack.112.refs_0_
  211.5 2.3 collective-permute-done.15.refs_2_
  213.8 8.7 %shard_map.169 = bf16[512,640]{1,0:T(8,128)(2,1)} custom-call(s32[6]{0:T(128)} %stack.112.refs_0_, bf16[512,2048]{1,0:T(8,128)(2,1)} %shard_map.168.refs_1_, bf16[512,2048]{1,0:T(8,128)(2,1)} %collective-permute-done.15.refs_2_, bf16[160,4096]{1,0:T(8,128)(2,1)} %copy-done.19, bf16[160,4096]{1,0:T(8,128)(2,1)} %copy-done.2, ...), custom_call_target="tpu_custom_call" | custom-call | tf_op jit(solution)/shard_map/pallas_call | solution.py:209
  222.5 0.6 collective-permute-start.16
  223.1 0.6 stack.115.refs_0_
  223.7 2.7 %collective-permute-done.13.refs_6_.refs_8_ = bf16[80,4096]{1,0:T(8,128)(2,1)S(1)} collective-permute-done((bf16[80,4096]{1,0:T(8,128)(2,1)S(1)}, bf16[80,4096]{1,0:T(8,128)(2,1)S(1)}, u32[]{:S(2)}, u32[]{:S(2)}) %collective-permute-start.13) | collective-permute-done | bytes 655392 | tf_op jit(solution)/shard_map/ppermute | solution.py:14
  226.4 0.8 copy-done.21
  227.2 6.7 %shard_map.170.refs_9_ = bf16[512,320]{1,0:T(8,128)(2,1)} custom-call(s32[6]{0:T(128)} %stack.115.refs_0_, bf16[512,2048]{1,0:T(8,128)(2,1)} %shard_map.168.refs_1_, bf16[512,2048]{1,0:T(8,128)(2,1)} %collective-permute-done.15.refs_2_, bf16[80,4096]{1,0:T(8,128)(2,1)} %shard_map.165.refs_3_.refs_5_, ...), custom_call_target="tpu_custom_call" | custom-call | tf_op jit(solution)/shard_map/pallas_call | solution.py:209
  234.0 0.6 collective-permute-start.17
  235.3 8.8 %shard_map.171.kept_ref = bf16[512,640]{1,0:T(8,128)(2,1)} custom-call(s32[8]{0:T(128)} %stack.111.refs_0_, bf16[512,2048]{1,0:T(8,128)(2,1)} %shard_map.162.refs_1_, bf16[512,2048]{1,0:T(8,128)(2,1)} %collective-permute-done.7.refs_2_, bf16[160,4096]{1,0:T(8,128)(2,1)} %shard_map.161.refs_8_.refs_5_.refs_3_, ...), custom_call_target="tpu_custom_call" | custom-call | tf_op jit(solution)/shard_map/pallas_call | solution.py:209
  244.1 3.8 %collective-permute-done.17.third_ref = bf16[512,320]{1,0:T(8,128)(2,1)S(1)} collective-permute-done((bf16[512,320]{1,0:T(8,128)(2,1)}, bf16[512,320]{1,0:T(8,128)(2,1)S(1)}, u32[]{:S(2)}, u32[]{:S(2)}) %collective-permute-start.17) | collective-permute-done | bytes 327712 | tf_op jit(solution)/shard_map/ppermute | solution.py:14
  248.0 1.1 copy-done.10
  249.0 3.2 %shard_map.172 = bf16[512,2560]{1,0:T(8,128)(2,1)} custom-call(s32[5]{0:T(128)S(1)} %stack.96.place_ref, bf16[512,960]{1,0:T(8,128)(2,1)S(1)} %copy-done.9, bf16[512,640]{1,0:T(8,128)(2,1)S(1)} %copy-done.10, bf16[512,640]{1,0:T(8,128)(2,1)S(1)} %collective-permute-done.16.two_ref, bf16[512,320]{1,0:T(8,128)(2,1)S(1)} %collective-permute-done.17.third_ref), custom_call_target="tpu_custom_call" | custom-call | tf_op jit(solution)/shard_map/pallas_call | solution.py:299
  (92 shorter events, 4.7 us)
Async XLA Ops:
  0.6 8.1 %copy-start.25 = (s32[1,16,32,1]{2,3,1,0:T(1,128)S(1)}, s32[1,16,32,1]{2,3,1,0:T(1,128)}, u32[]{:S(2)}) copy-start(s32[1,16,32,1]{2,3,1,0:T(1,128)} %param.25) | copy-start | bytes 6148
  0.6 9.1 %copy-start.24 = (s32[1,16,32]{2,1,0:T(8,128)S(1)}, s32[1,16,32]{2,1,0:T(8,128)}, u32[]{:S(2)}) copy-start(s32[1,16,32]{2,1,0:T(8,128)} %param.26) | copy-start | bytes 6148
  0.7 9.5 %copy-start.23 = (bf16[64,64]{1,0:T(8,128)(2,1)S(1)}, bf16[64,64]{1,0:T(8,128)(2,1)}, u32[]{:S(2)}) copy-start(bf16[64,64]{1,0:T(8,128)(2,1)} %param.24) | copy-start | bytes 24580
  3.2 30.7 %collective-permute-start = (bf16[160,4096]{1,0:T(8,128)(2,1)}, bf16[160,4096]{1,0:T(8,128)(2,1)S(1)}, u32[]{:S(2)}, u32[]{:S(2)}) collective-permute-start(bf16[160,4096]{1,0:T(8,128)(2,1)} %dynamic-slice_bitcast_fusion), channel_id=1, source_target_pairs={{0,4},{2,6},{4,0},{6,2},{8,12},{10,14},{12,8},{14,10},{1,5},{3,7},... | collective-permute-start | bytes 3932168 | tf_op jit(solution)/shard_map/ppermute | solution.py:14
  4.7 32.4 %collective-permute-start.1 = (bf16[160,4096]{1,0:T(8,128)(2,1)}, bf16[160,4096]{1,0:T(8,128)(2,1)}, u32[]{:S(2)}, u32[]{:S(2)}) collective-permute-start(bf16[160,4096]{1,0:T(8,128)(2,1)} %dynamic-slice_bitcast_fusion), channel_id=1, source_target_pairs={{4,8},{8,4},{6,10},{10,6},{5,9},{9,5},{7,11},{11,7},{20,24},{24,20... | collective-permute-start | bytes 3932168 | tf_op jit(solution)/shard_map/ppermute | solution.py:359
  6.7 30.6 %collective-permute-start.2 = (bf16[160,4096]{1,0:T(8,128)(2,1)}, bf16[160,4096]{1,0:T(8,128)(2,1)}, u32[]{:S(2)}, u32[]{:S(2)}) collective-permute-start(bf16[160,4096]{1,0:T(8,128)(2,1)} %dynamic-slice_bitcast_fusion), channel_id=1, source_target_pairs={{0,2},{2,0},{4,6},{6,4},{8,10},{10,8},{12,14},{14,12},{1,3},{3,1},... | collective-permute-start | bytes 3932168 | tf_op jit(solution)/shard_map/ppermute | solution.py:14
  33.9 3.4 %copy-start.19 = (bf16[160,4096]{1,0:T(8,128)(2,1)}, bf16[160,4096]{1,0:T(8,128)(2,1)S(1)}, u32[]{:S(2)}) copy-start(bf16[160,4096]{1,0:T(8,128)(2,1)S(1)} %collective-permute-done.refs_1_.in_ref.refs_6_.refs_3_) | copy-start | bytes 3932164
  37.3 5.7 %copy-start.28 = (s32[2]{0:T(128)S(1)}, s32[2]{0:T(128)}, u32[]{:S(2)}) copy-start(s32[2]{0:T(128)} %param.27) | copy-start | bytes 28
  37.3 5.7 %copy-start.29 = (f32[16]{0:T(128)S(1)}, f32[16]{0:T(128)}, u32[]{:S(2)}) copy-start(f32[16]{0:T(128)} %param.21) | copy-start | bytes 196
  37.3 5.7 %copy-start.27 = (s32[2]{0:T(128)S(1)}, s32[2]{0:T(128)}, u32[]{:S(2)}) copy-start(s32[2]{0:T(128)} %param.28) | copy-start | bytes 28
  37.3 13.1 %copy-start.22 = (f32[2,256,16]{1,2,0:T(8,128)S(1)}, f32[2,256,16]{1,2,0:T(8,128)}, u32[]{:S(2)}) copy-start(f32[2,256,16]{1,2,0:T(8,128)} %param.19) | copy-start | bytes 98308
  37.3 13.9 %copy-start.26 = (f32[16]{0:T(128)S(1)}, f32[16]{0:T(128)}, u32[]{:S(2)}) copy-start(f32[16]{0:T(128)} %param.20) | copy-start | bytes 196
  37.3 110.0 %all-to-all-start = ((bf16[128,64,256]{2,1,0:T(8,128)(2,1)}), bf16[128,64,256]{2,1,0:T(8,128)(2,1)}, u32[]{:S(2)}, u32[]{:S(2)}) async-start(bf16[128,64,256]{2,1,0:T(8,128)(2,1)} %shard_map.158.refs_10_), calls=%async_computation | async-start | bytes 8388608 | tf_op jit(solution)/shard_map/all_to_all | solution.py:382
  43.1 31.9 %collective-permute-start.6 = (bf16[160,4096]{1,0:T(8,128)(2,1)}, bf16[160,4096]{1,0:T(8,128)(2,1)S(1)}, u32[]{:S(2)}, u32[]{:S(2)}) collective-permute-start(bf16[160,4096]{1,0:T(8,128)(2,1)} %collective-permute-done.2.refs_3_.refs_4_), channel_id=1, source_target_pairs={{0,16},{16,0},{1,17},{17,1},{2,18},{18,2},{3,19},{19,3},{4,20},{20... | collective-permute-start | bytes 3932168 | tf_op jit(solution)/shard_map/ppermute | solution.py:14
  44.6 92.1 %collective-permute-start.4 = (bf16[160,4096]{1,0:T(8,128)(2,1)}, bf16[160,4096]{1,0:T(8,128)(2,1)}, u32[]{:S(2)}, u32[]{:S(2)}) collective-permute-start(bf16[160,4096]{1,0:T(8,128)(2,1)} %collective-permute-done.1.refs_2_.yes_ref), channel_id=1, source_target_pairs={{4,0},{6,2},{8,12},{10,14},{5,1},{7,3},{9,13},{11,15},{20,16},{22,... | collective-permute-start | bytes 3932168 | tf_op jit(solution)/shard_map/ppermute | solution.py:408
  49.0 50.9 %collective-permute-start.5 = (bf16[160,4096]{1,0:T(8,128)(2,1)}, bf16[160,4096]{1,0:T(8,128)(2,1)S(1)}, u32[]{:S(2)}, u32[]{:S(2)}) collective-permute-start(bf16[160,4096]{1,0:T(8,128)(2,1)} %copy-done.19), channel_id=1, source_target_pairs={{0,16},{16,0},{1,17},{17,1},{2,18},{18,2},{3,19},{19,3},{4,20},{20... | collective-permute-start | bytes 3932168 | tf_op jit(solution)/shard_map/ppermute | solution.py:14
  50.5 0.7 copy-start.20
  51.4 11.5 %copy-start.12 = (bf16[2,256,256]{2,1,0:T(8,128)(2,1)S(1)}, bf16[2,256,256]{2,1,0:T(8,128)(2,1)}, u32[]{:S(2)}) copy-start(bf16[2,256,256]{2,1,0:T(8,128)(2,1)} %refs_2_.3) | copy-start | bytes 786436
  51.4 11.5 %copy-start.13 = (bf16[2,256,256]{2,1,0:T(8,128)(2,1)S(1)}, bf16[2,256,256]{2,1,0:T(8,128)(2,1)}, u32[]{:S(2)}) copy-start(bf16[2,256,256]{2,1,0:T(8,128)(2,1)} %refs_4_.3) | copy-start | bytes 786436
  51.4 11.5 %copy-start.18 = (f32[16]{0:T(128)S(1)}, f32[16]{0:T(128)}, u32[]{:S(2)}) copy-start(f32[16]{0:T(128)} %refs_0_.1) | copy-start | bytes 196
  55.3 92.0 %collective-permute-start.3 = (bf16[80,4096]{1,0:T(8,128)(2,1)}, bf16[80,4096]{1,0:T(8,128)(2,1)}, u32[]{:S(2)}, u32[]{:S(2)}) collective-permute-start(bf16[80,4096]{1,0:T(8,128)(2,1)} %get-tuple-element.36), channel_id=1, source_target_pairs={{4,8},{8,4},{6,10},{10,6},{5,9},{9,5},{7,11},{11,7},{20,24},{24,20... | collective-permute-start | bytes 1966088 | tf_op jit(solution)/shard_map/ppermute | solution.py:379
  59.9 14.8 %copy-start.8 = (f32[2,16,256]{1,2,0:T(8,128)}, f32[2,16,256]{1,2,0:T(8,128)S(1)}, u32[]{:S(2)}) copy-start(f32[2,16,256]{1,2,0:T(8,128)S(1)} %get-tuple-element.65) | copy-start | bytes 98308
  62.9 1.6 copy-start.5
  64.5 1.6 copy-start.11
  66.1 0.9 copy-start.15
  67.0 0.9 copy-start.17
  75.1 72.3 %copy-start.7 = (bf16[160,4096]{1,0:T(8,128)(2,1)}, bf16[160,4096]{1,0:T(8,128)(2,1)S(1)}, u32[]{:S(2)}) copy-start(bf16[160,4096]{1,0:T(8,128)(2,1)S(1)} %collective-permute-done.6.refs_6_.refs_5_) | copy-start | bytes 3932164
  99.9 58.4 %copy-start.2 = (bf16[160,4096]{1,0:T(8,128)(2,1)}, bf16[160,4096]{1,0:T(8,128)(2,1)S(1)}, u32[]{:S(2)}) copy-start(bf16[160,4096]{1,0:T(8,128)(2,1)S(1)} %collective-permute-done.5.refs_7_.refs_4_) | copy-start | bytes 3932164
  147.3 1.3 copy-start
  158.3 6.2 %copy-start.1 = (bf16[160,4096]{1,0:T(8,128)(2,1)S(1)}, bf16[160,4096]{1,0:T(8,128)(2,1)}, u32[]{:S(2)}) copy-start(bf16[160,4096]{1,0:T(8,128)(2,1)} %shard_map.161.refs_8_.refs_5_.refs_3_) | copy-start | bytes 3932164
  158.3 8.3 %collective-permute-start.7 = (bf16[512,2048]{1,0:T(8,128)(2,1)}, bf16[512,2048]{1,0:T(8,128)(2,1)}, u32[]{:S(2)}, u32[]{:S(2)}) collective-permute-start(bf16[512,2048]{1,0:T(8,128)(2,1)} %shard_map.162.refs_1_), channel_id=1, source_target_pairs={{0,1},{1,0},{2,3},{3,2},{4,5},{5,4},{6,7},{7,6},{8,9},{9,8},{10,11... | collective-permute-start | bytes 6291464 | tf_op jit(solution)/shard_map/ppermute | solution.py:14
  158.4 50.9 %collective-permute-start.14 = (bf16[512,2048]{1,0:T(8,128)(2,1)}, bf16[512,2048]{1,0:T(8,128)(2,1)}, u32[]{:S(2)}, u32[]{:S(2)}) collective-permute-start(bf16[512,2048]{1,0:T(8,128)(2,1)} %shard_map.162.refs_1_), channel_id=1, source_target_pairs={{0,2},{2,0},{4,6},{6,4},{8,10},{10,8},{12,14},{14,12},{1,3},{3,1},... | collective-permute-start | bytes 6291464 | tf_op jit(solution)/shard_map/ppermute | solution.py:14
  159.0 19.0 %collective-permute-start.9 = (bf16[80,4096]{1,0:T(8,128)(2,1)}, bf16[80,4096]{1,0:T(8,128)(2,1)}, u32[]{:S(2)}, u32[]{:S(2)}) collective-permute-start(bf16[80,4096]{1,0:T(8,128)(2,1)} %shard_map.164), channel_id=1, source_target_pairs={{4,8},{8,4},{6,10},{10,6},{5,9},{9,5},{7,11},{11,7},{20,24},{24,20... | collective-permute-start | bytes 1966088 | tf_op jit(solution)/shard_map/ppermute | solution.py:428
  162.4 17.8 %collective-permute-start.11 = (bf16[80,4096]{1,0:T(8,128)(2,1)}, bf16[80,4096]{1,0:T(8,128)(2,1)}, u32[]{:S(2)}, u32[]{:S(2)}) collective-permute-start(bf16[80,4096]{1,0:T(8,128)(2,1)} %collective-permute-done.3.refs_5_.yes_ref), channel_id=1, source_target_pairs={{4,0},{6,2},{8,12},{10,14},{5,1},{7,3},{9,13},{11,15},{20,16},{22,... | collective-permute-start | bytes 1966088 | tf_op jit(solution)/shard_map/ppermute | solution.py:416
  164.5 41.5 %collective-permute-start.8 = (bf16[160,4096]{1,0:T(8,128)(2,1)S(1)}, bf16[160,4096]{1,0:T(8,128)(2,1)}, u32[]{:S(2)}, u32[]{:S(2)}) collective-permute-start(bf16[160,4096]{1,0:T(8,128)(2,1)S(1)} %copy-done.1), channel_id=1, source_target_pairs={{0,16},{16,0},{1,17},{17,1},{2,18},{18,2},{3,19},{19,3},{4,20},{20... | collective-permute-start | bytes 3932168 | tf_op jit(solution)/shard_map/ppermute | solution.py:14
  177.3 18.4 %copy-start.6 = (bf16[2,256,2048]{2,1,0:T(8,128)(2,1)S(1)}, bf16[2,256,2048]{2,1,0:T(8,128)(2,1)}, u32[]{:S(2)}) copy-start(bf16[2,256,2048]{2,1,0:T(8,128)(2,1)} %refs_3_.3) | copy-start | bytes 6291460
  178.0 15.5 %collective-permute-start.10 = (bf16[80,4096]{1,0:T(8,128)(2,1)}, bf16[80,4096]{1,0:T(8,128)(2,1)}, u32[]{:S(2)}, u32[]{:S(2)}) collective-permute-start(bf16[80,4096]{1,0:T(8,128)(2,1)} %collective-permute-done.9.yes_ref), channel_id=1, source_target_pairs={{4,0},{6,2},{8,12},{10,14},{5,1},{7,3},{9,13},{11,15},{20,16},{22,... | collective-permute-start | bytes 1966088 | tf_op jit(solution)/shard_map/ppermute | solution.py:462
  182.3 26.9 %collective-permute-start.12 = (bf16[80,4096]{1,0:T(8,128)(2,1)}, bf16[80,4096]{1,0:T(8,128)(2,1)}, u32[]{:S(2)}, u32[]{:S(2)}) collective-permute-start(bf16[80,4096]{1,0:T(8,128)(2,1)} %shard_map.165.refs_3_.refs_5_), channel_id=1, source_target_pairs={{0,16},{16,0},{1,17},{17,1},{2,18},{18,2},{3,19},{19,3},{4,20},{20... | collective-permute-start | bytes 1966088 | tf_op jit(solution)/shard_map/ppermute | solution.py:14
  195.7 1.1 copy-start.3
  196.8 0.9 copy-start.14
  197.8 0.9 copy-start.16
  206.0 3.2 %copy-start.4 = (bf16[80,4096]{1,0:T(8,128)(2,1)S(1)}, bf16[80,4096]{1,0:T(8,128)(2,1)}, u32[]{:S(2)}) copy-start(bf16[80,4096]{1,0:T(8,128)(2,1)} %shard_map.166.refs_6_.refs_5_.refs_7_) | copy-start | bytes 1966084
  209.3 4.5 %collective-permute-start.15 = (bf16[512,2048]{1,0:T(8,128)(2,1)}, bf16[512,2048]{1,0:T(8,128)(2,1)}, u32[]{:S(2)}, u32[]{:S(2)}) collective-permute-start(bf16[512,2048]{1,0:T(8,128)(2,1)} %shard_map.168.refs_1_), channel_id=1, source_target_pairs={{0,1},{1,0},{2,3},{3,2},{4,5},{5,4},{6,7},{7,6},{8,9},{9,8},{10,11... | collective-permute-start | bytes 6291464 | tf_op jit(solution)/shard_map/ppermute | solution.py:14
  209.3 17.1 %collective-permute-start.13 = (bf16[80,4096]{1,0:T(8,128)(2,1)S(1)}, bf16[80,4096]{1,0:T(8,128)(2,1)S(1)}, u32[]{:S(2)}, u32[]{:S(2)}) collective-permute-start(bf16[80,4096]{1,0:T(8,128)(2,1)S(1)} %copy-done.4), channel_id=1, source_target_pairs={{0,16},{16,0},{1,17},{17,1},{2,18},{18,2},{3,19},{19,3},{4,20},{20... | collective-permute-start | bytes 1966088 | tf_op jit(solution)/shard_map/ppermute | solution.py:14
  222.5 21.7 %collective-permute-start.16 = (bf16[512,640]{1,0:T(8,128)(2,1)}, bf16[512,640]{1,0:T(8,128)(2,1)S(1)}, u32[]{:S(2)}, u32[]{:S(2)}) collective-permute-start(bf16[512,640]{1,0:T(8,128)(2,1)} %shard_map.169), channel_id=1, source_target_pairs={{0,2},{2,0},{4,6},{6,4},{8,10},{10,8},{12,14},{14,12},{1,3},{3,1},... | collective-permute-start | bytes 1966088 | tf_op jit(solution)/shard_map/ppermute | solution.py:14
  226.4 0.8 copy-start.21
  234.0 14.0 %collective-permute-start.17 = (bf16[512,320]{1,0:T(8,128)(2,1)}, bf16[512,320]{1,0:T(8,128)(2,1)S(1)}, u32[]{:S(2)}, u32[]{:S(2)}) collective-permute-start(bf16[512,320]{1,0:T(8,128)(2,1)} %shard_map.170.refs_9_), channel_id=1, source_target_pairs={{0,2},{2,0},{4,6},{6,4},{8,10},{10,8},{12,14},{14,12},{1,3},{3,1},... | collective-permute-start | bytes 983048 | tf_op jit(solution)/shard_map/ppermute | solution.py:14
  235.3 12.6 %copy-start.9 = (bf16[512,960]{1,0:T(8,128)(2,1)S(1)}, bf16[512,960]{1,0:T(8,128)(2,1)}, u32[]{:S(2)}) copy-start(bf16[512,960]{1,0:T(8,128)(2,1)} %shard_map.163.own_ref) | copy-start | bytes 2949124
  248.0 1.1 copy-start.10

commit v4 on v3

--- a/solution.py
+++ b/solution.py
@@ -124,7 +124,7 @@
             + [ANYWHERE] * len(earlier),
             out_specs=one(out),
         ),
-        compiler_params=pltpu.CompilerParams(vmem_limit_bytes=48 * 2**20),
+        compiler_params=pltpu.CompilerParams(vmem_limit_bytes=60 * 2**20),
         cost_estimate=NO_COST,
     )(where_from, kept_share, got_pages, x_inputs, b_proj, weight, *earlier)
 
@@ -142,7 +142,7 @@
 def gate(where_from, got_pages, c_proj, local, factor, earlier):
     reqs_dev, slots, inner_tp = local.shape
     _, page_rows, state_width = got_pages.shape
-    pages = min(8, inner_tp // page_rows)
+    pages = inner_tp // page_rows
     wide = pages * page_rows
     steps = inner_tp // wide
     wide_spec = pl.BlockSpec((1, slots, wide), lambda request, step, where_ref: (request, 0, step))
@@ -178,7 +178,7 @@
         copies.append(
             pltpu.make_async_copy(ref, held_rows.at[pl.ds(first, count), lanes], sems.at[at])
         )
-    for at, (ref, count) in enumerate(zip(block_refs, blocks), len(rows)):
+    for at, (ref, (count, _)) in enumerate(zip(block_refs, blocks), len(rows)):
         first = place_ref[at]
         first = 0 if len(blocks) == 1 else pl.multiple_of(first, 16)
         copies.append(
@@ -186,11 +186,15 @@
         )
     for copy in copies:
         copy.start()
-    for copy in copies:
+    for copy in copies[: len(rows)]:
         copy.wait()
     columns = held_blocks.shape[0]
+    waited = len(rows)
     for first in range(0, columns, 256):
         at = slice(first, min(first + 256, columns))
+        while waited < len(copies) and blocks[waited - len(rows)][1] < at.stop:
+            copies[waited].wait()
+            waited += 1
         out_ref[:, at] = lax.dot_general(
             held_rows[...], held_blocks[at, :], (((1,), (1,)), ((), ())), preferred_element_type=F32
         ).astype(BF16)
@@ -198,14 +202,14 @@
 
 def project(rows, blocks, earlier=()):
     count = max(first + array.shape[0] for array, first, _ in rows)
-    columns = sum(array.shape[0] for array, _ in blocks)
+    columns = sum(array.shape[0] for array, _, _ in blocks)
     inner = blocks[0][0].shape[1]
     place = jnp.stack(
         [jnp.asarray(at, jnp.int32) for _, _, at in rows]
-        + [jnp.asarray(at, jnp.int32) for _, at in blocks]
+        + [jnp.asarray(at, jnp.int32) for _, at, _ in blocks]
     )
     row_plan = [(first,) + array.shape for array, first, _ in rows]
-    block_plan = [array.shape[0] for array, _ in blocks]
+    block_plan = [(array.shape[0], least) for array, _, least in blocks]
     return pl.pallas_call(
         lambda *refs: project_kernel(row_plan, block_plan, len(earlier), *refs),
         out_shape=jax.ShapeDtypeStruct((count, columns), BF16),
@@ -222,7 +226,7 @@
         ),
         compiler_params=pltpu.CompilerParams(vmem_limit_bytes=60 * 2**20),
         cost_estimate=NO_COST,
-    )(place, *[array for array, _, _ in rows], *[array for array, _ in blocks], *earlier)
+    )(place, *[array for array, _, _ in rows], *[array for array, _, _ in blocks], *earlier)
 
 
 def pick_kernel(flag_ref, yes_ref, no_ref, *refs):
@@ -265,7 +269,7 @@
     )(array)
 
 
-def assemble_kernel(place_ref, own_ref, kept_ref, two_ref, third_ref, out_ref):
+def assemble_kernel(place_ref, own_ref, kept_second_ref, kept_third_ref, two_ref, third_ref, out_ref):
     even = place_ref[0] == 1
     columns = third_ref.shape[1]
     pair = 2 * columns
@@ -277,8 +281,8 @@
     pairs = (
         own_ref[:, :pair],
         both(own_ref[:, pair:], two_ref[:, :columns]),
-        both(kept_ref[:, :columns], two_ref[:, columns:]),
-        both(kept_ref[:, columns:], third_ref[...]),
+        both(kept_second_ref[...], two_ref[:, columns:]),
+        both(kept_third_ref[...], third_ref[...]),
     )
     for at, value in enumerate(pairs):
         first = pl.multiple_of(place_ref[1 + at], 128)
@@ -302,12 +306,12 @@
         grid_spec=pltpu.PrefetchScalarGridSpec(
             num_scalar_prefetch=1,
             grid=(tokens // tile,),
-            in_specs=[spec(part.shape[1]) for part in (own, kept, came_two, came_third)],
+            in_specs=[spec(part.shape[1]) for part in (own, *kept, came_two, came_third)],
             out_specs=spec(8 * columns),
         ),
         compiler_params=pltpu.CompilerParams(vmem_limit_bytes=16 * 2**20),
         cost_estimate=NO_COST,
-    )(place, own, kept, came_two, came_third)
+    )(place, own, *kept, came_two, came_third)
 
 
 def on_device(
@@ -437,18 +441,21 @@
     if chain:
         mine_first, across_first = group * share, (1 - group) * share
 
-        def halved(mine, across, first):
-            return [(mine, first + mine_first), (across, first + across_first)]
-
-        def quartered(mine, across, first):
+        def halved(mine, across, least, more=0):
+            return [
+                (mine, least + more + mine_first, least),
+                (across, least + more + across_first, least),
+            ]
+
+        def quartered(mine, across, least):
             quarters = []
             for at in range(2):
-                quarters += halved(mine[at], across[at], first + at * (share // 2))
+                quarters += halved(mine[at], across[at], least, at * (share // 2))
             return quarters
 
         parity = own_index % 2
-        own_blocks = [(block, parity * columns)]
-        own_blocks += halved(beside, beside_across, (1 - parity) * columns)
+        own_blocks = [(block, parity * columns, 0)]
+        own_blocks += halved(beside, beside_across, 0, (1 - parity) * columns)
         own_blocks += halved(near, near_across, 2 * columns)
         own_out = in_turn(project(own_rows, own_blocks))
         third, third_across = [], []
@@ -461,24 +468,21 @@
         third_inner[1] = in_turn(third_inner[1])
         third_outer += [lax.ppermute(third_inner[1], "req", outward)]
         third_part(0)
+        end_state = state([third[0]])
         third_part(1)
-        end_state = state([third[1]])
         second_across = in_turn(second_across)
+        kept = [in_turn(project(own_rows, halved(second, second_across, 0), [third[1]]))]
         third_across[0] = in_turn(third_across[0])
         theirs = held(theirs, second_across, third_across[0])
         theirs_other = in_turn(swapped(theirs, "tp", 1))
         their_rows = [(theirs, 0, first_unit), (theirs_other, 0, other_unit)]
         far_blocks = halved(near, near_across, 0) + halved(second, second_across, columns)
-        came_two = swapped(in_turn(project(their_rows, far_blocks, [end_state])), "req", 1)
+        came_two = swapped(in_turn(project(their_rows, far_blocks, kept)), "req", 1)
         third_across[1] = in_turn(third_across[1])
         third_blocks = quartered(third, third_across, 0)
         came_third = in_turn(project(their_rows, third_blocks))
         came_two = in_turn(came_two)
-        kept = project(
-            own_rows,
-            halved(second, second_across, 0) + quartered(third, third_across, columns),
-            [came_third],
-        )
+        kept += [project(own_rows, third_blocks, [came_third])]
         came_third = swapped(came_third, "req", 1)
         mixed_out = assemble(spot, even, own_out, kept, came_two, came_third)
     else:
@@ -489,7 +493,7 @@
         first_half = jnp.where(group == 0, mine, across)
         second_half = jnp.where(group == 0, across, mine)
         whole = jnp.concatenate([first_half, second_half], axis=1)
-        blocks = [(whole.reshape(line * columns, inner), 0)]
+        blocks = [(whole.reshape(line * columns, inner), 0, 0)]
         their_rows = [(theirs, 0, first_unit), (swapped(theirs, "tp", 1), 0, other_unit)]
         came = swapped(project(their_rows, blocks), "req", 1).reshape(tokens, line, columns)
         kept = project(own_rows, blocks).reshape(tokens, line, columns)

time: 255 us -> 251 us (0.984)
  waiting for transfers between devices: 112 us -> 99.4 us
  local copies, waits for them, and re-layouts: 23.7 us -> 28.6 us
  other arithmetic: 11 us -> 14.7 us
    ppermute x1, waiting for transfers between devices: 6.98 us -> 0.01 us  [on_device(): third_outer += [lax.ppermute(third_inner[1], 'req', outward)]]
    ppermute x12, waiting for transfers between devices: 56.3 us -> 51.7 us  [swapped(): return lax.ppermute(value, axis, pairs)]
    unnamed x61 -> x75, local copies, waits for them, and re-layouts: 12.6 us -> 16.7 us
    pallas_call x4 -> x5, Pallas kernels: 34.9 us -> 38.8 us  [project(): pl.pallas_call(lambda *refs: project_kernel(row_plan, block_plan, len(ear...]
    pallas_call x1, Pallas kernels: 9.64 us -> 6.66 us  [gate(): pl.pallas_call(lambda *refs: gate_kernel(pages, *refs), out_shape=jax.Sha...]
  transfers between devices with their start and end apart: 19 -> 19, of which waited for: 13 -> 11; matrix products, arithmetic and copies ran while one was open for 8% -> 10% of each run, Pallas kernels for 23% -> 25%
where the time goes in v4:
time: 251 us; the launch traced here: 249 us
  waiting for transfers between devices  99.4 us (40%)
  Pallas kernels  72.5 us (29%)
  starting transfers between devices  33.2 us (13%)
  local copies, waits for them, and re-layouts  28.6 us (11%)
  other arithmetic  14.7 us (6%)
    ppermute x12, waiting for transfers between devices, swapped(): return lax.ppermute(value, axis, pairs)  51.7 us
    pallas_call x5, Pallas kernels, project(): pl.pallas_call(lambda *refs: project_kernel(row_plan, block_plan, len(ear...  38.8 us
    ppermute x1, waiting for transfers between devices, on_device(): second_outer = lax.ppermute(second_inner, 'req', outward)  35.7 us
    unnamed x75, local copies, waits for them, and re-layouts  16.7 us
    ppermute x12, starting transfers between devices, swapped(): return lax.ppermute(value, axis, pairs)  11.7 us
    pallas_call x1, Pallas kernels, state_part(): pl.pallas_call(lambda *refs: state_kernel(heads, *refs), out_shape=out, g...  7.91 us
    ppermute x1, waiting for transfers between devices, on_device(): third_inner = [lax.ppermute(near_halves[0], 'req', middle)]  7.63 us
    pallas_call x3, Pallas kernels, pick(): pl.pallas_call(pick_kernel, out_shape=jax.ShapeDtypeStruct(yes.shape, yes...  7.33 us
  transfers between devices with their start and end apart: 19, of which 11 were waited for; matrix products, arithmetic and copies ran while one was open for 10% of the time, Pallas kernels for 25%

profile of v4, /device:TPU:16, one launch (start us, length us, event | category | flops | bytes accessed | tf_op | source)
XLA Modules:
  0.0 249.3 jit_solution(5419240755598193861)
XLA Ops:
  0.7 2.5 %dynamic-slice_bitcast_fusion = bf16[160,4096]{1,0:T(8,128)(2,1)} fusion(bf16[4096,1,320]{0,2,1:T(8,128)(2,1)} %param.29, s32[]{:T(128)S(6)} %select_n.52), kind=kLoop, calls=%fused_computation.2 | loop fusion | bytes 2621444 | tf_op jit(solution)/shard_map/dynamic_slice | solution.py:352
  3.2 1.6 collective-permute-start
  4.7 1.9 collective-permute-start.1
  6.7 1.6 collective-permute-start.2
  8.8 0.7 reduce.5
  10.2 2.0 multiply_convert_fusion
  12.1 2.8 %gather_fusion = bf16[128,64,256]{2,1,0:T(8,128)(2,1)} fusion(bf16[64,64,256]{2,1,0:T(8,128)(2,1)S(1)} %multiply_convert_fusion, s32[1024]{0:T(1024)S(1)} %pad_clamp_fusion), kind=kCustom, calls=%fused_computation | custom fusion | bytes 8389120 | tf_op jit(solution)/shard_map/gather | solution.py:377
  14.9 19.0 %collective-permute-done.refs_1_.in_ref.refs_6_.refs_3_ = bf16[160,4096]{1,0:T(8,128)(2,1)S(1)} collective-permute-done((bf16[160,4096]{1,0:T(8,128)(2,1)}, bf16[160,4096]{1,0:T(8,128)(2,1)S(1)}, u32[]{:S(2)}, u32[]{:S(2)}) %collective-permute-start) | collective-permute-done | bytes 1310752 | tf_op jit(solution)/shard_map/ppermute | solution.py:14
  33.9 3.3 %collective-permute-done.1.refs_2_.yes_ref = bf16[160,4096]{1,0:T(8,128)(2,1)} collective-permute-done((bf16[160,4096]{1,0:T(8,128)(2,1)}, bf16[160,4096]{1,0:T(8,128)(2,1)}, u32[]{:S(2)}, u32[]{:S(2)}) %collective-permute-start.1) | collective-permute-done | bytes 1310752 | tf_op jit(solution)/shard_map/ppermute | solution.py:363
  37.3 5.6 %all-to-all-start = ((bf16[128,64,256]{2,1,0:T(8,128)(2,1)}), bf16[128,64,256]{2,1,0:T(8,128)(2,1)}, u32[]{:S(2)}, u32[]{:S(2)}) async-start(bf16[128,64,256]{2,1,0:T(8,128)(2,1)} %shard_map.158.refs_10_), calls=%async_computation | async-start | bytes 8388608 | tf_op jit(solution)/shard_map/all_to_all | solution.py:386
  44.2 1.5 collective-permute-start.6
  45.7 4.5 %collective-permute-start.4 = (bf16[160,4096]{1,0:T(8,128)(2,1)}, bf16[160,4096]{1,0:T(8,128)(2,1)}, u32[]{:S(2)}, u32[]{:S(2)}) collective-permute-start(bf16[160,4096]{1,0:T(8,128)(2,1)} %collective-permute-done.1.refs_2_.yes_ref), channel_id=1, source_target_pairs={{4,0},{6,2},{8,12},{10,14},{5,1},{7,3},{9,13},{11,15},{20,16},{22,... | collective-permute-start | bytes 3932168 | tf_op jit(solution)/shard_map/ppermute | solution.py:412
  50.7 0.8 fusion.1.refs_9_
  52.0 1.1 reduce-window.6
  53.3 2.5 shard_map.159
  55.8 1.9 collective-permute-start.3
  57.7 1.5 broadcast_add_fusion
  59.1 1.6 copy.38
  60.7 1.7 exponential_multiply_fusion.1
  62.5 0.7 copy.39.refs_6_
  63.2 1.8 fusion.6
  65.0 1.7 copy.40.refs_7_
  66.7 1.6 copy-done.3
  68.3 1.6 copy-done.8
  69.9 0.9 copy-done.10
  70.8 0.9 copy-done.12
  71.8 0.9 copy-done.13
  72.7 0.9 copy-done.14
  73.7 0.8 copy-done.15
  74.4 0.8 copy-done.16
  75.2 6.5 %shard_map.160 = (f32[2,256,2048]{2,1,0:T(8,128)}, f32[2,256,2048]{2,1,0:T(8,128)}) custom-call(f32[16]{0:T(128)S(1)} %copy-done.18, bf16[2,256,2048]{2,1,0:T(8,128)(2,1)S(1)} %copy-done.3, bf16[2,256,2048]{2,1,0:T(8,128)(2,1)S(1)} %copy-done.8, bf16[2,256,256]{2,1,0:T(8,128)(2,1)S(1)} %copy-done.12, bf16[2,256,256]{2,1,0:T(8,128)(2,1)S(1)} %copy-done.10, ...), custom_call_target="tpu_custom_call" | custom-call | tf_op jit(solution)/shard_map/pallas_call | solution.py:80
  81.7 19.3 %collective-permute-done.5.refs_7_.refs_4_ = bf16[160,4096]{1,0:T(8,128)(2,1)S(1)} collective-permute-done((bf16[160,4096]{1,0:T(8,128)(2,1)}, bf16[160,4096]{1,0:T(8,128)(2,1)S(1)}, u32[]{:S(2)}, u32[]{:S(2)}) %collective-permute-start.5) | collective-permute-done | bytes 1310752 | tf_op jit(solution)/shard_map/ppermute | solution.py:14
  101.0 35.7 %collective-permute-done.4.no_ref = bf16[160,4096]{1,0:T(8,128)(2,1)} collective-permute-done((bf16[160,4096]{1,0:T(8,128)(2,1)}, bf16[160,4096]{1,0:T(8,128)(2,1)}, u32[]{:S(2)}, u32[]{:S(2)}) %collective-permute-start.4) | collective-permute-done | bytes 1310752 | tf_op jit(solution)/shard_map/ppermute | solution.py:412
  136.7 2.9 %shard_map.161.refs_8_.refs_3_.refs_5_ = bf16[160,4096]{1,0:T(8,128)(2,1)} custom-call(s32[1]{0:T(128)} %bitcast.17.flag_ref, bf16[160,4096]{1,0:T(8,128)(2,1)} %collective-permute-done.1.refs_2_.yes_ref, bf16[160,4096]{1,0:T(8,128)(2,1)} %collective-permute-done.4.no_ref), custom_call_target="tpu_custom_call" | custom-call | tf_op jit(solution)/shard_map/pallas_call | solution.py:239
  139.6 7.6 %collective-permute-done.3.refs_5_.yes_ref = bf16[80,4096]{1,0:T(8,128)(2,1)S(1)} collective-permute-done((bf16[80,4096]{1,0:T(8,128)(2,1)}, bf16[80,4096]{1,0:T(8,128)(2,1)S(1)}, u32[]{:S(2)}, u32[]{:S(2)}) %collective-permute-start.3) | collective-permute-done | bytes 655392 | tf_op jit(solution)/shard_map/ppermute | solution.py:383
  147.3 1.5 copy-done
  148.8 0.9 copy-done.11
  149.8 6.7 %shard_map.162.refs_1_ = bf16[512,2048]{1,0:T(8,128)(2,1)} custom-call(s32[64]{0:T(128)S(1)} %multiply_add_fusion.refs_0_, bf16[128,64,256]{2,1,0:T(8,128)(2,1)} %all-to-all-done.refs_1_.refs_2_, bf16[2,256,256]{2,1,0:T(8,128)(2,1)S(1)} %copy-done.11, f32[2,256,2048]{2,1,0:T(8,128)} %get-tuple-element.40.refs_3_, f32[2,256,2048]{2,1,0:T(8,128)} %get-tuple-element.47.refs_4_, ...), custom_call_target="tpu_custom_call" | custom-call | tf_op jit(solution)/shard_map/pallas_call | solution.py:150
  157.1 3.4 %collective-permute-start.9 = (bf16[80,4096]{1,0:T(8,128)(2,1)}, bf16[80,4096]{1,0:T(8,128)(2,1)}, u32[]{:S(2)}, u32[]{:S(2)}) collective-permute-start(bf16[80,4096]{1,0:T(8,128)(2,1)} %shard_map.164), channel_id=1, source_target_pairs={{4,8},{8,4},{6,10},{10,6},{5,9},{9,5},{7,11},{11,7},{20,24},{24,20... | collective-permute-start | bytes 1966088 | tf_op jit(solution)/shard_map/ppermute | solution.py:432
  160.5 1.6 collective-permute-start.8
  162.1 2.1 collective-permute-start.11
  164.8 10.3 %shard_map.163.own_ref = bf16[512,960]{1,0:T(8,128)(2,1)} custom-call(s32[7]{0:T(128)} %stack.103.refs_0_, bf16[512,2048]{1,0:T(8,128)(2,1)} %shard_map.162.refs_1_, bf16[512,2048]{1,0:T(8,128)(2,1)} %collective-permute-done.7.refs_2_, bf16[320,4096]{1,0:T(8,128)(2,1)} %bitcast.47, bf16[160,4096]{1,0:T(8,128)(2,1)} %collective-permute-done.2.refs_3_.refs_4_, ...), custom_call_target="tpu_custom_call" | custom-call | tf_op jit(solution)/shard_map/pallas_call | solution.py:213
  175.1 1.0 collective-permute-done.9.yes_ref
  176.1 2.1 collective-permute-start.10
  178.3 2.2 shard_map.165.refs_6_.refs_3_
  180.5 1.5 collective-permute-start.12
  183.3 1.9 exponential_multiply_fusion.refs_5_
  185.1 7.9 %shard_map.166 = bf16[2,2048,256]{2,1,0:T(8,128)(2,1)} custom-call(s32[64]{0:T(128)} %copy-done.17, f32[2,16]{1,0:T(2,128)} %exponential_multiply_fusion.2.refs_1_, bf16[128,64,256]{2,1,0:T(8,128)(2,1)} %all-to-all-done.refs_1_.refs_2_, bf16[2,256,2048]{2,1,0:T(8,128)(2,1)} %refs_3_.3, bf16[2,256,256]{2,1,0:T(8,128)(2,1)} %refs_4_.3, ...), custom_call_target="tpu_custom_call" | custom-call | tf_op jit(solution)/shard_map/pallas_call | solution.py:117
  193.1 2.2 shard_map.167.refs_5_
  195.3 1.1 copy-done.20
  196.3 6.7 %shard_map.168.refs_7_.kept_second_ref = bf16[512,320]{1,0:T(8,128)(2,1)} custom-call(s32[4]{0:T(128)} %pad_add_fusion.refs_0_, bf16[512,2048]{1,0:T(8,128)(2,1)} %shard_map.162.refs_1_, bf16[512,2048]{1,0:T(8,128)(2,1)} %collective-permute-done.7.refs_2_, bf16[160,4096]{1,0:T(8,128)(2,1)} %shard_map.161.refs_8_.refs_3_.refs_5_, ...), custom_call_target="tpu_custom_call" | custom-call | tf_op jit(solution)/shard_map/pallas_call | solution.py:213
  203.1 2.1 collective-permute-done.12.refs_2_.refs_4_
  205.2 0.8 copy-done.23
  206.0 1.5 collective-permute-start.13
  208.2 2.2 collective-permute-done.15.refs_2_
  210.4 1.4 copy-done.22
  211.8 8.1 %shard_map.170 = bf16[512,640]{1,0:T(8,128)(2,1)} custom-call(s32[6]{0:T(128)} %stack.112.refs_0_, bf16[512,2048]{1,0:T(8,128)(2,1)} %shard_map.169.refs_1_, bf16[512,2048]{1,0:T(8,128)(2,1)} %copy-done.22, bf16[160,4096]{1,0:T(8,128)(2,1)} %copy-done.19, bf16[160,4096]{1,0:T(8,128)(2,1)} %copy-done.2, bf16[160,4096]{1,0:T(8,128)(2,1)} %shard_map.161.refs_8_.refs_3_.refs_5_, ...), custom_call_target="tpu_custom_call" | custom-call | tf_op jit(solution)/shard_map/pallas_call | solution.py:213
  221.2 2.0 collective-permute-done.13.refs_6_
  223.2 0.8 copy-done.25
  224.0 6.7 %shard_map.171.refs_7_ = bf16[512,320]{1,0:T(8,128)(2,1)} custom-call(s32[6]{0:T(128)} %stack.109.refs_0_, bf16[512,2048]{1,0:T(8,128)(2,1)} %shard_map.169.refs_1_, bf16[512,2048]{1,0:T(8,128)(2,1)} %copy-done.22, bf16[80,4096]{1,0:T(8,128)(2,1)} %shard_map.165.refs_6_.refs_3_, bf16[80,4096]{1,0:T(8,128)(2,1)} %copy-done.23, ...), custom_call_target="tpu_custom_call" | custom-call | tf_op jit(solution)/shard_map/pallas_call | solution.py:213
  231.5 6.9 %shard_map.172.kept_third_ref = bf16[512,320]{1,0:T(8,128)(2,1)} custom-call(s32[6]{0:T(128)} %stack.109.refs_0_, bf16[512,2048]{1,0:T(8,128)(2,1)} %shard_map.162.refs_1_, bf16[512,2048]{1,0:T(8,128)(2,1)} %collective-permute-done.7.refs_2_, bf16[80,4096]{1,0:T(8,128)(2,1)} %shard_map.165.refs_6_.refs_3_, bf16[80,4096]{1,0:T(8,128)(2,1)} %copy-done.23, ...), custom_call_target="tpu_custom_call" | custom-call | tf_op jit(solution)/shard_map/pallas_call | solution.py:213
  238.4 7.0 %collective-permute-done.17.third_ref = bf16[512,320]{1,0:T(8,128)(2,1)S(1)} collective-permute-done((bf16[512,320]{1,0:T(8,128)(2,1)}, bf16[512,320]{1,0:T(8,128)(2,1)S(1)}, u32[]{:S(2)}, u32[]{:S(2)}) %collective-permute-start.17) | collective-permute-done | bytes 327712 | tf_op jit(solution)/shard_map/ppermute | solution.py:14
  245.4 1.0 copy-done.9
  246.4 2.9 %shard_map.173 = bf16[512,2560]{1,0:T(8,128)(2,1)} custom-call(s32[5]{0:T(128)S(1)} %stack.95.place_ref, bf16[512,960]{1,0:T(8,128)(2,1)S(1)} %copy-done.5, bf16[512,320]{1,0:T(8,128)(2,1)S(1)} %copy-done.6, bf16[512,320]{1,0:T(8,128)(2,1)S(1)} %copy-done.9, bf16[512,640]{1,0:T(8,128)(2,1)S(1)} %collective-permute-done.16.two_ref, ...), custom_call_target="tpu_custom_call" | custom-call | tf_op jit(solution)/shard_map/pallas_call | solution.py:303
  (107 shorter events, 9.1 us)
Async XLA Ops:
  0.6 8.1 %copy-start.30 = (s32[1,16,32,1]{2,3,1,0:T(1,128)S(1)}, s32[1,16,32,1]{2,3,1,0:T(1,128)}, u32[]{:S(2)}) copy-start(s32[1,16,32,1]{2,3,1,0:T(1,128)} %param.25) | copy-start | bytes 6148
  0.6 9.1 %copy-start.29 = (s32[1,16,32]{2,1,0:T(8,128)S(1)}, s32[1,16,32]{2,1,0:T(8,128)}, u32[]{:S(2)}) copy-start(s32[1,16,32]{2,1,0:T(8,128)} %param.26) | copy-start | bytes 6148
  0.7 9.5 %copy-start.28 = (bf16[64,64]{1,0:T(8,128)(2,1)S(1)}, bf16[64,64]{1,0:T(8,128)(2,1)}, u32[]{:S(2)}) copy-start(bf16[64,64]{1,0:T(8,128)(2,1)} %param.24) | copy-start | bytes 24580
  3.2 30.7 %collective-permute-start = (bf16[160,4096]{1,0:T(8,128)(2,1)}, bf16[160,4096]{1,0:T(8,128)(2,1)S(1)}, u32[]{:S(2)}, u32[]{:S(2)}) collective-permute-start(bf16[160,4096]{1,0:T(8,128)(2,1)} %dynamic-slice_bitcast_fusion), channel_id=1, source_target_pairs={{0,4},{2,6},{4,0},{6,2},{8,12},{10,14},{12,8},{14,10},{1,5},{3,7},... | collective-permute-start | bytes 3932168 | tf_op jit(solution)/shard_map/ppermute | solution.py:14
  4.7 32.4 %collective-permute-start.1 = (bf16[160,4096]{1,0:T(8,128)(2,1)}, bf16[160,4096]{1,0:T(8,128)(2,1)}, u32[]{:S(2)}, u32[]{:S(2)}) collective-permute-start(bf16[160,4096]{1,0:T(8,128)(2,1)} %dynamic-slice_bitcast_fusion), channel_id=1, source_target_pairs={{4,8},{8,4},{6,10},{10,6},{5,9},{9,5},{7,11},{11,7},{20,24},{24,20... | collective-permute-start | bytes 3932168 | tf_op jit(solution)/shard_map/ppermute | solution.py:363
  6.7 30.6 %collective-permute-start.2 = (bf16[160,4096]{1,0:T(8,128)(2,1)}, bf16[160,4096]{1,0:T(8,128)(2,1)}, u32[]{:S(2)}, u32[]{:S(2)}) collective-permute-start(bf16[160,4096]{1,0:T(8,128)(2,1)} %dynamic-slice_bitcast_fusion), channel_id=1, source_target_pairs={{0,2},{2,0},{4,6},{6,4},{8,10},{10,8},{12,14},{14,12},{1,3},{3,1},... | collective-permute-start | bytes 3932168 | tf_op jit(solution)/shard_map/ppermute | solution.py:14
  33.9 3.4 %copy-start.19 = (bf16[160,4096]{1,0:T(8,128)(2,1)}, bf16[160,4096]{1,0:T(8,128)(2,1)S(1)}, u32[]{:S(2)}) copy-start(bf16[160,4096]{1,0:T(8,128)(2,1)S(1)} %collective-permute-done.refs_1_.in_ref.refs_6_.refs_3_) | copy-start | bytes 3932164
  37.3 5.7 %copy-start.35 = (s32[2]{0:T(128)S(1)}, s32[2]{0:T(128)}, u32[]{:S(2)}) copy-start(s32[2]{0:T(128)} %param.27) | copy-start | bytes 28
  37.3 6.3 %copy-start.36 = (f32[16]{0:T(128)S(1)}, f32[16]{0:T(128)}, u32[]{:S(2)}) copy-start(f32[16]{0:T(128)} %param.21) | copy-start | bytes 196
  37.3 6.8 %copy-start.33 = (s32[2]{0:T(128)S(1)}, s32[2]{0:T(128)}, u32[]{:S(2)}) copy-start(s32[2]{0:T(128)} %param.28) | copy-start | bytes 28
  37.3 14.2 %copy-start.27 = (f32[2,256,16]{1,2,0:T(8,128)S(1)}, f32[2,256,16]{1,2,0:T(8,128)}, u32[]{:S(2)}) copy-start(f32[2,256,16]{1,2,0:T(8,128)} %param.19) | copy-start | bytes 98308
  37.3 14.3 %copy-start.31 = (f32[16]{0:T(128)S(1)}, f32[16]{0:T(128)}, u32[]{:S(2)}) copy-start(f32[16]{0:T(128)} %param.20) | copy-start | bytes 196
  37.3 109.9 %all-to-all-start = ((bf16[128,64,256]{2,1,0:T(8,128)(2,1)}), bf16[128,64,256]{2,1,0:T(8,128)(2,1)}, u32[]{:S(2)}, u32[]{:S(2)}) async-start(bf16[128,64,256]{2,1,0:T(8,128)(2,1)} %shard_map.158.refs_10_), calls=%async_computation | async-start | bytes 8388608 | tf_op jit(solution)/shard_map/all_to_all | solution.py:386
  44.2 37.5 %collective-permute-start.6 = (bf16[160,4096]{1,0:T(8,128)(2,1)}, bf16[160,4096]{1,0:T(8,128)(2,1)S(1)}, u32[]{:S(2)}, u32[]{:S(2)}) collective-permute-start(bf16[160,4096]{1,0:T(8,128)(2,1)} %collective-permute-done.2.refs_3_.refs_4_), channel_id=1, source_target_pairs={{0,16},{16,0},{1,17},{17,1},{2,18},{18,2},{3,19},{19,3},{4,20},{20... | collective-permute-start | bytes 3932168 | tf_op jit(solution)/shard_map/ppermute | solution.py:14
  45.7 91.0 %collective-permute-start.4 = (bf16[160,4096]{1,0:T(8,128)(2,1)}, bf16[160,4096]{1,0:T(8,128)(2,1)}, u32[]{:S(2)}, u32[]{:S(2)}) collective-permute-start(bf16[160,4096]{1,0:T(8,128)(2,1)} %collective-permute-done.1.refs_2_.yes_ref), channel_id=1, source_target_pairs={{4,0},{6,2},{8,12},{10,14},{5,1},{7,3},{9,13},{11,15},{20,16},{22,... | collective-permute-start | bytes 3932168 | tf_op jit(solution)/shard_map/ppermute | solution.py:412
  50.2 50.8 %collective-permute-start.5 = (bf16[160,4096]{1,0:T(8,128)(2,1)}, bf16[160,4096]{1,0:T(8,128)(2,1)S(1)}, u32[]{:S(2)}, u32[]{:S(2)}) collective-permute-start(bf16[160,4096]{1,0:T(8,128)(2,1)} %copy-done.19), channel_id=1, source_target_pairs={{0,16},{16,0},{1,17},{17,1},{2,18},{18,2},{3,19},{19,3},{4,20},{20... | collective-permute-start | bytes 3932168 | tf_op jit(solution)/shard_map/ppermute | solution.py:14
  50.7 96.5 %copy-start.17 = (s32[64]{0:T(128)}, s32[64]{0:T(128)S(1)}, u32[]{:S(2)}) copy-start(s32[64]{0:T(128)S(1)} %multiply_add_fusion.refs_0_) | copy-start | bytes 772
  51.7 7.5 %copy-start.24 = (f32[2,256,16]{2,1,0:T(8,128)}, f32[2,256,16]{2,1,0:T(8,128)S(1)}, u32[]{:S(2)}) copy-start(f32[2,256,16]{2,1,0:T(8,128)S(1)} %copy.35) | copy-start | bytes 98308
  51.8 14.8 %copy-start.18 = (f32[16]{0:T(128)S(1)}, f32[16]{0:T(128)}, u32[]{:S(2)}) copy-start(f32[16]{0:T(128)} %refs_0_.1) | copy-start | bytes 196
  53.1 2.7 %copy-start.26 = (f32[2,16,2,128]{3,1,2,0:T(8,128)}, f32[2,16,2,128]{3,1,2,0:T(8,128)S(1)}, u32[]{:S(2)}) copy-start(f32[2,16,2,128]{3,1,2,0:T(8,128)S(1)} %reduce-window.6) | copy-start | bytes 98308
  55.8 91.5 %collective-permute-start.3 = (bf16[80,4096]{1,0:T(8,128)(2,1)}, bf16[80,4096]{1,0:T(8,128)(2,1)S(1)}, u32[]{:S(2)}, u32[]{:S(2)}) collective-permute-start(bf16[80,4096]{1,0:T(8,128)(2,1)} %get-tuple-element.37), channel_id=1, source_target_pairs={{4,8},{8,4},{6,10},{10,6},{5,9},{9,5},{7,11},{11,7},{20,24},{24,20... | collective-permute-start | bytes 1966088 | tf_op jit(solution)/shard_map/ppermute | solution.py:383
  66.7 1.6 copy-start.3
  68.3 1.6 copy-start.8
  69.9 0.9 copy-start.10
  70.8 0.9 copy-start.12
  71.8 0.9 copy-start.13
  72.7 0.9 copy-start.14
  73.7 0.8 copy-start.15
  74.4 0.8 copy-start.16
  81.7 65.6 %copy-start.4 = (bf16[160,4096]{1,0:T(8,128)(2,1)}, bf16[160,4096]{1,0:T(8,128)(2,1)S(1)}, u32[]{:S(2)}) copy-start(bf16[160,4096]{1,0:T(8,128)(2,1)S(1)} %collective-permute-done.6.refs_6_.refs_5_) | copy-start | bytes 3932164
  101.0 55.4 %copy-start.2 = (bf16[160,4096]{1,0:T(8,128)(2,1)}, bf16[160,4096]{1,0:T(8,128)(2,1)S(1)}, u32[]{:S(2)}) copy-start(bf16[160,4096]{1,0:T(8,128)(2,1)S(1)} %collective-permute-done.5.refs_7_.refs_4_) | copy-start | bytes 3932164
  147.2 14.8 %copy-start.7 = (bf16[80,4096]{1,0:T(8,128)(2,1)}, bf16[80,4096]{1,0:T(8,128)(2,1)S(1)}, u32[]{:S(2)}) copy-start(bf16[80,4096]{1,0:T(8,128)(2,1)S(1)} %collective-permute-done.3.refs_5_.yes_ref) | copy-start | bytes 1966084
  147.3 1.6 copy-start
  148.8 0.9 copy-start.11
  156.4 4.1 %copy-start.1 = (bf16[160,4096]{1,0:T(8,128)(2,1)S(1)}, bf16[160,4096]{1,0:T(8,128)(2,1)}, u32[]{:S(2)}) copy-start(bf16[160,4096]{1,0:T(8,128)(2,1)} %shard_map.161.refs_8_.refs_3_.refs_5_) | copy-start | bytes 3932164
  156.4 8.4 %collective-permute-start.7 = (bf16[512,2048]{1,0:T(8,128)(2,1)}, bf16[512,2048]{1,0:T(8,128)(2,1)}, u32[]{:S(2)}, u32[]{:S(2)}) collective-permute-start(bf16[512,2048]{1,0:T(8,128)(2,1)} %shard_map.162.refs_1_), channel_id=1, source_target_pairs={{0,1},{1,0},{2,3},{3,2},{4,5},{5,4},{6,7},{7,6},{8,9},{9,8},{10,11... | collective-permute-start | bytes 6291464 | tf_op jit(solution)/shard_map/ppermute | solution.py:14
  156.5 48.7 %collective-permute-start.14 = (bf16[512,2048]{1,0:T(8,128)(2,1)}, bf16[512,2048]{1,0:T(8,128)(2,1)}, u32[]{:S(2)}, u32[]{:S(2)}) collective-permute-start(bf16[512,2048]{1,0:T(8,128)(2,1)} %shard_map.162.refs_1_), channel_id=1, source_target_pairs={{0,2},{2,0},{4,6},{6,4},{8,10},{10,8},{12,14},{14,12},{1,3},{3,1},... | collective-permute-start | bytes 6291464 | tf_op jit(solution)/shard_map/ppermute | solution.py:14
  157.1 19.0 %collective-permute-start.9 = (bf16[80,4096]{1,0:T(8,128)(2,1)}, bf16[80,4096]{1,0:T(8,128)(2,1)}, u32[]{:S(2)}, u32[]{:S(2)}) collective-permute-start(bf16[80,4096]{1,0:T(8,128)(2,1)} %shard_map.164), channel_id=1, source_target_pairs={{4,8},{8,4},{6,10},{10,6},{5,9},{9,5},{7,11},{11,7},{20,24},{24,20... | collective-permute-start | bytes 1966088 | tf_op jit(solution)/shard_map/ppermute | solution.py:432
  160.5 34.7 %collective-permute-start.8 = (bf16[160,4096]{1,0:T(8,128)(2,1)S(1)}, bf16[160,4096]{1,0:T(8,128)(2,1)S(1)}, u32[]{:S(2)}, u32[]{:S(2)}) collective-permute-start(bf16[160,4096]{1,0:T(8,128)(2,1)S(1)} %copy-done.1), channel_id=1, source_target_pairs={{0,16},{16,0},{1,17},{17,1},{2,18},{18,2},{3,19},{19,3},{4,20},{20... | collective-permute-start | bytes 3932168 | tf_op jit(solution)/shard_map/ppermute | solution.py:14
  162.1 16.2 %collective-permute-start.11 = (bf16[80,4096]{1,0:T(8,128)(2,1)S(1)}, bf16[80,4096]{1,0:T(8,128)(2,1)}, u32[]{:S(2)}, u32[]{:S(2)}) collective-permute-start(bf16[80,4096]{1,0:T(8,128)(2,1)S(1)} %collective-permute-done.3.refs_5_.yes_ref), channel_id=1, source_target_pairs={{4,0},{6,2},{8,12},{10,14},{5,1},{7,3},{9,13},{11,15},{20,16},{22,... | collective-permute-start | bytes 1966088 | tf_op jit(solution)/shard_map/ppermute | solution.py:420
  164.8 17.8 %copy-start.34 = (f32[2]{0:T(128)S(1)}, f32[2]{0:T(128)}, u32[]{:S(2)}) copy-start(f32[2]{0:T(128)} %compare_convert_fusion.1) | copy-start | bytes 28
  164.8 18.4 %copy-start.32 = (f32[16]{0:T(128)S(1)}, f32[16]{0:T(128)}, u32[]{:S(2)}) copy-start(f32[16]{0:T(128)} %param.20) | copy-start | bytes 196
  176.1 16.9 %collective-permute-start.10 = (bf16[80,4096]{1,0:T(8,128)(2,1)}, bf16[80,4096]{1,0:T(8,128)(2,1)}, u32[]{:S(2)}, u32[]{:S(2)}) collective-permute-start(bf16[80,4096]{1,0:T(8,128)(2,1)} %collective-permute-done.9.yes_ref), channel_id=1, source_target_pairs={{4,0},{6,2},{8,12},{10,14},{5,1},{7,3},{9,13},{11,15},{20,16},{22,... | collective-permute-start | bytes 1966088 | tf_op jit(solution)/shard_map/ppermute | solution.py:469
  180.5 24.7 %collective-permute-start.12 = (bf16[80,4096]{1,0:T(8,128)(2,1)}, bf16[80,4096]{1,0:T(8,128)(2,1)S(1)}, u32[]{:S(2)}, u32[]{:S(2)}) collective-permute-start(bf16[80,4096]{1,0:T(8,128)(2,1)} %shard_map.165.refs_6_.refs_3_), channel_id=1, source_target_pairs={{0,16},{16,0},{1,17},{17,1},{2,18},{18,2},{3,19},{19,3},{4,20},{20... | collective-permute-start | bytes 1966088 | tf_op jit(solution)/shard_map/ppermute | solution.py:14
  195.3 1.1 copy-start.20
  203.1 3.0 %copy-start.21 = (bf16[80,4096]{1,0:T(8,128)(2,1)S(1)}, bf16[80,4096]{1,0:T(8,128)(2,1)}, u32[]{:S(2)}) copy-start(bf16[80,4096]{1,0:T(8,128)(2,1)} %shard_map.167.refs_5_) | copy-start | bytes 1966084
  205.2 0.8 copy-start.23
  206.0 4.4 %collective-permute-start.15 = (bf16[512,2048]{1,0:T(8,128)(2,1)}, bf16[512,2048]{1,0:T(8,128)(2,1)S(1)}, u32[]{:S(2)}, u32[]{:S(2)}) collective-permute-start(bf16[512,2048]{1,0:T(8,128)(2,1)} %shard_map.169.refs_1_), channel_id=1, source_target_pairs={{0,1},{1,0},{2,3},{3,2},{4,5},{5,4},{6,7},{7,6},{8,9},{9,8},{10,11... | collective-permute-start | bytes 6291464 | tf_op jit(solution)/shard_map/ppermute | solution.py:14
  206.0 17.1 %collective-permute-start.13 = (bf16[80,4096]{1,0:T(8,128)(2,1)S(1)}, bf16[80,4096]{1,0:T(8,128)(2,1)S(1)}, u32[]{:S(2)}, u32[]{:S(2)}) collective-permute-start(bf16[80,4096]{1,0:T(8,128)(2,1)S(1)} %copy-done.21), channel_id=1, source_target_pairs={{0,16},{16,0},{1,17},{17,1},{2,18},{18,2},{3,19},{19,3},{4,20},{20... | collective-permute-start | bytes 1966088 | tf_op jit(solution)/shard_map/ppermute | solution.py:14
  210.4 1.4 copy-start.22
  219.9 18.5 %collective-permute-start.16 = (bf16[512,640]{1,0:T(8,128)(2,1)}, bf16[512,640]{1,0:T(8,128)(2,1)S(1)}, u32[]{:S(2)}, u32[]{:S(2)}) collective-permute-start(bf16[512,640]{1,0:T(8,128)(2,1)} %shard_map.170), channel_id=1, source_target_pairs={{0,2},{2,0},{4,6},{6,4},{8,10},{10,8},{12,14},{14,12},{1,3},{3,1},... | collective-permute-start | bytes 1966088 | tf_op jit(solution)/shard_map/ppermute | solution.py:14
  223.2 0.8 copy-start.25
  230.8 14.6 %collective-permute-start.17 = (bf16[512,320]{1,0:T(8,128)(2,1)}, bf16[512,320]{1,0:T(8,128)(2,1)S(1)}, u32[]{:S(2)}, u32[]{:S(2)}) collective-permute-start(bf16[512,320]{1,0:T(8,128)(2,1)} %shard_map.171.refs_7_), channel_id=1, source_target_pairs={{0,2},{2,0},{4,6},{6,4},{8,10},{10,8},{12,14},{14,12},{1,3},{3,1},... | collective-permute-start | bytes 983048 | tf_op jit(solution)/shard_map/ppermute | solution.py:14
  231.5 13.9 %copy-start.5 = (bf16[512,960]{1,0:T(8,128)(2,1)S(1)}, bf16[512,960]{1,0:T(8,128)(2,1)}, u32[]{:S(2)}) copy-start(bf16[512,960]{1,0:T(8,128)(2,1)} %shard_map.163.own_ref) | copy-start | bytes 2949124
  231.5 13.9 %copy-start.6 = (bf16[512,320]{1,0:T(8,128)(2,1)S(1)}, bf16[512,320]{1,0:T(8,128)(2,1)}, u32[]{:S(2)}) copy-start(bf16[512,320]{1,0:T(8,128)(2,1)} %shard_map.168.refs_7_.kept_second_ref) | copy-start | bytes 983044
  245.4 1.0 copy-start.9

commit v5 on v4

--- a/solution.py
+++ b/solution.py
@@ -85,7 +85,7 @@
         + [one(array) for array in operands]
         + [ANYWHERE] * len(earlier),
         out_specs=[one(out), one(out)],
-        compiler_params=pltpu.CompilerParams(vmem_limit_bytes=48 * 2**20),
+        compiler_params=pltpu.CompilerParams(vmem_limit_bytes=63 * 2**20),
         cost_estimate=NO_COST,
     )(d_skip, *operands, *earlier)
 
@@ -124,7 +124,7 @@
             + [ANYWHERE] * len(earlier),
             out_specs=one(out),
         ),
-        compiler_params=pltpu.CompilerParams(vmem_limit_bytes=60 * 2**20),
+        compiler_params=pltpu.CompilerParams(vmem_limit_bytes=63 * 2**20),
         cost_estimate=NO_COST,
     )(where_from, kept_share, got_pages, x_inputs, b_proj, weight, *earlier)
 
@@ -164,7 +164,7 @@
             + [ANYWHERE] * len(earlier),
             out_specs=pl.BlockSpec((slots, wide), lambda request, step, where_ref: (request, step)),
         ),
-        compiler_params=pltpu.CompilerParams(vmem_limit_bytes=48 * 2**20),
+        compiler_params=pltpu.CompilerParams(vmem_limit_bytes=63 * 2**20),
         cost_estimate=NO_COST,
     )(where_from, got_pages, c_proj, local, factor, *earlier)
 
@@ -224,7 +224,7 @@
                 pltpu.SemaphoreType.DMA((len(rows) + len(blocks),)),
             ],
         ),
-        compiler_params=pltpu.CompilerParams(vmem_limit_bytes=60 * 2**20),
+        compiler_params=pltpu.CompilerParams(vmem_limit_bytes=63 * 2**20),
         cost_estimate=NO_COST,
     )(place, *[array for array, _, _ in rows], *[array for array, _, _ in blocks], *earlier)
 
@@ -292,7 +292,7 @@
 def assemble(spot, even, own, kept, came_two, came_third):
     tokens = own.shape[0]
     columns = came_third.shape[1]
-    tile = min(128, tokens)
+    tile = min(256, tokens)
 
     def spec(width):
         return pl.BlockSpec((tile, width), lambda step, place_ref: (step, 0))
@@ -309,7 +309,7 @@
             in_specs=[spec(part.shape[1]) for part in (own, *kept, came_two, came_third)],
             out_specs=spec(8 * columns),
         ),
-        compiler_params=pltpu.CompilerParams(vmem_limit_bytes=16 * 2**20),
+        compiler_params=pltpu.CompilerParams(vmem_limit_bytes=63 * 2**20),
         cost_estimate=NO_COST,
     )(place, own, *kept, came_two, came_third)
 

time: 251 us -> 246 us (0.980)
  local copies, waits for them, and re-layouts: 28.6 us -> 10.1 us
  waiting for transfers between devices: 99.4 us -> 116 us
  other arithmetic: 14.7 us -> 9.2 us
    ppermute x12, waiting for transfers between devices: 51.7 us -> 67.7 us  [swapped(): return lax.ppermute(value, axis, pairs)]
    unnamed x75 -> x25, local copies, waits for them, and re-layouts: 16.7 us -> 1.32 us
  transfers between devices with their start and end apart: 19 -> 19, of which waited for: 11 -> 12; matrix products, arithmetic and copies ran while one was open for 10% -> 7% of each run, Pallas kernels for 25% -> 26%
where the time goes in v5:
time: 246 us; the launch traced here: 245 us
  waiting for transfers between devices  116 us (47%)
  Pallas kernels  74.8 us (30%)
  starting transfers between devices  33.3 us (14%)
  local copies, waits for them, and re-layouts  10.1 us (4%)
  other arithmetic  9.2 us (4%)
    ppermute x12, waiting for transfers between devices, swapped(): return lax.ppermute(value, axis, pairs)  67.7 us
    pallas_call x5, Pallas kernels, project(): pl.pallas_call(lambda *refs: project_kernel(row_plan, block_plan, len(ear...  38.7 us
    ppermute x1, waiting for transfers between devices, on_device(): second_outer = lax.ppermute(second_inner, 'req', outward)  36.7 us
    ppermute x12, starting transfers between devices, swapped(): return lax.ppermute(value, axis, pairs)  11.7 us
    pallas_call x1, Pallas kernels, state_part(): pl.pallas_call(lambda *refs: state_kernel(heads, *refs), out_shape=out, g...  7.91 us
    ppermute x1, waiting for transfers between devices, on_device(): third_inner = [lax.ppermute(near_halves[0], 'req', middle)]  7.75 us
    pallas_call x1, Pallas kernels, local_part(): pl.pallas_call(lambda *refs: local_kernel(heads, *refs), out_shape=[out,...  7.72 us
    pallas_call x3, Pallas kernels, pick(): pl.pallas_call(pick_kernel, out_shape=jax.ShapeDtypeStruct(yes.shape, yes...  7.31 us
  transfers between devices with their start and end apart: 19, of which 12 were waited for; matrix products, arithmetic and copies ran while one was open for 7% of the time, Pallas kernels for 26%

profile of v5, /device:TPU:16, one launch (start us, length us, event | category | flops | bytes accessed | tf_op | source)
XLA Modules:
  0.0 244.7 jit_solution(2372970772969620500)
XLA Ops:
  0.7 1.4 dynamic-slice_bitcast_fusion
  2.1 1.6 collective-permute-start
  3.7 1.9 collective-permute-start.1
  5.6 1.6 collective-permute-start.2
  7.2 0.5 broadcast.86
  7.7 0.7 reduce.5
  8.5 0.2 reduce_window_sum.26
  8.8 0.2 select_reduce_fusion
  9.1 2.0 multiply_convert_fusion
  11.1 2.7 %gather_fusion = bf16[128,64,256]{2,1,0:T(8,128)(2,1)} fusion(bf16[64,64,256]{2,1,0:T(8,128)(2,1)S(1)} %multiply_convert_fusion, s32[1024]{0:T(1024)S(1)} %pad_clamp_fusion), kind=kCustom, calls=%fused_computation | custom fusion | bytes 8389120 | tf_op jit(solution)/shard_map/gather | solution.py:377
  13.8 18.9 %collective-permute-done.refs_1_.in_ref.refs_6_.refs_3_ = bf16[160,4096]{1,0:T(8,128)(2,1)} collective-permute-done((bf16[160,4096]{1,0:T(8,128)(2,1)S(1)}, bf16[160,4096]{1,0:T(8,128)(2,1)}, u32[]{:S(2)}, u32[]{:S(2)}) %collective-permute-start) | collective-permute-done | bytes 1310752 | tf_op jit(solution)/shard_map/ppermute | solution.py:14
  32.8 3.2 %collective-permute-done.1.refs_2_.yes_ref = bf16[160,4096]{1,0:T(8,128)(2,1)} collective-permute-done((bf16[160,4096]{1,0:T(8,128)(2,1)S(1)}, bf16[160,4096]{1,0:T(8,128)(2,1)}, u32[]{:S(2)}, u32[]{:S(2)}) %collective-permute-start.1) | collective-permute-done | bytes 1310752 | tf_op jit(solution)/shard_map/ppermute | solution.py:363
  36.1 5.6 %all-to-all-start = ((bf16[128,64,256]{2,1,0:T(8,128)(2,1)}), bf16[128,64,256]{2,1,0:T(8,128)(2,1)}, u32[]{:S(2)}, u32[]{:S(2)}) async-start(bf16[128,64,256]{2,1,0:T(8,128)(2,1)} %shard_map.158.refs_10_), calls=%async_computation | async-start | bytes 8388608 | tf_op jit(solution)/shard_map/all_to_all | solution.py:386
  41.9 1.5 collective-permute-start.6
  43.4 4.5 %collective-permute-start.4 = (bf16[160,4096]{1,0:T(8,128)(2,1)}, bf16[160,4096]{1,0:T(8,128)(2,1)}, u32[]{:S(2)}, u32[]{:S(2)}) collective-permute-start(bf16[160,4096]{1,0:T(8,128)(2,1)} %collective-permute-done.1.refs_2_.yes_ref), channel_id=1, source_target_pairs={{4,0},{6,2},{8,12},{10,14},{5,1},{7,3},{9,13},{11,15},{20,16},{22,... | collective-permute-start | bytes 3932168 | tf_op jit(solution)/shard_map/ppermute | solution.py:412
  47.9 0.6 collective-permute-start.5
  48.4 0.6 multiply_add_fusion.refs_0_
  49.0 0.8 fusion.1.refs_9_
  50.0 0.2 fusion
  50.2 1.1 reduce-window.6
  51.6 2.4 shard_map.159
  54.0 1.9 collective-permute-start.3
  56.1 0.8 exponential_multiply_fusion.1
  56.9 0.7 copy.39.refs_6_
  57.7 0.2 fusion.6
  57.8 0.7 copy.40.refs_7_
  58.5 7.7 %shard_map.160 = (f32[2,256,2048]{2,1,0:T(8,128)}, f32[2,256,2048]{2,1,0:T(8,128)}) custom-call(f32[16]{0:T(128)} %refs_0_.1, bf16[2,256,2048]{2,1,0:T(8,128)(2,1)} %refs_3_.3, bf16[2,256,2048]{2,1,0:T(8,128)(2,1)} %refs_2_.2, bf16[2,256,256]{2,1,0:T(8,128)(2,1)} %refs_4_.3, bf16[2,256,256]{2,1,0:T(8,128)(2,1)} %refs_2_.3, f32[2,256,16]{2,1,0:T(8,128)} %bitcast.46, ...), custom_call_target="tpu_custom_call" | custom-call | tf_op jit(solution)/shard_map/pallas_call | solution.py:80
  66.3 7.6 %collective-permute-done.6.refs_6_.refs_5_ = bf16[160,4096]{1,0:T(8,128)(2,1)} collective-permute-done((bf16[160,4096]{1,0:T(8,128)(2,1)}, bf16[160,4096]{1,0:T(8,128)(2,1)}, u32[]{:S(2)}, u32[]{:S(2)}) %collective-permute-start.6) | collective-permute-done | bytes 1310752 | tf_op jit(solution)/shard_map/ppermute | solution.py:14
  73.9 24.9 %collective-permute-done.5.refs_7_.refs_4_ = bf16[160,4096]{1,0:T(8,128)(2,1)} collective-permute-done((bf16[160,4096]{1,0:T(8,128)(2,1)}, bf16[160,4096]{1,0:T(8,128)(2,1)}, u32[]{:S(2)}, u32[]{:S(2)}) %collective-permute-start.5) | collective-permute-done | bytes 1310752 | tf_op jit(solution)/shard_map/ppermute | solution.py:14
  98.8 36.7 %collective-permute-done.4.no_ref = bf16[160,4096]{1,0:T(8,128)(2,1)} collective-permute-done((bf16[160,4096]{1,0:T(8,128)(2,1)}, bf16[160,4096]{1,0:T(8,128)(2,1)}, u32[]{:S(2)}, u32[]{:S(2)}) %collective-permute-start.4) | collective-permute-done | bytes 1310752 | tf_op jit(solution)/shard_map/ppermute | solution.py:412
  135.4 2.9 %shard_map.161.refs_8_.refs_3_.refs_5_ = bf16[160,4096]{1,0:T(8,128)(2,1)} custom-call(s32[1]{0:T(128)} %bitcast.17.flag_ref, bf16[160,4096]{1,0:T(8,128)(2,1)} %collective-permute-done.1.refs_2_.yes_ref, bf16[160,4096]{1,0:T(8,128)(2,1)} %collective-permute-done.4.no_ref), custom_call_target="tpu_custom_call" | custom-call | tf_op jit(solution)/shard_map/pallas_call | solution.py:239
  138.3 7.8 %collective-permute-done.3.refs_5_.yes_ref = bf16[80,4096]{1,0:T(8,128)(2,1)} collective-permute-done((bf16[80,4096]{1,0:T(8,128)(2,1)}, bf16[80,4096]{1,0:T(8,128)(2,1)}, u32[]{:S(2)}, u32[]{:S(2)}) %collective-permute-start.3) | collective-permute-done | bytes 655392 | tf_op jit(solution)/shard_map/ppermute | solution.py:383
  146.1 6.9 %shard_map.162.refs_1_ = bf16[512,2048]{1,0:T(8,128)(2,1)} custom-call(s32[64]{0:T(128)} %multiply_add_fusion.refs_0_, bf16[128,64,256]{2,1,0:T(8,128)(2,1)} %all-to-all-done.refs_1_.refs_2_, bf16[2,256,256]{2,1,0:T(8,128)(2,1)} %refs_2_.3, f32[2,256,2048]{2,1,0:T(8,128)} %get-tuple-element.40.refs_3_, f32[2,256,2048]{2,1,0:T(8,128)} %get-tuple-element.47.refs_4_, ...), custom_call_target="tpu_custom_call" | custom-call | tf_op jit(solution)/shard_map/pallas_call | solution.py:150
  153.0 0.6 collective-permute-start.14
  153.5 3.3 %collective-permute-start.9 = (bf16[80,4096]{1,0:T(8,128)(2,1)}, bf16[80,4096]{1,0:T(8,128)(2,1)}, u32[]{:S(2)}, u32[]{:S(2)}) collective-permute-start(bf16[80,4096]{1,0:T(8,128)(2,1)} %shard_map.164), channel_id=1, source_target_pairs={{4,8},{8,4},{6,10},{10,6},{5,9},{9,5},{7,11},{11,7},{20,24},{24,20... | collective-permute-start | bytes 1966088 | tf_op jit(solution)/shard_map/ppermute | solution.py:432
  156.9 1.6 collective-permute-start.8
  158.5 2.1 collective-permute-start.11
  160.6 0.6 stack.103.refs_0_
  161.2 10.3 %shard_map.163.own_ref = bf16[512,960]{1,0:T(8,128)(2,1)} custom-call(s32[7]{0:T(128)} %stack.103.refs_0_, bf16[512,2048]{1,0:T(8,128)(2,1)} %shard_map.162.refs_1_, bf16[512,2048]{1,0:T(8,128)(2,1)} %collective-permute-done.7.refs_2_, bf16[320,4096]{1,0:T(8,128)(2,1)} %bitcast.45, bf16[160,4096]{1,0:T(8,128)(2,1)} %collective-permute-done.2.refs_3_.refs_4_, ...), custom_call_target="tpu_custom_call" | custom-call | tf_op jit(solution)/shard_map/pallas_call | solution.py:213
  171.5 1.1 collective-permute-done.9.yes_ref
  172.6 2.2 collective-permute-start.10
  174.8 2.2 shard_map.165.refs_6_.refs_3_
  177.0 1.5 collective-permute-start.12
  178.5 0.7 pad_add_fusion.refs_0_
  179.2 0.6 exponential_multiply_fusion.2.refs_1_
  179.8 0.9 exponential_multiply_fusion.refs_5_
  180.7 7.9 %shard_map.166 = bf16[2,2048,256]{2,1,0:T(8,128)(2,1)} custom-call(s32[64]{0:T(128)} %multiply_add_fusion.refs_0_, f32[2,16]{1,0:T(2,128)} %exponential_multiply_fusion.2.refs_1_, bf16[128,64,256]{2,1,0:T(8,128)(2,1)} %all-to-all-done.refs_1_.refs_2_, bf16[2,256,2048]{2,1,0:T(8,128)(2,1)} %refs_3_.3, bf16[2,256,256]{2,1,0:T(8,128)(2,1)} %refs_4_.3, ...), custom_call_target="tpu_custom_call" | custom-call | tf_op jit(solution)/shard_map/pallas_call | solution.py:117
  188.6 2.2 shard_map.167.refs_5_
  190.8 6.8 %shard_map.168.refs_7_.kept_second_ref = bf16[512,320]{1,0:T(8,128)(2,1)} custom-call(s32[4]{0:T(128)} %pad_add_fusion.refs_0_, bf16[512,2048]{1,0:T(8,128)(2,1)} %shard_map.162.refs_1_, bf16[512,2048]{1,0:T(8,128)(2,1)} %collective-permute-done.7.refs_2_, bf16[160,4096]{1,0:T(8,128)(2,1)} %shard_map.161.refs_8_.refs_3_.refs_5_, ...), custom_call_target="tpu_custom_call" | custom-call | tf_op jit(solution)/shard_map/pallas_call | solution.py:213
  197.6 4.4 %collective-permute-done.12.refs_2_.refs_4_ = bf16[80,4096]{1,0:T(8,128)(2,1)} collective-permute-done((bf16[80,4096]{1,0:T(8,128)(2,1)}, bf16[80,4096]{1,0:T(8,128)(2,1)}, u32[]{:S(2)}, u32[]{:S(2)}) %collective-permute-start.12) | collective-permute-done | bytes 655392 | tf_op jit(solution)/shard_map/ppermute | solution.py:14
  202.0 1.6 collective-permute-start.13
  203.5 0.6 stack.112.refs_0_
  204.2 2.3 collective-permute-done.15.refs_2_
  206.5 8.1 %shard_map.170 = bf16[512,640]{1,0:T(8,128)(2,1)} custom-call(s32[6]{0:T(128)} %stack.112.refs_0_, bf16[512,2048]{1,0:T(8,128)(2,1)} %shard_map.169.refs_1_, bf16[512,2048]{1,0:T(8,128)(2,1)} %collective-permute-done.15.refs_2_, bf16[160,4096]{1,0:T(8,128)(2,1)} %collective-permute-done.refs_1_.in_ref.refs_6_.refs_3_, ...), custom_call_target="tpu_custom_call" | custom-call | tf_op jit(solution)/shard_map/pallas_call | solution.py:213
  214.6 0.6 collective-permute-start.16
  215.3 0.6 stack.109.refs_0_
  215.9 3.3 %collective-permute-done.13.refs_6_ = bf16[80,4096]{1,0:T(8,128)(2,1)} collective-permute-done((bf16[80,4096]{1,0:T(8,128)(2,1)S(1)}, bf16[80,4096]{1,0:T(8,128)(2,1)}, u32[]{:S(2)}, u32[]{:S(2)}) %collective-permute-start.13) | collective-permute-done | bytes 655392 | tf_op jit(solution)/shard_map/ppermute | solution.py:14
  219.2 6.7 %shard_map.171.refs_7_ = bf16[512,320]{1,0:T(8,128)(2,1)} custom-call(s32[6]{0:T(128)} %stack.109.refs_0_, bf16[512,2048]{1,0:T(8,128)(2,1)} %shard_map.169.refs_1_, bf16[512,2048]{1,0:T(8,128)(2,1)} %collective-permute-done.15.refs_2_, bf16[80,4096]{1,0:T(8,128)(2,1)} %shard_map.165.refs_6_.refs_3_, ...), custom_call_target="tpu_custom_call" | custom-call | tf_op jit(solution)/shard_map/pallas_call | solution.py:213
  226.0 0.6 collective-permute-start.17
  226.6 0.6 stack.95.place_ref
  227.2 6.7 %shard_map.172.kept_third_ref = bf16[512,320]{1,0:T(8,128)(2,1)} custom-call(s32[6]{0:T(128)} %stack.109.refs_0_, bf16[512,2048]{1,0:T(8,128)(2,1)} %shard_map.162.refs_1_, bf16[512,2048]{1,0:T(8,128)(2,1)} %collective-permute-done.7.refs_2_, bf16[80,4096]{1,0:T(8,128)(2,1)} %shard_map.165.refs_6_.refs_3_, ...), custom_call_target="tpu_custom_call" | custom-call | tf_op jit(solution)/shard_map/pallas_call | solution.py:213
  234.0 6.1 %collective-permute-done.17.third_ref = bf16[512,320]{1,0:T(8,128)(2,1)S(1)} collective-permute-done((bf16[512,320]{1,0:T(8,128)(2,1)}, bf16[512,320]{1,0:T(8,128)(2,1)S(1)}, u32[]{:S(2)}, u32[]{:S(2)}) %collective-permute-start.17) | collective-permute-done | bytes 327712 | tf_op jit(solution)/shard_map/ppermute | solution.py:14
  240.1 0.8 copy-done.3
  240.9 3.9 %shard_map.173 = bf16[512,2560]{1,0:T(8,128)(2,1)} custom-call(s32[5]{0:T(128)} %stack.95.place_ref, bf16[512,960]{1,0:T(8,128)(2,1)} %shard_map.163.own_ref, bf16[512,320]{1,0:T(8,128)(2,1)} %shard_map.168.refs_7_.kept_second_ref, bf16[512,320]{1,0:T(8,128)(2,1)} %shard_map.172.kept_third_ref, bf16[512,640]{1,0:T(8,128)(2,1)} %collective-permute-done.16.two_ref, ...), custom_call_target="tpu_custom_call" | custom-call | tf_op jit(solution)/shard_map/pallas_call | solution.py:303
  (57 shorter events, 1.2 us)
Async XLA Ops:
  0.6 7.1 %copy-start.7 = (s32[1,16,32,1]{2,3,1,0:T(1,128)S(1)}, s32[1,16,32,1]{2,3,1,0:T(1,128)}, u32[]{:S(2)}) copy-start(s32[1,16,32,1]{2,3,1,0:T(1,128)} %param.25) | copy-start | bytes 6148
  0.6 8.1 %copy-start.6 = (s32[1,16,32]{2,1,0:T(8,128)S(1)}, s32[1,16,32]{2,1,0:T(8,128)}, u32[]{:S(2)}) copy-start(s32[1,16,32]{2,1,0:T(8,128)} %param.26) | copy-start | bytes 6148
  0.7 8.4 %copy-start.5 = (bf16[64,64]{1,0:T(8,128)(2,1)S(1)}, bf16[64,64]{1,0:T(8,128)(2,1)}, u32[]{:S(2)}) copy-start(bf16[64,64]{1,0:T(8,128)(2,1)} %param.24) | copy-start | bytes 24580
  2.1 30.7 %collective-permute-start = (bf16[160,4096]{1,0:T(8,128)(2,1)S(1)}, bf16[160,4096]{1,0:T(8,128)(2,1)}, u32[]{:S(2)}, u32[]{:S(2)}) collective-permute-start(bf16[160,4096]{1,0:T(8,128)(2,1)S(1)} %dynamic-slice_bitcast_fusion), channel_id=1, source_target_pairs={{0,4},{2,6},{4,0},{6,2},{8,12},{10,14},{12,8},{14,10},{1,5},{3,7},... | collective-permute-start | bytes 3932168 | tf_op jit(solution)/shard_map/ppermute | solution.py:14
  3.7 32.2 %collective-permute-start.1 = (bf16[160,4096]{1,0:T(8,128)(2,1)S(1)}, bf16[160,4096]{1,0:T(8,128)(2,1)}, u32[]{:S(2)}, u32[]{:S(2)}) collective-permute-start(bf16[160,4096]{1,0:T(8,128)(2,1)S(1)} %dynamic-slice_bitcast_fusion), channel_id=1, source_target_pairs={{4,8},{8,4},{6,10},{10,6},{5,9},{9,5},{7,11},{11,7},{20,24},{24,20... | collective-permute-start | bytes 3932168 | tf_op jit(solution)/shard_map/ppermute | solution.py:363
  5.6 30.4 %collective-permute-start.2 = (bf16[160,4096]{1,0:T(8,128)(2,1)S(1)}, bf16[160,4096]{1,0:T(8,128)(2,1)}, u32[]{:S(2)}, u32[]{:S(2)}) collective-permute-start(bf16[160,4096]{1,0:T(8,128)(2,1)S(1)} %dynamic-slice_bitcast_fusion), channel_id=1, source_target_pairs={{0,2},{2,0},{4,6},{6,4},{8,10},{10,8},{12,14},{14,12},{1,3},{3,1},... | collective-permute-start | bytes 3932168 | tf_op jit(solution)/shard_map/ppermute | solution.py:14
  36.1 5.7 %copy-start.10 = (s32[2]{0:T(128)S(1)}, s32[2]{0:T(128)}, u32[]{:S(2)}) copy-start(s32[2]{0:T(128)} %param.27) | copy-start | bytes 28
  36.1 5.7 %copy-start.11 = (f32[16]{0:T(128)S(1)}, f32[16]{0:T(128)}, u32[]{:S(2)}) copy-start(f32[16]{0:T(128)} %param.21) | copy-start | bytes 196
  36.1 5.7 %copy-start.9 = (s32[2]{0:T(128)S(1)}, s32[2]{0:T(128)}, u32[]{:S(2)}) copy-start(s32[2]{0:T(128)} %param.28) | copy-start | bytes 28
  36.1 13.8 %copy-start.4 = (f32[2,256,16]{1,2,0:T(8,128)S(1)}, f32[2,256,16]{1,2,0:T(8,128)}, u32[]{:S(2)}) copy-start(f32[2,256,16]{1,2,0:T(8,128)} %param.19) | copy-start | bytes 98308
  36.1 13.9 %copy-start.8 = (f32[16]{0:T(128)S(1)}, f32[16]{0:T(128)}, u32[]{:S(2)}) copy-start(f32[16]{0:T(128)} %param.20) | copy-start | bytes 196
  36.1 110.0 %all-to-all-start = ((bf16[128,64,256]{2,1,0:T(8,128)(2,1)}), bf16[128,64,256]{2,1,0:T(8,128)(2,1)}, u32[]{:S(2)}, u32[]{:S(2)}) async-start(bf16[128,64,256]{2,1,0:T(8,128)(2,1)} %shard_map.158.refs_10_), calls=%async_computation | async-start | bytes 8388608 | tf_op jit(solution)/shard_map/all_to_all | solution.py:386
  41.9 32.0 %collective-permute-start.6 = (bf16[160,4096]{1,0:T(8,128)(2,1)}, bf16[160,4096]{1,0:T(8,128)(2,1)}, u32[]{:S(2)}, u32[]{:S(2)}) collective-permute-start(bf16[160,4096]{1,0:T(8,128)(2,1)} %collective-permute-done.2.refs_3_.refs_4_), channel_id=1, source_target_pairs={{0,16},{16,0},{1,17},{17,1},{2,18},{18,2},{3,19},{19,3},{4,20},{20... | collective-permute-start | bytes 3932168 | tf_op jit(solution)/shard_map/ppermute | solution.py:14
  43.4 92.1 %collective-permute-start.4 = (bf16[160,4096]{1,0:T(8,128)(2,1)}, bf16[160,4096]{1,0:T(8,128)(2,1)}, u32[]{:S(2)}, u32[]{:S(2)}) collective-permute-start(bf16[160,4096]{1,0:T(8,128)(2,1)} %collective-permute-done.1.refs_2_.yes_ref), channel_id=1, source_target_pairs={{4,0},{6,2},{8,12},{10,14},{5,1},{7,3},{9,13},{11,15},{20,16},{22,... | collective-permute-start | bytes 3932168 | tf_op jit(solution)/shard_map/ppermute | solution.py:412
  47.9 50.9 %collective-permute-start.5 = (bf16[160,4096]{1,0:T(8,128)(2,1)}, bf16[160,4096]{1,0:T(8,128)(2,1)}, u32[]{:S(2)}, u32[]{:S(2)}) collective-permute-start(bf16[160,4096]{1,0:T(8,128)(2,1)} %collective-permute-done.refs_1_.in_ref.refs_6_.refs_3_), channel_id=1, source_target_pairs={{0,16},{16,0},{1,17},{17,1},{2,18},{18,2},{3,19},{19,3},{4,20},{20... | collective-permute-start | bytes 3932168 | tf_op jit(solution)/shard_map/ppermute | solution.py:14
  54.0 92.1 %collective-permute-start.3 = (bf16[80,4096]{1,0:T(8,128)(2,1)}, bf16[80,4096]{1,0:T(8,128)(2,1)}, u32[]{:S(2)}, u32[]{:S(2)}) collective-permute-start(bf16[80,4096]{1,0:T(8,128)(2,1)} %get-tuple-element.37), channel_id=1, source_target_pairs={{4,8},{8,4},{6,10},{10,6},{5,9},{9,5},{7,11},{11,7},{20,24},{24,20... | collective-permute-start | bytes 1966088 | tf_op jit(solution)/shard_map/ppermute | solution.py:383
  56.9 1.6 copy-start.1
  153.0 8.2 %collective-permute-start.7 = (bf16[512,2048]{1,0:T(8,128)(2,1)}, bf16[512,2048]{1,0:T(8,128)(2,1)}, u32[]{:S(2)}, u32[]{:S(2)}) collective-permute-start(bf16[512,2048]{1,0:T(8,128)(2,1)} %shard_map.162.refs_1_), channel_id=1, source_target_pairs={{0,1},{1,0},{2,3},{3,2},{4,5},{5,4},{6,7},{7,6},{8,9},{9,8},{10,11... | collective-permute-start | bytes 6291464 | tf_op jit(solution)/shard_map/ppermute | solution.py:14
  153.0 49.0 %collective-permute-start.14 = (bf16[512,2048]{1,0:T(8,128)(2,1)}, bf16[512,2048]{1,0:T(8,128)(2,1)}, u32[]{:S(2)}, u32[]{:S(2)}) collective-permute-start(bf16[512,2048]{1,0:T(8,128)(2,1)} %shard_map.162.refs_1_), channel_id=1, source_target_pairs={{0,2},{2,0},{4,6},{6,4},{8,10},{10,8},{12,14},{14,12},{1,3},{3,1},... | collective-permute-start | bytes 6291464 | tf_op jit(solution)/shard_map/ppermute | solution.py:14
  153.5 19.1 %collective-permute-start.9 = (bf16[80,4096]{1,0:T(8,128)(2,1)}, bf16[80,4096]{1,0:T(8,128)(2,1)}, u32[]{:S(2)}, u32[]{:S(2)}) collective-permute-start(bf16[80,4096]{1,0:T(8,128)(2,1)} %shard_map.164), channel_id=1, source_target_pairs={{4,8},{8,4},{6,10},{10,6},{5,9},{9,5},{7,11},{11,7},{20,24},{24,20... | collective-permute-start | bytes 1966088 | tf_op jit(solution)/shard_map/ppermute | solution.py:432
  156.9 33.9 %collective-permute-start.8 = (bf16[160,4096]{1,0:T(8,128)(2,1)}, bf16[160,4096]{1,0:T(8,128)(2,1)}, u32[]{:S(2)}, u32[]{:S(2)}) collective-permute-start(bf16[160,4096]{1,0:T(8,128)(2,1)} %shard_map.161.refs_8_.refs_3_.refs_5_), channel_id=1, source_target_pairs={{0,16},{16,0},{1,17},{17,1},{2,18},{18,2},{3,19},{19,3},{4,20},{20... | collective-permute-start | bytes 3932168 | tf_op jit(solution)/shard_map/ppermute | solution.py:14
  158.5 16.3 %collective-permute-start.11 = (bf16[80,4096]{1,0:T(8,128)(2,1)}, bf16[80,4096]{1,0:T(8,128)(2,1)}, u32[]{:S(2)}, u32[]{:S(2)}) collective-permute-start(bf16[80,4096]{1,0:T(8,128)(2,1)} %collective-permute-done.3.refs_5_.yes_ref), channel_id=1, source_target_pairs={{4,0},{6,2},{8,12},{10,14},{5,1},{7,3},{9,13},{11,15},{20,16},{22,... | collective-permute-start | bytes 1966088 | tf_op jit(solution)/shard_map/ppermute | solution.py:420
  161.2 17.9 %copy-start.2 = (f32[2,16,256]{1,2,0:T(8,128)S(1)}, f32[2,16,256]{1,2,0:T(8,128)}, u32[]{:S(2)}) copy-start(f32[2,16,256]{1,2,0:T(8,128)} %copy-done.1) | copy-start | bytes 98308
  172.6 16.0 %collective-permute-start.10 = (bf16[80,4096]{1,0:T(8,128)(2,1)}, bf16[80,4096]{1,0:T(8,128)(2,1)}, u32[]{:S(2)}, u32[]{:S(2)}) collective-permute-start(bf16[80,4096]{1,0:T(8,128)(2,1)} %collective-permute-done.9.yes_ref), channel_id=1, source_target_pairs={{4,0},{6,2},{8,12},{10,14},{5,1},{7,3},{9,13},{11,15},{20,16},{22,... | collective-permute-start | bytes 1966088 | tf_op jit(solution)/shard_map/ppermute | solution.py:469
  177.0 24.9 %collective-permute-start.12 = (bf16[80,4096]{1,0:T(8,128)(2,1)}, bf16[80,4096]{1,0:T(8,128)(2,1)}, u32[]{:S(2)}, u32[]{:S(2)}) collective-permute-start(bf16[80,4096]{1,0:T(8,128)(2,1)} %shard_map.165.refs_6_.refs_3_), channel_id=1, source_target_pairs={{0,16},{16,0},{1,17},{17,1},{2,18},{18,2},{3,19},{19,3},{4,20},{20... | collective-permute-start | bytes 1966088 | tf_op jit(solution)/shard_map/ppermute | solution.py:14
  197.6 4.4 %copy-start = (bf16[80,4096]{1,0:T(8,128)(2,1)S(1)}, bf16[80,4096]{1,0:T(8,128)(2,1)}, u32[]{:S(2)}) copy-start(bf16[80,4096]{1,0:T(8,128)(2,1)} %shard_map.167.refs_5_) | copy-start | bytes 1966084
  202.0 4.5 %collective-permute-start.15 = (bf16[512,2048]{1,0:T(8,128)(2,1)}, bf16[512,2048]{1,0:T(8,128)(2,1)}, u32[]{:S(2)}, u32[]{:S(2)}) collective-permute-start(bf16[512,2048]{1,0:T(8,128)(2,1)} %shard_map.169.refs_1_), channel_id=1, source_target_pairs={{0,1},{1,0},{2,3},{3,2},{4,5},{5,4},{6,7},{7,6},{8,9},{9,8},{10,11... | collective-permute-start | bytes 6291464 | tf_op jit(solution)/shard_map/ppermute | solution.py:14
  202.0 17.2 %collective-permute-start.13 = (bf16[80,4096]{1,0:T(8,128)(2,1)S(1)}, bf16[80,4096]{1,0:T(8,128)(2,1)}, u32[]{:S(2)}, u32[]{:S(2)}) collective-permute-start(bf16[80,4096]{1,0:T(8,128)(2,1)S(1)} %copy-done), channel_id=1, source_target_pairs={{0,16},{16,0},{1,17},{17,1},{2,18},{18,2},{3,19},{19,3},{4,20},{20... | collective-permute-start | bytes 1966088 | tf_op jit(solution)/shard_map/ppermute | solution.py:14
  214.6 19.3 %collective-permute-start.16 = (bf16[512,640]{1,0:T(8,128)(2,1)}, bf16[512,640]{1,0:T(8,128)(2,1)}, u32[]{:S(2)}, u32[]{:S(2)}) collective-permute-start(bf16[512,640]{1,0:T(8,128)(2,1)} %shard_map.170), channel_id=1, source_target_pairs={{0,2},{2,0},{4,6},{6,4},{8,10},{10,8},{12,14},{14,12},{1,3},{3,1},... | collective-permute-start | bytes 1966088 | tf_op jit(solution)/shard_map/ppermute | solution.py:14
  226.0 14.1 %collective-permute-start.17 = (bf16[512,320]{1,0:T(8,128)(2,1)}, bf16[512,320]{1,0:T(8,128)(2,1)S(1)}, u32[]{:S(2)}, u32[]{:S(2)}) collective-permute-start(bf16[512,320]{1,0:T(8,128)(2,1)} %shard_map.171.refs_7_), channel_id=1, source_target_pairs={{0,2},{2,0},{4,6},{6,4},{8,10},{10,8},{12,14},{14,12},{1,3},{3,1},... | collective-permute-start | bytes 983048 | tf_op jit(solution)/shard_map/ppermute | solution.py:14
  240.1 0.8 copy-start.3
